TPU v7x, 512 devices: a whole 4x4x16 slice. The times are simulated.
512 devices in a mesh: row: 64 (over x, y, z_hi, core), col: 8 (over z_lo).
Axes of the slice: x: 4, y: 4, z: 16 (z_hi: 2, z_lo: 8; z = z_hi * 8 + z_lo), core: 2. Of those that a mesh axis runs over, the one named last changes fastest.
Arguments:
- amplitudes: float32 [192, 40, 1152], P('row', 'col'), may hold values from -3 to 3
- integrals: float32 [192, 40, 7680], P('row', 'col'), may hold values from -0.0625 to 0.0625
- residual: float32 [192, 40, 1152], P('row', 'col'), may hold values from -6 to 6
- occupied_energy: float32 [40], replicated, may hold values from -3 to -0.5
- virtual_energy: float32 [192], replicated, may hold values from 0.3 to 4
- window_start: int32 [1], replicated, may hold values from 0 to 34
Outputs:
- residual_new: float32 [192, 40, 1152], P('row', 'col')
- increment: float32 [192, 40, 1152], P('row', 'col')
All inputs are finite; a program needn't handle non-finite values.
Results may differ from a plain program's by a relative error of at most 0.000053.
Values sent between devices are 32-bit elements; how exact they have to be, the bound alone decides.
No kernel may reach another device: no remote copies, remote signals or barrier semaphores. Data moves between devices by JAX's collectives and lax.ppermute only.
A program may use at most 64 MiB of HBM per device.

v0:
```python
import jax
import jax.numpy as jnp
from jax import lax
from jax.sharding import PartitionSpec as P


def contract(left_form, first, second):
    return jnp.einsum(
        left_form,
        first,
        second,
        precision=lax.Precision.HIGHEST,
        preferred_element_type=jnp.float32,
    )


def mixed_block(amps):
    received = lax.all_to_all(amps, "row", split_axis=3, concat_axis=0, tiled=True)
    swapped = jnp.transpose(received, (3, 1, 2, 0))
    return 2.0 * amps - swapped


def body(amplitudes, integrals, residual, occupied_energy, virtual_energy, window_start):
    rows_here = amplitudes.shape[0]
    cols_here = amplitudes.shape[1]
    virt_count = virtual_energy.shape[0]
    window_size = amplitudes.shape[2] // virt_count
    occ_count = integrals.shape[2] // virt_count
    amps = amplitudes.reshape(rows_here, cols_here, window_size, virt_count)
    ints = integrals.reshape(rows_here, cols_here, occ_count, virt_count)
    position = lax.axis_index("row")
    mixed_amps = mixed_block(amps).reshape(rows_here, cols_here, window_size * virt_count)
    block_rows = lax.all_gather(mixed_amps, "row", axis=0, tiled=True)
    block_four = block_rows.reshape(block_rows.shape[0], cols_here, window_size, virt_count)
    partial_value = contract("bkjc,akic->bjia", ints, block_four)
    reduced = lax.psum_scatter(partial_value, "col", scatter_dimension=1, tiled=True)
    summed = lax.all_to_all(reduced, "row", split_axis=3, concat_axis=0, tiled=True)
    cycle_term = jnp.transpose(summed, (3, 1, 2, 0))
    residual_new = residual.reshape(rows_here, cols_here, window_size, virt_count) + cycle_term
    virtual_here = lax.dynamic_slice_in_dim(virtual_energy, position * rows_here, rows_here)
    occupied_here = lax.dynamic_slice_in_dim(
        occupied_energy, lax.axis_index("col") * cols_here, cols_here
    )
    occupied_window = lax.dynamic_slice_in_dim(occupied_energy, window_start[0], window_size)
    denominator = (
        virtual_here[:, None, None, None]
        + virtual_energy[None, None, None, :]
        - occupied_window[None, None, :, None]
        - occupied_here[None, :, None, None]
    )
    increment = residual_new / denominator
    flat_shape = (rows_here, cols_here, window_size * virt_count)
    return (residual_new.reshape(flat_shape), increment.reshape(flat_shape))


def solution(mesh):
    in_specs = (P("row", "col", None), P("row", "col", None), P("row", "col", None), P(), P(), P())
    out_specs = (P("row", "col", None), P("row", "col", None))
    return jax.shard_map(body, mesh=mesh, in_specs=in_specs, out_specs=out_specs, check_vma=False)
```

profile of v0, /device:TPU:1, one launch (start us, length us, event | category | flops | bytes accessed | tf_op | source)
XLA Modules:
  0.0 341.1 jit_solution(5123302554177389163)
XLA Ops:
  7.2 1.0 reshape.62
  8.2 1.3 copy.28
  9.6 1.2 reshape.71
  10.8 39.0 %all_to_all.36 = f32[64,1,270]{2,1,0:T(1,128)S(1)} all-to-all(f32[64,1,270]{2,1,0:T(1,128)S(1)} %reshape.71), channel_id=1, replica_groups=mesh['row'=64,'col'=8] {'row'}, dimensions={0} | all-to-all | bytes 138240 | tf_op jit(solution)/shard_map/all_to_all | solution.py:18
  50.4 0.9 reduce
  51.2 2.1 reshape.72
  53.4 9.0 %copy.42 = f32[3,5,6,64,3]{0,3,2,4,1:T(8,128)S(1)} copy(f32[3,5,6,64,3]{2,0,1,4,3:T(4,128)} %bitcast.53) | data formatting | bytes 138240 | tf_op jit(solution)/shard_map/all_to_all | solution.py:18
  62.4 2.0 all_to_all.29
  65.4 1.4 reshape.65
  66.8 149.2 %all-gather.2.cloned.1.call-done = f32[192,5,1152]{2,1,0:T(8,128)} async-done(((f32[3,5,1152]{2,1,0:T(8,128)}), f32[192,5,1152]{2,1,0:T(8,128)}) %all-gather.2.cloned.1.call-update) | async-done | bytes 4423696 | tf_op jit(solution)/shard_map/all_gather | solution.py:33
  216.1 7.8 %copy.32 = f32[192,5,1152]{0,2,1:T(8,128)} copy(f32[192,5,1152]{2,1,0:T(8,128)} %all-gather.2.cloned.1.call-done) | data formatting | bytes 8847360 | tf_op jit(solution)/shard_map/all_gather | solution.py:33
  223.9 5.7 %fusion.2 = f32[3,40,6,192]{3,1,0,2:T(8,128)S(1)} fusion(f32[192,5,6,192,1]{0,3,2,1,4:T(8,128)} %bitcast.50, f32[3,5,40,192]{3,2,0,1:T(8,128)S(1)} %reshape.65), kind=kOutput, calls=%fused_computation.2 | convolution fusion | flops 1592524800 | bytes 5437440 | tf_op jit(solution)/shard_map/bkjc,akic->bjia/dot_general | solution.py:8
  229.6 1.2 copy.35
  230.9 51.5 %reduce-scatter.2.cloned.1.call-done = f32[3,5,6,192]{3,2,0,1:T(8,128)} async-done(((f32[3,40,6,192]{3,2,0,1:T(8,128)}), f32[3,5,6,192]{3,2,0,1:T(8,128)}) %reduce-scatter.2.cloned.1.call-update) | async-done | bytes 69136 | tf_op jit(solution)/shard_map/reduce_scatter | solution.py:36
  282.4 2.1 copy.36
  284.6 1.9 reshape.73
  286.4 15.3 %all-to-all-start.1 = ((f32[64,1,270]{2,1,0:T(1,128)}), f32[64,1,270]{2,1,0:T(1,128)S(1)}, u32[]{:S(2)}, u32[]{:S(2)}) async-start(f32[64,1,270]{2,1,0:T(1,128)} %reshape.73), calls=%async_computation.2 | async-start | bytes 196608 | tf_op jit(solution)/shard_map/all_to_all | solution.py:37
  302.8 15.8 %all-to-all-done.1 = f32[64,1,270]{2,1,0:T(1,128)S(1)} async-done(((f32[64,1,270]{2,1,0:T(1,128)}), f32[64,1,270]{2,1,0:T(1,128)S(1)}, u32[]{:S(2)}, u32[]{:S(2)}) %all-to-all-start.1) | async-done | bytes 69152 | tf_op jit(solution)/shard_map/all_to_all | solution.py:37
  318.6 0.9 reduce.1
  319.5 2.1 reshape.74
  321.6 9.0 %copy.46 = f32[3,5,6,64,3]{0,3,2,4,1:T(8,128)S(1)} copy(f32[3,5,6,64,3]{2,0,1,4,3:T(4,128)} %bitcast.55) | data formatting | bytes 138240 | tf_op jit(solution)/shard_map/all_to_all | solution.py:37
  330.6 2.0 all_to_all.33
  332.7 0.7 reshape.66
  333.5 0.7 reshape.67
  (21 shorter events, 2.2 us)
Async XLA Ops:
  7.2 208.9 %all-gather.2.cloned.1.call-start = ((), (), s32[]{:S(2)}) async-start(), calls=%async_computation.3 | async-start | bytes 7188480 | tf_op jit(solution)/shard_map/all_gather | solution.py:33
  65.2 217.3 %reduce-scatter.2.cloned.1.call-start = ((), (), s32[]{:S(2)}) async-start(), calls=%async_computation.4 | async-start | bytes 1105920 | tf_op jit(solution)/shard_map/reduce_scatter | solution.py:36
  223.9 6.9 %copy-start.1 = (f32[192]{0:T(256)S(1)}, f32[192]{0:T(256)}, u32[]{:S(2)}) copy-start(f32[192]{0:T(256)} %param.10) | copy-start | bytes 2308
  223.9 78.6 %copy-start.2 = (f32[40]{0:T(128)S(1)}, f32[40]{0:T(128)}, u32[]{:S(2)}) copy-start(f32[40]{0:T(128)} %param.9) | copy-start | bytes 484
  223.9 78.7 %copy-start = (f32[3,5,1152]{2,0,1:T(4,128)S(1)}, f32[3,5,1152]{2,0,1:T(4,128)}, u32[]{:S(2)}) copy-start(f32[3,5,1152]{2,0,1:T(4,128)} %param.8) | copy-start | bytes 207364
  286.4 32.2 %all-to-all-start.1 = ((f32[64,1,270]{2,1,0:T(1,128)}), f32[64,1,270]{2,1,0:T(1,128)S(1)}, u32[]{:S(2)}, u32[]{:S(2)}) async-start(f32[64,1,270]{2,1,0:T(1,128)} %reshape.73), calls=%async_computation.2 | async-start | bytes 196608 | tf_op jit(solution)/shard_map/all_to_all | solution.py:37
Sparse Core Ops, SparseCore 0:
  65.3 150.7 all-gather.1
  230.9 51.4 reduce-scatter.1
where the time goes:
time: 342 us; the launch traced here: 341 us
  waiting for transfers between devices  217 us (63%)
  local copies, waits for them, and re-layouts  47.3 us (14%)
  blocking collectives  39 us (11%)
  starting transfers between devices  15.5 us (5%)
  between operations  14.8 us (4%)
  matrix products  5.69 us (2%)
    all_gather x1, waiting for transfers between devices, body(): block_rows = lax.all_gather(mixed_amps, 'row', axis=0, tiled=True)  149 us
    reduce_scatter x1, waiting for transfers between devices, body(): lax.psum_scatter(partial_value, 'col', scatter_dimension=1, tiled=True)  51.5 us
    all_to_all x1, blocking collectives, mixed_block(): lax.all_to_all(amps, 'row', split_axis=3, concat_axis=0, tiled=True)  39 us
    all_to_all x1, waiting for transfers between devices, body(): lax.all_to_all(reduced, 'row', split_axis=3, concat_axis=0, tiled=True)  15.8 us
    all_to_all x1, starting transfers between devices, body(): lax.all_to_all(reduced, 'row', split_axis=3, concat_axis=0, tiled=True)  15.3 us
    all_to_all x3, local copies, waits for them, and re-layouts, mixed_block(): lax.all_to_all(amps, 'row', split_axis=3, concat_axis=0, tiled=True)  11.5 us
    all_to_all x2, local copies, waits for them, and re-layouts, body(): lax.all_to_all(reduced, 'row', split_axis=3, concat_axis=0, tiled=True)  11 us
    all_gather x1, local copies, waits for them, and re-layouts, body(): block_rows = lax.all_gather(mixed_amps, 'row', axis=0, tiled=True)  7.79 us
  transfers between devices with their start and end apart: 3, of which 3 were waited for; matrix products, arithmetic and copies ran while one was open for 1% of the time, Pallas kernels for 0%

commit v1 on v0

v1 whole, which is shorter than its diff:
```python
import functools

import jax
import jax.numpy as jnp
import ml_dtypes
import numpy as np
from jax import lax
from jax.experimental import pallas as pl
from jax.experimental.pallas import tpu as pltpu
from jax.sharding import Mesh, PartitionSpec as P

AXES = ("x", "y", "zh", "core", "col")
SIZES = (4, 4, 2, 2, 8)
F32, BF16 = jnp.float32, jnp.bfloat16
VMEM = pl.BlockSpec(memory_space=pltpu.VMEM)
SMEM = pl.BlockSpec(memory_space=pltpu.SMEM)
NT = (((1,), (1,)), ((), ()))
NN = (((1,), (0,)), ((), ()))


def one_hots():
    order = np.zeros((256, 256), np.float32)
    choose = np.zeros((256, 256), np.float32)
    for x in range(4):
        for y in range(4):
            for zh in range(2):
                for core in range(2):
                    for m in range(3):
                        v = x * 48 + y * 12 + zh * 6 + core * 3 + m
                        order[v, ((x * 4 + y) * 2 + core) * 8 + zh * 3 + m] = 1
                        choose[v, (x * 2 + core) * 24 + (y * 2 + zh) * 3 + m] = 1
    turn = np.zeros((800, 768), np.float32)
    for k in range(5):
        for yz in range(8):
            for i in range(6):
                for m in range(3):
                    turn[k * 160 + yz // 2 * 40 + yz % 2 * 18 + i * 3 + m, i * 128 + k * 24 + yz * 3 + m] = 1
    spread = np.zeros((128, 1280), np.float32)
    for x in range(4):
        for core in range(2):
            for j in range(5):
                for m in range(3):
                    spread[(x * 2 + core) * 16 + j * 3 + m, j * 256 + x * 48 + core * 3 + m] = 1
    return [a.astype(ml_dtypes.bfloat16) for a in (order, choose, turn, spread)]


def dot(a, b, dims=NN):
    return lax.dot_general(a, b, dims, preferred_element_type=F32)


def split2(v):
    high = v.astype(BF16)
    return high, (v - high.astype(F32)).astype(BF16)


def moved(v, hot):
    high = v.astype(BF16)
    rest = v - high.astype(F32)
    mid = rest.astype(BF16)
    low = (rest - mid.astype(F32)).astype(BF16)
    return (dot(low, hot) + dot(mid, hot)) + dot(high, hot)


def lanes192(ref, lead, n):
    if n % 2 == 0:
        return ref[lead, :, n * 192:n * 192 + 256]
    return pltpu.roll(ref[lead, :, n * 192 - 64:n * 192 + 192], 192, 1)


def weights_kernel(ints_ref, order_ref, out_ref, rows):
    rows[...] = jnp.zeros_like(rows)
    for k in range(5):
        for j in range(40):
            at = k * 128 + j // 5 * 16 + j % 5 * 3
            rows[at:at + 3, :] = lanes192(ints_ref, k, j)
        out_ref[k] = moved(rows[k * 128:(k + 1) * 128, :], order_ref[...])


def amps_kernel(zh_ref, own_ref, other_ref, order_ref, choose_ref, one_ref, two_ref, rows1, rows2):
    first = zh_ref[0] == 0
    rows1[...] = jnp.zeros_like(rows1)
    rows2[...] = jnp.zeros_like(rows2)
    for k in range(5):
        for i in range(6):
            own = lanes192(own_ref, k, i)
            other = lanes192(other_ref, k, i)
            for zh, v in ((0, jnp.where(first, own, other)), (1, jnp.where(first, other, own))):
                at = k * 40 + zh * 18 + i * 3
                rows1[at:at + 3, :] = v
                at = k * 48 + i * 8 + zh * 3
                rows2[at:at + 3, :] = v
    chosen = moved(rows2[...], choose_ref[...])
    lane = lax.broadcasted_iota(jnp.int32, (48, 128), 1)
    for n in range(8):
        part = jnp.zeros((48, 128), F32)
        for k in range(5):
            v = pltpu.roll(chosen[k * 48:(k + 1) * 48, :], (k * 24 - n * 24) % 256, 1)[:, :128]
            part = jnp.where((lane >= k * 24) & (lane < k * 24 + 24), v, part)
        for y in range(4):
            two_ref[(n // 2 * 4 + y) * 2 + n % 2] = part
    ordered = moved(rows1[...], order_ref[...])
    for y in range(4):
        one_ref[y] = ordered


def product_kernel(one_ref, two_ref, turn_ref, *refs):
    weights, out_ref = refs[:8], refs[8]
    two_high, two_low, mixed_high, mixed_low = refs[9:]
    for i in range(6):
        high, low = split2(two_ref[:, i * 8:(i + 1) * 8, :].reshape(256, 128))
        two_high[:, i * 128:(i + 1) * 128] = high
        two_low[:, i * 128:(i + 1) * 128] = low
    for k in range(5):
        turn = turn_ref[k * 160:(k + 1) * 160, :]
        swapped = dot(turn, two_high[...], NT) + dot(turn, two_low[...], NT)
        straight = jnp.concatenate([one_ref[y, k * 40:(k + 1) * 40, :] for y in range(4)], 0)
        high, low = split2(2.0 * straight - swapped)
        mixed_high[k] = high
        mixed_low[k] = low
    for pair in range(4):
        total = jnp.zeros((160, 256), F32)
        for k in range(5):
            w = jnp.concatenate(
                [ref[k, z * 16:(z + 1) * 16, :] for z in (2 * pair, 2 * pair + 1) for ref in weights], 0
            )
            high, low = split2(w)
            total += dot(mixed_high[k], low, NT) + dot(mixed_low[k], high, NT) + dot(mixed_high[k], high, NT)
        for yz in range(8):
            for half in range(2):
                to = (yz * 8 + 2 * pair + half) * 18
                at = yz // 2 * 40 + yz % 2 * 18
                out_ref[to:to + 18, :] = total[at:at + 18, half * 128:(half + 1) * 128]


def final_kernel(place_ref, occ_ref, va_ref, got_ref, spread_ref, vb_ref, res_ref, new_ref, inc_ref, sums, cyc, den):
    sums[...] = jnp.zeros_like(sums)
    for yz in range(8):
        total = got_ref[yz * 144:yz * 144 + 18, :]
        for z in range(1, 8):
            at = (yz * 8 + z) * 18
            total += got_ref[at:at + 18, :]
        sums[yz * 24:yz * 24 + 18, :] = total
    v = pltpu.roll(sums[...], place_ref[0] * 32, 1)
    lane = lax.broadcasted_iota(jnp.int32, v.shape, 1)
    other = jnp.where((lane & 16) == 0, pltpu.roll(v, 112, 1), pltpu.roll(v, 16, 1))
    v = jnp.where(place_ref[1] == 0, v, other)
    wide = moved(v, spread_ref[...])
    row = lax.broadcasted_iota(jnp.int32, (3, 192), 0)
    va = [va_ref[place_ref[2] + m] for m in range(3)]
    va = jnp.where(row == 0, va[0], jnp.where(row == 1, va[1], va[2]))
    base = vb_ref[...] + va
    for i in range(6):
        den[:, i * 192:(i + 1) * 192] = base - occ_ref[place_ref[4] + i]
    for j in range(5):
        total = wide[0:24, j * 256:(j + 1) * 256]
        for yz in range(1, 8):
            total += pltpu.roll(wide[yz * 24:(yz + 1) * 24, j * 256:(j + 1) * 256], yz * 6, 1)
        for i in range(6):
            cyc[:, i * 192:(i + 1) * 192] = total[i * 3:(i + 1) * 3, :192]
        new = res_ref[j] + cyc[...]
        new_ref[j] = new
        inc_ref[j] = new / (den[...] - occ_ref[place_ref[3] + j])


def call(kernel, n_smem, n_vmem, outs, scratch):
    shapes = [jax.ShapeDtypeStruct(s, F32) for s in outs]
    return pl.pallas_call(
        kernel,
        out_shape=shapes if len(shapes) > 1 else shapes[0],
        in_specs=[SMEM] * n_smem + [VMEM] * n_vmem,
        out_specs=[VMEM] * len(shapes) if len(shapes) > 1 else VMEM,
        scratch_shapes=scratch,
        compiler_params=pltpu.CompilerParams(vmem_limit_bytes=48 * 1024 * 1024),
    )


def body(amplitudes, integrals, residual, occupied_energy, virtual_energy, window_start):
    order, choose, turn, spread = [jnp.asarray(a) for a in one_hots()]
    x, y, zh, core, col = [lax.axis_index(a).astype(jnp.int32) for a in AXES]
    amps = jnp.transpose(amplitudes, (1, 0, 2))
    ints = jnp.transpose(integrals, (1, 0, 2))
    res = jnp.transpose(residual, (1, 0, 2))
    other = lax.ppermute(amps, "zh", [(0, 1), (1, 0)])
    weights = call(weights_kernel, 0, 2, [(5, 128, 256)], [pltpu.VMEM((640, 256), F32)])(ints, order)
    along = [weights] + [
        lax.ppermute(weights, "x", [(s, (s - d) % 4) for s in range(4)]) for d in (1, 2, 3)
    ]
    across = [lax.ppermute(w, "core", [(0, 1), (1, 0)]) for w in along]
    one, two = call(
        amps_kernel, 1, 4, [(4, 200, 256), (32, 48, 128)],
        [pltpu.VMEM((200, 256), F32), pltpu.VMEM((240, 256), F32)],
    )(zh.reshape(1), amps, other, order, choose)
    two = lax.all_to_all(two, ("x", "y", "core"), 0, 0, tiled=True)
    one = lax.all_to_all(one, "y", 0, 0, tiled=True)
    ordered = [w for pair in zip(along, across) for w in pair]
    partial = call(
        product_kernel, 0, 11, [(1152, 128)],
        [pltpu.VMEM((256, 768), BF16)] * 2 + [pltpu.VMEM((5, 160, 256), BF16)] * 2,
    )(one, two, turn, *ordered)
    got = lax.all_to_all(partial, ("y", "zh", "col"), 0, 0, tiled=True)
    r = ((x * 4 + y) * 2 + zh) * 2 + core
    place = jnp.stack([x, core, r * 3, col * 5, window_start[0]])
    new, inc = call(
        final_kernel, 3, 4, [(5, 3, 1152)] * 2,
        [pltpu.VMEM((192, 128), F32), pltpu.VMEM((3, 1152), F32), pltpu.VMEM((3, 1152), F32)],
    )(place, occupied_energy, virtual_energy, got, spread, virtual_energy.reshape(1, 192), res)
    return jnp.transpose(new, (1, 0, 2)), jnp.transpose(inc, (1, 0, 2))


def solution(mesh):
    fine = Mesh(mesh.devices.reshape(SIZES), AXES)
    split = P(("x", "y", "zh", "core"), "col", None)
    return jax.shard_map(
        body, mesh=fine, in_specs=(split, split, split, P(), P(), P()), out_specs=(split, split), check_vma=False
    )
```

time: 342 us -> 147 us (0.43)
  the two profiles are of different devices: /device:TPU:1 before, /device:TPU:8 now
where the time goes in v1:
time: 147 us; the launch traced here: 146 us
  waiting for transfers between devices  64.9 us (44%)
  starting transfers between devices  63.2 us (43%)
  Pallas kernels  11 us (7%)
  local copies, waits for them, and re-layouts  5.71 us (4%)
  between operations  1.49 us (1%)
    all_to_all x1, waiting for transfers between devices, body(): got = lax.all_to_all(partial, ('y', 'zh', 'col'), 0, 0, tiled=True)  42.4 us
    all_to_all x1, starting transfers between devices, body(): got = lax.all_to_all(partial, ('y', 'zh', 'col'), 0, 0, tiled=True)  16 us
    ppermute x1, starting transfers between devices, body(): other = lax.ppermute(amps, 'zh', [(0, 1), (1, 0)])  15.9 us
    ppermute x3, waiting for transfers between devices, body(): lax.ppermute(weights, 'x', [(s, (s - d) % 4) for s in range(4)])  15.6 us
    ppermute x3, starting transfers between devices, body(): lax.ppermute(weights, 'x', [(s, (s - d) % 4) for s in range(4)])  8.43 us
    ppermute x4, starting transfers between devices, body(): across = [lax.ppermute(w, 'core', [(0, 1), (1, 0)]) for w in along]  8.3 us
    all_to_all x1, starting transfers between devices, body(): two = lax.all_to_all(two, ('x', 'y', 'core'), 0, 0, tiled=True)  7.92 us
    all_to_all x1, starting transfers between devices, body(): one = lax.all_to_all(one, 'y', 0, 0, tiled=True)  6.65 us
  transfers between devices with their start and end apart: 11, of which 4 were waited for; matrix products, arithmetic and copies ran while one was open for 0% of the time, Pallas kernels for 0%

profile of v1, /device:TPU:8, one launch (start us, length us, event | category | flops | bytes accessed | tf_op | source)
XLA Modules:
  0.0 146.3 jit_solution(10764168685276768175)
XLA Ops:
  0.6 15.9 %collective-permute-start = (f32[5,3,1152]{2,1,0:T(4,128)}, f32[5,3,1152]{2,1,0:T(4,128)S(1)}, u32[]{:S(2)}, u32[]{:S(2)}) collective-permute-start(f32[5,3,1152]{2,1,0:T(4,128)} %bitcast.12), channel_id=1, source_target_pairs={{0,16},{16,0},{1,17},{17,1},{2,18},{18,2},{3,19},{19,3},{4,20},{20... | collective-permute-start | bytes 207368 | tf_op jit(solution)/shard_map/ppermute | solution.py:183
  16.5 3.2 %collective-permute-done.other_ref = f32[5,3,1152]{2,1,0:T(4,128)S(1)} collective-permute-done((f32[5,3,1152]{2,1,0:T(4,128)}, f32[5,3,1152]{2,1,0:T(4,128)S(1)}, u32[]{:S(2)}, u32[]{:S(2)}) %collective-permute-start) | collective-permute-done | bytes 69152 | tf_op jit(solution)/shard_map/ppermute | solution.py:183
  19.7 0.9 copy-done.3
  20.6 0.9 copy-done.6
  21.5 0.9 copy-done.7
  22.4 1.8 %shard_map.113 = (f32[4,200,256]{2,1,0:T(8,128)}, f32[32,48,128]{2,1,0:T(8,128)}) custom-call(s32[1]{0:T(128)} %bitcast.4.zh_ref, f32[5,3,1152]{2,1,0:T(4,128)S(1)} %bitcast.13, f32[5,3,1152]{2,1,0:T(4,128)S(1)} %collective-permute-done.other_ref, bf16[256,256]{1,0:T(8,128)(2,1)S(1)} %copy-done.3, bf16[256,256]{1,0:T(8,128)(2,1)S(1)} %copy-done.6), custom_call_target="tpu_custom_call" | custom-call | tf_op jit(solution)/shard_map/pallas_call | solution.py:189
  24.2 6.7 %all-to-all-start = ((f32[4,200,256]{2,1,0:T(8,128)}), f32[4,200,256]{2,1,0:T(8,128)}, u32[]{:S(2)}, u32[]{:S(2)}) async-start(f32[4,200,256]{2,1,0:T(8,128)} %get-tuple-element.6), calls=%async_computation | async-start | bytes 1638400 | tf_op jit(solution)/shard_map/all_to_all | solution.py:194
  31.4 2.9 %collective-permute-start.2 = (f32[5,128,256]{2,1,0:T(8,128)S(1)}, f32[5,128,256]{2,1,0:T(8,128)S(1)}, u32[]{:S(2)}, u32[]{:S(2)}) collective-permute-start(f32[5,128,256]{2,1,0:T(8,128)S(1)} %shard_map.114.refs_0_), channel_id=1, source_target_pairs={{0,384},{128,0},{256,128},{384,256},{1,385},{129,1},{257,129},{385... | collective-permute-start | bytes 1966088 | tf_op jit(solution)/shard_map/ppermute | solution.py:186
  34.3 2.7 %collective-permute-start.4 = (f32[5,128,256]{2,1,0:T(8,128)S(1)}, f32[5,128,256]{2,1,0:T(8,128)S(1)}, u32[]{:S(2)}, u32[]{:S(2)}) collective-permute-start(f32[5,128,256]{2,1,0:T(8,128)S(1)} %shard_map.114.refs_0_), channel_id=1, source_target_pairs={{0,256},{128,384},{256,0},{384,128},{1,257},{129,385},{257,1},{385... | collective-permute-start | bytes 1966088 | tf_op jit(solution)/shard_map/ppermute | solution.py:186
  37.1 2.8 %collective-permute-start.6 = (f32[5,128,256]{2,1,0:T(8,128)S(1)}, f32[5,128,256]{2,1,0:T(8,128)S(1)}, u32[]{:S(2)}, u32[]{:S(2)}) collective-permute-start(f32[5,128,256]{2,1,0:T(8,128)S(1)} %shard_map.114.refs_0_), channel_id=1, source_target_pairs={{0,128},{128,256},{256,384},{384,0},{1,129},{129,257},{257,385},{3... | collective-permute-start | bytes 1966088 | tf_op jit(solution)/shard_map/ppermute | solution.py:186
  39.9 7.9 %all-to-all-start.1 = ((f32[32,48,128]{2,1,0:T(8,128)}), f32[32,48,128]{2,1,0:T(8,128)}, u32[]{:S(2)}, u32[]{:S(2)}) async-start(f32[32,48,128]{2,1,0:T(8,128)} %get-tuple-element.7), calls=%async_computation.1 | async-start | bytes 1572864 | tf_op jit(solution)/shard_map/all_to_all | solution.py:193
  47.8 2.1 %collective-permute-start.1 = (f32[5,128,256]{2,1,0:T(8,128)S(1)}, f32[5,128,256]{2,1,0:T(8,128)S(1)}, u32[]{:S(2)}, u32[]{:S(2)}) collective-permute-start(f32[5,128,256]{2,1,0:T(8,128)S(1)} %shard_map.114.refs_0_), channel_id=1, source_target_pairs={{0,8},{8,0},{1,9},{9,1},{2,10},{10,2},{3,11},{11,3},{4,12},{12,4},... | collective-permute-start | bytes 1966088 | tf_op jit(solution)/shard_map/ppermute | solution.py:188
  49.9 15.6 %collective-permute-done.2.refs_2_ = f32[5,128,256]{2,1,0:T(8,128)S(1)} collective-permute-done((f32[5,128,256]{2,1,0:T(8,128)S(1)}, f32[5,128,256]{2,1,0:T(8,128)S(1)}, u32[]{:S(2)}, u32[]{:S(2)}) %collective-permute-start.2) | collective-permute-done | bytes 655392 | tf_op jit(solution)/shard_map/ppermute | solution.py:186
  65.4 1.9 %collective-permute-start.3 = (f32[5,128,256]{2,1,0:T(8,128)S(1)}, f32[5,128,256]{2,1,0:T(8,128)}, u32[]{:S(2)}, u32[]{:S(2)}) collective-permute-start(f32[5,128,256]{2,1,0:T(8,128)S(1)} %collective-permute-done.2.refs_2_), channel_id=1, source_target_pairs={{0,8},{8,0},{1,9},{9,1},{2,10},{10,2},{3,11},{11,3},{4,12},{12,4},... | collective-permute-start | bytes 1966088 | tf_op jit(solution)/shard_map/ppermute | solution.py:188
  67.4 2.4 %collective-permute-start.5 = (f32[5,128,256]{2,1,0:T(8,128)S(1)}, f32[5,128,256]{2,1,0:T(8,128)}, u32[]{:S(2)}, u32[]{:S(2)}) collective-permute-start(f32[5,128,256]{2,1,0:T(8,128)S(1)} %collective-permute-done.4.refs_4_), channel_id=1, source_target_pairs={{0,8},{8,0},{1,9},{9,1},{2,10},{10,2},{3,11},{11,3},{4,12},{12,4},... | collective-permute-start | bytes 1966088 | tf_op jit(solution)/shard_map/ppermute | solution.py:188
  69.8 1.9 %collective-permute-start.7 = (f32[5,128,256]{2,1,0:T(8,128)S(1)}, f32[5,128,256]{2,1,0:T(8,128)}, u32[]{:S(2)}, u32[]{:S(2)}) collective-permute-start(f32[5,128,256]{2,1,0:T(8,128)S(1)} %collective-permute-done.6.refs_6_), channel_id=1, source_target_pairs={{0,8},{8,0},{1,9},{9,1},{2,10},{10,2},{3,11},{11,3},{4,12},{12,4},... | collective-permute-start | bytes 1966088 | tf_op jit(solution)/shard_map/ppermute | solution.py:188
  71.8 0.8 copy-done
  72.6 3.7 %all-to-all-done.1.two_ref = f32[32,48,128]{2,1,0:T(8,128)} async-done(((f32[32,48,128]{2,1,0:T(8,128)}), f32[32,48,128]{2,1,0:T(8,128)}, u32[]{:S(2)}, u32[]{:S(2)}) %all-to-all-start.1) | async-done | bytes 786464 | tf_op jit(solution)/shard_map/all_to_all | solution.py:193
  76.4 1.1 copy-done.1
  77.4 6.4 %shard_map.115 = f32[1152,128]{1,0:T(8,128)S(1)} custom-call(f32[4,200,256]{2,1,0:T(8,128)} %all-to-all-done.one_ref, f32[32,48,128]{2,1,0:T(8,128)} %all-to-all-done.1.two_ref, bf16[800,768]{1,0:T(8,128)(2,1)} %constant.39.clone.turn_ref, f32[5,128,256]{2,1,0:T(8,128)S(1)} %shard_map.114.refs_0_, f32[5,128,256]{2,1,0:T(8,128)S(1)} %copy-done.1, ...), custom_call_target="tpu_custom_call" | custom-call | tf_op jit(solution)/shard_map/pallas_call | solution.py:196
  83.9 0.9 all_to_all.15
  84.8 16.0 %all-to-all-start.2 = ((f32[64,18,128]{2,1,0:T(8,128)}), f32[64,18,128]{2,1,0:T(8,128)S(1)}, u32[]{:S(2)}, u32[]{:S(2)}) async-start(f32[64,18,128]{2,1,0:T(8,128)} %all_to_all.15), calls=%async_computation.2 | async-start | bytes 1572864 | tf_op jit(solution)/shard_map/all_to_all | solution.py:200
  101.6 42.4 %all-to-all-done.2 = f32[64,18,128]{2,1,0:T(8,128)S(1)} async-done(((f32[64,18,128]{2,1,0:T(8,128)}), f32[64,18,128]{2,1,0:T(8,128)S(1)}, u32[]{:S(2)}, u32[]{:S(2)}) %all-to-all-start.2) | async-done | bytes 589856 | tf_op jit(solution)/shard_map/all_to_all | solution.py:200
  144.1 2.2 %shard_map.116 = (f32[5,3,1152]{2,1,0:T(4,128)}, f32[5,3,1152]{2,1,0:T(4,128)}) custom-call(s32[5]{0:T(128)S(1)} %stack.19.place_ref, f32[40]{0:T(128)S(1)} %copy-done.10, f32[192]{0:T(256)S(1)} %copy-done.9, f32[1152,128]{1,0:T(8,128)S(1)} %all_to_all.17.got_ref, bf16[128,1280]{1,0:T(8,128)(2,1)S(1)} %copy-done.5, f32[1,192]{1,0:T(1,128)S(1)} %bitcast.15, ...), custom_call_target="tpu_custom_call" | custom-call | tf_op jit(solution)/shard_map/pallas_call | solution.py:203
  (27 shorter events, 0.8 us)
Async XLA Ops:
  0.6 30.2 %copy-start.2 = (f32[3,5,7680]{2,0,1:T(4,128)S(1)}, f32[3,5,7680]{2,0,1:T(4,128)}, u32[]{:S(2)}) copy-start(f32[3,5,7680]{2,0,1:T(4,128)} %param.11) | copy-start | bytes 1382404
  0.6 19.0 %collective-permute-start = (f32[5,3,1152]{2,1,0:T(4,128)}, f32[5,3,1152]{2,1,0:T(4,128)S(1)}, u32[]{:S(2)}, u32[]{:S(2)}) collective-permute-start(f32[5,3,1152]{2,1,0:T(4,128)} %bitcast.12), channel_id=1, source_target_pairs={{0,16},{16,0},{1,17},{17,1},{2,18},{18,2},{3,19},{19,3},{4,20},{20... | collective-permute-start | bytes 207368 | tf_op jit(solution)/shard_map/ppermute | solution.py:183
  19.7 0.9 copy-start.3
  20.6 0.9 copy-start.6
  21.5 0.9 copy-start.7
  22.4 8.5 %copy-start.4 = (bf16[256,256]{1,0:T(8,128)(2,1)S(1)}, bf16[256,256]{1,0:T(8,128)(2,1)}, u32[]{:S(2)}) copy-start(bf16[256,256]{1,0:T(8,128)(2,1)} %constant.37.clone.order_ref) | copy-start | bytes 393220
  24.2 15.7 %all-to-all-start = ((f32[4,200,256]{2,1,0:T(8,128)}), f32[4,200,256]{2,1,0:T(8,128)}, u32[]{:S(2)}, u32[]{:S(2)}) async-start(f32[4,200,256]{2,1,0:T(8,128)} %get-tuple-element.6), calls=%async_computation | async-start | bytes 1638400 | tf_op jit(solution)/shard_map/all_to_all | solution.py:194
  31.4 34.0 %collective-permute-start.2 = (f32[5,128,256]{2,1,0:T(8,128)S(1)}, f32[5,128,256]{2,1,0:T(8,128)S(1)}, u32[]{:S(2)}, u32[]{:S(2)}) collective-permute-start(f32[5,128,256]{2,1,0:T(8,128)S(1)} %shard_map.114.refs_0_), channel_id=1, source_target_pairs={{0,384},{128,0},{256,128},{384,256},{1,385},{129,1},{257,129},{385... | collective-permute-start | bytes 1966088 | tf_op jit(solution)/shard_map/ppermute | solution.py:186
  34.3 33.0 %collective-permute-start.4 = (f32[5,128,256]{2,1,0:T(8,128)S(1)}, f32[5,128,256]{2,1,0:T(8,128)S(1)}, u32[]{:S(2)}, u32[]{:S(2)}) collective-permute-start(f32[5,128,256]{2,1,0:T(8,128)S(1)} %shard_map.114.refs_0_), channel_id=1, source_target_pairs={{0,256},{128,384},{256,0},{384,128},{1,257},{129,385},{257,1},{385... | collective-permute-start | bytes 1966088 | tf_op jit(solution)/shard_map/ppermute | solution.py:186
  37.1 32.7 %collective-permute-start.6 = (f32[5,128,256]{2,1,0:T(8,128)S(1)}, f32[5,128,256]{2,1,0:T(8,128)S(1)}, u32[]{:S(2)}, u32[]{:S(2)}) collective-permute-start(f32[5,128,256]{2,1,0:T(8,128)S(1)} %shard_map.114.refs_0_), channel_id=1, source_target_pairs={{0,128},{128,256},{256,384},{384,0},{1,129},{129,257},{257,385},{3... | collective-permute-start | bytes 1966088 | tf_op jit(solution)/shard_map/ppermute | solution.py:186
  39.9 36.5 %all-to-all-start.1 = ((f32[32,48,128]{2,1,0:T(8,128)}), f32[32,48,128]{2,1,0:T(8,128)}, u32[]{:S(2)}, u32[]{:S(2)}) async-start(f32[32,48,128]{2,1,0:T(8,128)} %get-tuple-element.7), calls=%async_computation.1 | async-start | bytes 1572864 | tf_op jit(solution)/shard_map/all_to_all | solution.py:193
  47.8 23.9 %collective-permute-start.1 = (f32[5,128,256]{2,1,0:T(8,128)S(1)}, f32[5,128,256]{2,1,0:T(8,128)S(1)}, u32[]{:S(2)}, u32[]{:S(2)}) collective-permute-start(f32[5,128,256]{2,1,0:T(8,128)S(1)} %shard_map.114.refs_0_), channel_id=1, source_target_pairs={{0,8},{8,0},{1,9},{9,1},{2,10},{10,2},{3,11},{11,3},{4,12},{12,4},... | collective-permute-start | bytes 1966088 | tf_op jit(solution)/shard_map/ppermute | solution.py:188
  65.4 10.9 %collective-permute-start.3 = (f32[5,128,256]{2,1,0:T(8,128)S(1)}, f32[5,128,256]{2,1,0:T(8,128)}, u32[]{:S(2)}, u32[]{:S(2)}) collective-permute-start(f32[5,128,256]{2,1,0:T(8,128)S(1)} %collective-permute-done.2.refs_2_), channel_id=1, source_target_pairs={{0,8},{8,0},{1,9},{9,1},{2,10},{10,2},{3,11},{11,3},{4,12},{12,4},... | collective-permute-start | bytes 1966088 | tf_op jit(solution)/shard_map/ppermute | solution.py:188
  67.4 9.0 %collective-permute-start.5 = (f32[5,128,256]{2,1,0:T(8,128)S(1)}, f32[5,128,256]{2,1,0:T(8,128)}, u32[]{:S(2)}, u32[]{:S(2)}) collective-permute-start(f32[5,128,256]{2,1,0:T(8,128)S(1)} %collective-permute-done.4.refs_4_), channel_id=1, source_target_pairs={{0,8},{8,0},{1,9},{9,1},{2,10},{10,2},{3,11},{11,3},{4,12},{12,4},... | collective-permute-start | bytes 1966088 | tf_op jit(solution)/shard_map/ppermute | solution.py:188
  69.8 6.5 %collective-permute-start.7 = (f32[5,128,256]{2,1,0:T(8,128)S(1)}, f32[5,128,256]{2,1,0:T(8,128)}, u32[]{:S(2)}, u32[]{:S(2)}) collective-permute-start(f32[5,128,256]{2,1,0:T(8,128)S(1)} %collective-permute-done.6.refs_6_), channel_id=1, source_target_pairs={{0,8},{8,0},{1,9},{9,1},{2,10},{10,2},{3,11},{11,3},{4,12},{12,4},... | collective-permute-start | bytes 1966088 | tf_op jit(solution)/shard_map/ppermute | solution.py:188
  71.7 0.8 copy-start
  76.3 1.1 copy-start.1
  84.8 59.2 %copy-start.5 = (bf16[128,1280]{1,0:T(8,128)(2,1)S(1)}, bf16[128,1280]{1,0:T(8,128)(2,1)}, u32[]{:S(2)}) copy-start(bf16[128,1280]{1,0:T(8,128)(2,1)} %constant.40.clone.spread_ref) | copy-start | bytes 983044
  84.8 59.3 %copy-start.8 = (f32[3,5,1152]{2,0,1:T(4,128)S(1)}, f32[3,5,1152]{2,0,1:T(4,128)}, u32[]{:S(2)}) copy-start(f32[3,5,1152]{2,0,1:T(4,128)} %param.12) | copy-start | bytes 207364
  84.8 59.3 %copy-start.9 = (f32[192]{0:T(256)S(1)}, f32[192]{0:T(256)}, u32[]{:S(2)}) copy-start(f32[192]{0:T(256)} %va_ref.1) | copy-start | bytes 2308
  84.8 59.3 %copy-start.10 = (f32[40]{0:T(128)S(1)}, f32[40]{0:T(128)}, u32[]{:S(2)}) copy-start(f32[40]{0:T(128)} %occ_ref.1) | copy-start | bytes 484
  84.8 59.2 %all-to-all-start.2 = ((f32[64,18,128]{2,1,0:T(8,128)}), f32[64,18,128]{2,1,0:T(8,128)S(1)}, u32[]{:S(2)}, u32[]{:S(2)}) async-start(f32[64,18,128]{2,1,0:T(8,128)} %all_to_all.15), calls=%async_computation.2 | async-start | bytes 1572864 | tf_op jit(solution)/shard_map/all_to_all | solution.py:200

commit v2 on v1

v2 whole, which is shorter than its diff:
```python
import jax
import jax.numpy as jnp
from jax import lax
from jax.experimental import pallas as pl
from jax.experimental.pallas import tpu as pltpu
from jax.sharding import Mesh, PartitionSpec as P

AXES = ("x", "y", "zh", "core", "col")
SIZES = (4, 4, 2, 2, 8)
F32, BF16 = jnp.float32, jnp.bfloat16
VMEM = pl.BlockSpec(memory_space=pltpu.VMEM)
SMEM = pl.BlockSpec(memory_space=pltpu.SMEM)
NT = (((1,), (1,)), ((), ()))
NN = (((1,), (0,)), ((), ()))


def index(shape, axis):
    return lax.broadcasted_iota(jnp.int32, shape, axis)


def third(n, count):
    return sum((n >= 3 * s).astype(jnp.int32) for s in range(1, count))


def hot(mask):
    return jnp.where(mask, 1.0, 0.0).astype(BF16)


def order_matrix():
    n = index((1, 256), 1)
    q = n & 7
    zh = third(q, 2)
    v = (n >> 6) * 48 + ((n >> 4) & 3) * 12 + zh * 6 + ((n >> 3) & 1) * 3 + q - zh * 3
    v = jnp.where(q < 6, v, -1)
    return hot(index((256, 256), 0) == v)


def choose_matrix():
    n = index((1, 256), 1)
    block = sum((n >= 24 * s).astype(jnp.int32) for s in range(1, 11))
    q = n - block * 24
    yz = third(q, 8)
    v = (block >> 1) * 48 + (block & 1) * 3 + yz * 6 + q - yz * 3
    v = jnp.where(block < 8, v, -1)
    return hot(index((256, 256), 0) == v)


def turn_matrix():
    n = index((1, 768), 1)
    i, q = n >> 7, n & 127
    k = sum((q >= 24 * s).astype(jnp.int32) for s in range(1, 6))
    q = q - k * 24
    yz = third(q, 8)
    row = k * 192 + (yz >> 1) * 48 + (i & 1) * 24 + (yz & 1) * 9 + (i >> 1) * 3 + q - yz * 3
    row = jnp.where(k < 5, row, -1)
    return hot(index((960, 768), 0) == row)


def spread_matrix():
    n = index((1, 1280), 1)
    j, q = n >> 8, n & 255
    x = sum((q >= 48 * s).astype(jnp.int32) for s in range(1, 6))
    q = q - x * 48
    core = third(q, 2)
    row = (x * 2 + core) * 16 + j * 3 + q - core * 3
    row = jnp.where((x < 4) & (q < 6), row, -1)
    return hot(index((128, 1280), 0) == row)


def dot(a, b, dims=NN):
    return lax.dot_general(a, b, dims, preferred_element_type=F32)


def split2(v):
    high = v.astype(BF16)
    return high, (v - high.astype(F32)).astype(BF16)


def moved(v, hot):
    high = v.astype(BF16)
    rest = v - high.astype(F32)
    mid = rest.astype(BF16)
    low = (rest - mid.astype(F32)).astype(BF16)
    return (dot(low, hot) + dot(mid, hot)) + dot(high, hot)


def lanes192(ref, lead, n):
    if n % 2 == 0:
        return ref[lead, :, n * 192:n * 192 + 256]
    return pltpu.roll(ref[lead, :, n * 192 - 64:n * 192 + 192], 192, 1)


def weights_kernel(ints_ref, out_ref, mark_ref):
    out_ref[...] = jnp.zeros_like(out_ref)
    mark_ref[...] = jnp.zeros_like(mark_ref)
    lane = index((3, 128), 1)
    for k in range(5):
        for j in range(20):
            at = j // 5 * 16 + j % 5 * 3
            near = lanes192(ints_ref, k, j)
            far = pltpu.roll(lanes192(ints_ref, k, j + 20), 64, 1)
            out_ref[k, at:at + 3, :128] = near[:, :128]
            out_ref[k, at:at + 3, 128:256] = jnp.where(lane < 64, near[:, 128:], far[:, :128])
            out_ref[k, at:at + 3, 256:] = far[:, 128:]


def amps_kernel(zh_ref, own_ref, other_ref, mark_ref, one_ref, two_ref, rows):
    first = zh_ref[0] == 0
    rows[...] = jnp.zeros_like(rows)
    one_ref[...] = jnp.zeros_like(one_ref)
    for k in range(5):
        for p in range(3):
            own = own_ref[k, :, p * 384:(p + 1) * 384]
            other = other_ref[k, :, p * 384:(p + 1) * 384]
            for zh, v in ((0, jnp.where(first, own, other)), (1, jnp.where(first, other, own))):
                at = k * 24 + zh * 9 + p * 3
                for y in range(4):
                    one_ref[y, at:at + 3, :] = v
                at = k * 48 + p * 16 + zh * 3
                rows[at:at + 3, :] = v[:, :256]
                rows[at + 8:at + 11, :] = pltpu.roll(v[:, 128:], 192, 1)
    chosen = moved(rows[...], choose_matrix())
    lane = index((48, 128), 1)
    for n in range(8):
        part = jnp.zeros((48, 128), F32)
        for k in range(5):
            v = pltpu.roll(chosen[k * 48:(k + 1) * 48, :], (k * 24 - n * 24) % 256, 1)[:, :128]
            part = jnp.where((lane >= k * 24) & (lane < k * 24 + 24), v, part)
        for y in range(4):
            two_ref[(n // 2 * 4 + y) * 2 + n % 2] = part


def product_kernel(one_ref, two_ref, *refs):
    weights, out_ref = refs[:8], refs[8]
    two_high, two_low, mixed_high, mixed_low = refs[9:]
    for i in range(6):
        high, low = split2(two_ref[:, i * 8:(i + 1) * 8, :].reshape(256, 128))
        two_high[:, i * 128:(i + 1) * 128] = high
        two_low[:, i * 128:(i + 1) * 128] = low
    order, turn = order_matrix(), turn_matrix()
    lane = index((24, 256), 1)
    for k in range(5):
        turn_k = turn[k * 192:(k + 1) * 192, :]
        swapped = dot(dot(turn_k, two_low[...], NT).astype(BF16), order, NT)
        swapped += dot(dot(turn_k, two_high[...], NT).astype(BF16), order, NT)
        straight = []
        for y in range(4):
            v = one_ref[y, k * 24:(k + 1) * 24, :]
            straight.append(jnp.where(lane < 192, v[:, :256], 0.0))
            straight.append(jnp.where(lane < 192, pltpu.roll(v[:, 128:], 192, 1), 0.0))
        high, low = split2(2.0 * jnp.concatenate(straight, 0) - swapped)
        mixed_high[k] = high
        mixed_low[k] = low
    for z in range(4):
        total = jnp.zeros((192, 256), F32)
        for k in range(5):
            rows = [ref[k, z * 16:(z + 1) * 16, :] for ref in weights]
            near = [v[:, :256] for v in rows]
            far = [pltpu.roll(v[:, 128:], 192, 1) for v in rows]
            high, low = split2(jnp.concatenate(near + far, 0))
            total += dot(mixed_high[k], low, NT) + dot(mixed_low[k], high, NT) + dot(mixed_high[k], high, NT)
        for yz in range(8):
            for half in range(2):
                for e in range(2):
                    to = (yz * 8 + z + 4 * half) * 18 + e * 9
                    at = yz // 2 * 48 + e * 24 + yz % 2 * 9
                    out_ref[to:to + 9, :] = total[at:at + 9, half * 128:(half + 1) * 128]


def final_kernel(place_ref, occ_ref, va_ref, got_ref, vb_ref, res_ref, new_ref, inc_ref, sums, cyc, den):
    sums[...] = jnp.zeros_like(sums)
    for yz in range(8):
        total = got_ref[yz * 144:yz * 144 + 18, :]
        for z in range(1, 8):
            at = (yz * 8 + z) * 18
            total += got_ref[at:at + 18, :]
        sums[yz * 24:yz * 24 + 18, :] = total
    v = pltpu.roll(sums[...], place_ref[0] * 32, 1)
    lane = lax.broadcasted_iota(jnp.int32, v.shape, 1)
    other = jnp.where((lane & 16) == 0, pltpu.roll(v, 112, 1), pltpu.roll(v, 16, 1))
    v = jnp.where(place_ref[1] == 0, v, other)
    wide = moved(v, spread_matrix())
    row = lax.broadcasted_iota(jnp.int32, (3, 192), 0)
    va = [va_ref[place_ref[2] + m] for m in range(3)]
    va = jnp.where(row == 0, va[0], jnp.where(row == 1, va[1], va[2]))
    base = vb_ref[...] + va
    for i in range(6):
        den[:, i * 192:(i + 1) * 192] = base - occ_ref[place_ref[4] + i]
    for j in range(5):
        total = wide[0:24, j * 256:(j + 1) * 256]
        for yz in range(1, 8):
            total += pltpu.roll(wide[yz * 24:(yz + 1) * 24, j * 256:(j + 1) * 256], yz * 6, 1)
        for i in range(6):
            cyc[:, i * 192:(i + 1) * 192] = total[i % 2 * 9 + i // 2 * 3:i % 2 * 9 + i // 2 * 3 + 3, :192]
        new = res_ref[j] + cyc[...]
        new_ref[j] = new
        inc_ref[j] = new / (den[...] - occ_ref[place_ref[3] + j])


def call(kernel, n_smem, n_vmem, outs, scratch):
    shapes = [jax.ShapeDtypeStruct(s, F32) for s in outs]
    return pl.pallas_call(
        kernel,
        out_shape=shapes if len(shapes) > 1 else shapes[0],
        in_specs=[SMEM] * n_smem + [VMEM] * n_vmem,
        out_specs=[VMEM] * len(shapes) if len(shapes) > 1 else VMEM,
        scratch_shapes=scratch,
        compiler_params=pltpu.CompilerParams(vmem_limit_bytes=48 * 1024 * 1024),
    )


def body(amplitudes, integrals, residual, occupied_energy, virtual_energy, window_start):
    x, y, zh, core, col = [lax.axis_index(a).astype(jnp.int32) for a in AXES]
    amps = jnp.transpose(amplitudes, (1, 0, 2))
    ints = jnp.transpose(integrals, (1, 0, 2))
    res = jnp.transpose(residual, (1, 0, 2))
    other = lax.ppermute(amps, "zh", [(0, 1), (1, 0)])
    weights, mark = call(weights_kernel, 0, 1, [(5, 64, 384), (8, 128)], [])(ints)
    along = [weights] + [
        lax.ppermute(weights, "x", [(s, (s - d) % 4) for s in range(4)]) for d in (1, 2, 3)
    ]
    across = [lax.ppermute(w, "core", [(0, 1), (1, 0)]) for w in along]
    one, two = call(amps_kernel, 1, 3, [(4, 120, 384), (32, 48, 128)], [pltpu.VMEM((240, 256), F32)])(
        zh.reshape(1), amps, other, mark
    )
    two = lax.all_to_all(two, ("x", "y", "core"), 0, 0, tiled=True)
    one = lax.all_to_all(one, "y", 0, 0, tiled=True)
    ordered = [w for pair in zip(along, across) for w in pair]
    partial = call(
        product_kernel, 0, 10, [(1152, 128)],
        [pltpu.VMEM((256, 768), BF16)] * 2 + [pltpu.VMEM((5, 192, 256), BF16)] * 2,
    )(one, two, *ordered)
    got = lax.all_to_all(partial.reshape(64, 1, 2304), ("y", "zh", "col"), 0, 0, tiled=True).reshape(1152, 128)
    r = ((x * 4 + y) * 2 + zh) * 2 + core
    place = jnp.stack([x, core, r * 3, col * 5, window_start[0]])
    new, inc = call(
        final_kernel, 3, 3, [(5, 3, 1152)] * 2,
        [pltpu.VMEM((192, 128), F32), pltpu.VMEM((3, 1152), F32), pltpu.VMEM((3, 1152), F32)],
    )(place, occupied_energy, virtual_energy, got, virtual_energy.reshape(1, 192), res)
    return jnp.transpose(new, (1, 0, 2)), jnp.transpose(inc, (1, 0, 2))


def solution(mesh):
    fine = Mesh(mesh.devices.reshape(SIZES), AXES)
    split = P(("x", "y", "zh", "core"), "col", None)
    return jax.shard_map(
        body, mesh=fine, in_specs=(split, split, split, P(), P(), P()), out_specs=(split, split), check_vma=False
    )
```

time: 147 us -> 128 us (0.87)
  waiting for transfers between devices: 64.9 us -> 48 us
  Pallas kernels: 11 us -> 13.5 us
  starting transfers between devices: 63.2 us -> 60.7 us
  local copies, waits for them, and re-layouts: 5.71 us -> 3.65 us
    all_to_all x1, waiting for transfers between devices: 42.4 us -> 34.1 us  [body(): lax.all_to_all(partial.reshape(64, 1, 2304), ('y', 'zh', 'col'), 0, 0, ti...]
    ppermute x3, waiting for transfers between devices: 15.6 us -> 8.1 us  [body(): lax.ppermute(weights, 'x', [(s, (s - d) % 4) for s in range(4)])]
    ppermute x1, waiting for transfers between devices: 3.15 us -> 0.01 us  [body(): other = lax.ppermute(amps, 'zh', [(0, 1), (1, 0)])]
    pallas_call x4, Pallas kernels: 11 us -> 13.5 us  [the longest x1 6.82 us: body(): call(product_kernel, 0, 10, [(1152, 128)], [pltpu.VMEM((256, 768), BF16)]...]
    all_to_all x1, waiting for transfers between devices: 3.75 us -> 5.8 us  [body(): two = lax.all_to_all(two, ('x', 'y', 'core'), 0, 0, tiled=True)]
    unnamed x22 -> x14, local copies, waits for them, and re-layouts: 4.64 us -> 3.56 us
  transfers between devices with their start and end apart: 11 -> 11, of which waited for: 4 -> 3; matrix products, arithmetic and copies ran while one was open for 0% -> 0% of each run, Pallas kernels for 0% -> 2%
where the time goes in v2:
time: 128 us; the launch traced here: 127 us
  starting transfers between devices  60.7 us (47%)
  waiting for transfers between devices  48 us (38%)
  Pallas kernels  13.5 us (11%)
  local copies, waits for them, and re-layouts  3.65 us (3%)
  between operations  1.47 us (1%)
    all_to_all x1, waiting for transfers between devices, body(): lax.all_to_all(partial.reshape(64, 1, 2304), ('y', 'zh', 'col'), 0, 0, ti...  34.1 us
    ppermute x1, starting transfers between devices, body(): other = lax.ppermute(amps, 'zh', [(0, 1), (1, 0)])  15.7 us
    all_to_all x1, starting transfers between devices, body(): lax.all_to_all(partial.reshape(64, 1, 2304), ('y', 'zh', 'col'), 0, 0, ti...  14.8 us
    ppermute x3, starting transfers between devices, body(): lax.ppermute(weights, 'x', [(s, (s - d) % 4) for s in range(4)])  9.82 us
    ppermute x4, starting transfers between devices, body(): across = [lax.ppermute(w, 'core', [(0, 1), (1, 0)]) for w in along]  8.3 us
    ppermute x3, waiting for transfers between devices, body(): lax.ppermute(weights, 'x', [(s, (s - d) % 4) for s in range(4)])  8.1 us
    pallas_call x1, Pallas kernels, body(): call(product_kernel, 0, 10, [(1152, 128)], [pltpu.VMEM((256, 768), BF16)]...  6.82 us
    all_to_all x1, starting transfers between devices, body(): two = lax.all_to_all(two, ('x', 'y', 'core'), 0, 0, tiled=True)  6.76 us
  transfers between devices with their start and end apart: 11, of which 3 were waited for; matrix products, arithmetic and copies ran while one was open for 0% of the time, Pallas kernels for 2%

profile of v2, /device:TPU:8, one launch (start us, length us, event | category | flops | bytes accessed | tf_op | source)
XLA Modules:
  0.0 127.3 jit_solution(13090607630578858844)
XLA Ops:
  0.6 15.7 %collective-permute-start = (f32[5,3,1152]{2,1,0:T(4,128)}, f32[5,3,1152]{2,1,0:T(4,128)S(1)}, u32[]{:S(2)}, u32[]{:S(2)}) collective-permute-start(f32[5,3,1152]{2,1,0:T(4,128)} %bitcast.15), channel_id=1, source_target_pairs={{0,16},{16,0},{1,17},{17,1},{2,18},{18,2},{3,19},{19,3},{4,20},{20... | collective-permute-start | bytes 207368 | tf_op jit(solution)/shard_map/ppermute | solution.py:217
  16.4 1.1 copy-done
  17.4 2.8 %shard_map.77 = (f32[5,64,384]{2,1,0:T(8,128)S(1)}, f32[8,128]{1,0:T(8,128)S(1)}) custom-call(f32[5,3,7680]{2,1,0:T(4,128)S(1)} %bitcast.14), custom_call_target="tpu_custom_call" | custom-call | tf_op jit(solution)/shard_map/pallas_call | solution.py:218
  20.2 1.8 %shard_map.78 = (f32[4,120,384]{2,1,0:T(8,128)}, f32[32,48,128]{2,1,0:T(8,128)}) custom-call(s32[1]{0:T(128)} %bitcast.4.zh_ref, f32[5,3,1152]{2,1,0:T(4,128)S(1)} %bitcast.16, f32[5,3,1152]{2,1,0:T(4,128)S(1)} %collective-permute-done.other_ref, f32[8,128]{1,0:T(8,128)S(1)} %get-tuple-element.8.mark_ref), custom_call_target="tpu_custom_call" | custom-call | tf_op jit(solution)/shard_map/pallas_call | solution.py:223
  22.0 5.2 %all-to-all-start = ((f32[4,120,384]{2,1,0:T(8,128)}), f32[4,120,384]{2,1,0:T(8,128)S(1)}, u32[]{:S(2)}, u32[]{:S(2)}) async-start(f32[4,120,384]{2,1,0:T(8,128)} %get-tuple-element.9), calls=%async_computation | async-start | bytes 1474560 | tf_op jit(solution)/shard_map/all_to_all | solution.py:227
  27.3 4.3 %collective-permute-start.2 = (f32[5,64,384]{2,1,0:T(8,128)S(1)}, f32[5,64,384]{2,1,0:T(8,128)S(1)}, u32[]{:S(2)}, u32[]{:S(2)}) collective-permute-start(f32[5,64,384]{2,1,0:T(8,128)S(1)} %get-tuple-element.11.refs_0_), channel_id=1, source_target_pairs={{0,384},{128,0},{256,128},{384,256},{1,385},{129,1},{257,129},{385... | collective-permute-start | bytes 1474568 | tf_op jit(solution)/shard_map/ppermute | solution.py:220
  31.6 2.7 %collective-permute-start.4 = (f32[5,64,384]{2,1,0:T(8,128)S(1)}, f32[5,64,384]{2,1,0:T(8,128)S(1)}, u32[]{:S(2)}, u32[]{:S(2)}) collective-permute-start(f32[5,64,384]{2,1,0:T(8,128)S(1)} %get-tuple-element.11.refs_0_), channel_id=1, source_target_pairs={{0,256},{128,384},{256,0},{384,128},{1,257},{129,385},{257,1},{385... | collective-permute-start | bytes 1474568 | tf_op jit(solution)/shard_map/ppermute | solution.py:220
  34.3 2.8 %collective-permute-start.6 = (f32[5,64,384]{2,1,0:T(8,128)S(1)}, f32[5,64,384]{2,1,0:T(8,128)S(1)}, u32[]{:S(2)}, u32[]{:S(2)}) collective-permute-start(f32[5,64,384]{2,1,0:T(8,128)S(1)} %get-tuple-element.11.refs_0_), channel_id=1, source_target_pairs={{0,128},{128,256},{256,384},{384,0},{1,129},{129,257},{257,385},{3... | collective-permute-start | bytes 1474568 | tf_op jit(solution)/shard_map/ppermute | solution.py:220
  37.1 0.0 all-to-all-done.one_ref
  37.1 6.8 %all-to-all-start.1 = ((f32[32,48,128]{2,1,0:T(8,128)}), f32[32,48,128]{2,1,0:T(8,128)S(1)}, u32[]{:S(2)}, u32[]{:S(2)}) async-start(f32[32,48,128]{2,1,0:T(8,128)} %get-tuple-element.10), calls=%async_computation.1 | async-start | bytes 1572864 | tf_op jit(solution)/shard_map/all_to_all | solution.py:226
  43.9 2.1 %collective-permute-start.1 = (f32[5,64,384]{2,1,0:T(8,128)S(1)}, f32[5,64,384]{2,1,0:T(8,128)S(1)}, u32[]{:S(2)}, u32[]{:S(2)}) collective-permute-start(f32[5,64,384]{2,1,0:T(8,128)S(1)} %get-tuple-element.11.refs_0_), channel_id=1, source_target_pairs={{0,8},{8,0},{1,9},{9,1},{2,10},{10,2},{3,11},{11,3},{4,12},{12,4},... | collective-permute-start | bytes 1474568 | tf_op jit(solution)/shard_map/ppermute | solution.py:222
  46.0 8.1 %collective-permute-done.2.refs_2_ = f32[5,64,384]{2,1,0:T(8,128)S(1)} collective-permute-done((f32[5,64,384]{2,1,0:T(8,128)S(1)}, f32[5,64,384]{2,1,0:T(8,128)S(1)}, u32[]{:S(2)}, u32[]{:S(2)}) %collective-permute-start.2) | collective-permute-done | bytes 491552 | tf_op jit(solution)/shard_map/ppermute | solution.py:220
  54.1 1.9 %collective-permute-start.3 = (f32[5,64,384]{2,1,0:T(8,128)S(1)}, f32[5,64,384]{2,1,0:T(8,128)}, u32[]{:S(2)}, u32[]{:S(2)}) collective-permute-start(f32[5,64,384]{2,1,0:T(8,128)S(1)} %collective-permute-done.2.refs_2_), channel_id=1, source_target_pairs={{0,8},{8,0},{1,9},{9,1},{2,10},{10,2},{3,11},{11,3},{4,12},{12,4},... | collective-permute-start | bytes 1474568 | tf_op jit(solution)/shard_map/ppermute | solution.py:222
  56.0 2.4 %collective-permute-start.5 = (f32[5,64,384]{2,1,0:T(8,128)S(1)}, f32[5,64,384]{2,1,0:T(8,128)}, u32[]{:S(2)}, u32[]{:S(2)}) collective-permute-start(f32[5,64,384]{2,1,0:T(8,128)S(1)} %collective-permute-done.4.refs_4_), channel_id=1, source_target_pairs={{0,8},{8,0},{1,9},{9,1},{2,10},{10,2},{3,11},{11,3},{4,12},{12,4},... | collective-permute-start | bytes 1474568 | tf_op jit(solution)/shard_map/ppermute | solution.py:222
  58.4 1.9 %collective-permute-start.7 = (f32[5,64,384]{2,1,0:T(8,128)S(1)}, f32[5,64,384]{2,1,0:T(8,128)}, u32[]{:S(2)}, u32[]{:S(2)}) collective-permute-start(f32[5,64,384]{2,1,0:T(8,128)S(1)} %collective-permute-done.6.refs_6_), channel_id=1, source_target_pairs={{0,8},{8,0},{1,9},{9,1},{2,10},{10,2},{3,11},{11,3},{4,12},{12,4},... | collective-permute-start | bytes 1474568 | tf_op jit(solution)/shard_map/ppermute | solution.py:222
  60.4 0.8 copy-done.1
  61.1 5.8 %all-to-all-done.1.two_ref = f32[32,48,128]{2,1,0:T(8,128)S(1)} async-done(((f32[32,48,128]{2,1,0:T(8,128)}), f32[32,48,128]{2,1,0:T(8,128)S(1)}, u32[]{:S(2)}, u32[]{:S(2)}) %all-to-all-start.1) | async-done | bytes 786464 | tf_op jit(solution)/shard_map/all_to_all | solution.py:226
  67.0 1.0 copy-done.2
  68.0 6.8 %shard_map.79 = f32[1152,128]{1,0:T(8,128)} custom-call(f32[4,120,384]{2,1,0:T(8,128)S(1)} %all-to-all-done.one_ref, f32[32,48,128]{2,1,0:T(8,128)S(1)} %all-to-all-done.1.two_ref, f32[5,64,384]{2,1,0:T(8,128)S(1)} %get-tuple-element.11.refs_0_, f32[5,64,384]{2,1,0:T(8,128)S(1)} %copy-done.2, f32[5,64,384]{2,1,0:T(8,128)S(1)} %collective-permute-done.2.refs_2_, ...), custom_call_target="tpu_custom_call" | custom-call | tf_op jit(solution)/shard_map/pallas_call | solution.py:229
  74.8 14.8 %all-to-all-start.2 = ((f32[64,1,2304]{2,1,0:T(1,128)}), f32[64,1,2304]{2,1,0:T(1,128)S(1)}, u32[]{:S(2)}, u32[]{:S(2)}) async-start(f32[64,1,2304]{2,1,0:T(1,128)} %bitcast.7), calls=%async_computation.2 | async-start | bytes 1179648 | tf_op jit(solution)/shard_map/all_to_all | solution.py:233
  90.3 0.1 stack.19.place_ref
  90.4 34.1 %all-to-all-done.2 = f32[64,1,2304]{2,1,0:T(1,128)S(1)} async-done(((f32[64,1,2304]{2,1,0:T(1,128)}), f32[64,1,2304]{2,1,0:T(1,128)S(1)}, u32[]{:S(2)}, u32[]{:S(2)}) %all-to-all-start.2) | async-done | bytes 589856 | tf_op jit(solution)/shard_map/all_to_all | solution.py:233
  124.5 0.7 copy-done.5
  125.2 2.1 %shard_map.80 = (f32[5,3,1152]{2,1,0:T(4,128)}, f32[5,3,1152]{2,1,0:T(4,128)}) custom-call(s32[5]{0:T(128)S(1)} %stack.19.place_ref, f32[40]{0:T(128)S(1)} %copy-done.6, f32[192]{0:T(256)S(1)} %copy-done.5, f32[1152,128]{1,0:T(8,128)S(1)} %bitcast.13, f32[1,192]{1,0:T(1,128)S(1)} %bitcast.18, f32[5,3,1152]{2,1,0:T(4,128)S(1)} %bitcast.17), custom_call_target="tpu_custom_call" | custom-call | tf_op jit(solution)/shard_map/pallas_call | solution.py:236
  (17 shorter events, 0.0 us)
Async XLA Ops:
  0.6 19.6 %collective-permute-start = (f32[5,3,1152]{2,1,0:T(4,128)}, f32[5,3,1152]{2,1,0:T(4,128)S(1)}, u32[]{:S(2)}, u32[]{:S(2)}) collective-permute-start(f32[5,3,1152]{2,1,0:T(4,128)} %bitcast.15), channel_id=1, source_target_pairs={{0,16},{16,0},{1,17},{17,1},{2,18},{18,2},{3,19},{19,3},{4,20},{20... | collective-permute-start | bytes 207368 | tf_op jit(solution)/shard_map/ppermute | solution.py:217
  16.4 1.1 copy-start
  17.4 2.8 %copy-start.3 = (f32[3,5,1152]{2,0,1:T(4,128)S(1)}, f32[3,5,1152]{2,0,1:T(4,128)}, u32[]{:S(2)}) copy-start(f32[3,5,1152]{2,0,1:T(4,128)} %param.6) | copy-start | bytes 207364
  22.0 15.1 %all-to-all-start = ((f32[4,120,384]{2,1,0:T(8,128)}), f32[4,120,384]{2,1,0:T(8,128)S(1)}, u32[]{:S(2)}, u32[]{:S(2)}) async-start(f32[4,120,384]{2,1,0:T(8,128)} %get-tuple-element.9), calls=%async_computation | async-start | bytes 1474560 | tf_op jit(solution)/shard_map/all_to_all | solution.py:227
  27.3 26.8 %collective-permute-start.2 = (f32[5,64,384]{2,1,0:T(8,128)S(1)}, f32[5,64,384]{2,1,0:T(8,128)S(1)}, u32[]{:S(2)}, u32[]{:S(2)}) collective-permute-start(f32[5,64,384]{2,1,0:T(8,128)S(1)} %get-tuple-element.11.refs_0_), channel_id=1, source_target_pairs={{0,384},{128,0},{256,128},{384,256},{1,385},{129,1},{257,129},{385... | collective-permute-start | bytes 1474568 | tf_op jit(solution)/shard_map/ppermute | solution.py:220
  31.6 24.4 %collective-permute-start.4 = (f32[5,64,384]{2,1,0:T(8,128)S(1)}, f32[5,64,384]{2,1,0:T(8,128)S(1)}, u32[]{:S(2)}, u32[]{:S(2)}) collective-permute-start(f32[5,64,384]{2,1,0:T(8,128)S(1)} %get-tuple-element.11.refs_0_), channel_id=1, source_target_pairs={{0,256},{128,384},{256,0},{384,128},{1,257},{129,385},{257,1},{385... | collective-permute-start | bytes 1474568 | tf_op jit(solution)/shard_map/ppermute | solution.py:220
  34.3 24.1 %collective-permute-start.6 = (f32[5,64,384]{2,1,0:T(8,128)S(1)}, f32[5,64,384]{2,1,0:T(8,128)S(1)}, u32[]{:S(2)}, u32[]{:S(2)}) collective-permute-start(f32[5,64,384]{2,1,0:T(8,128)S(1)} %get-tuple-element.11.refs_0_), channel_id=1, source_target_pairs={{0,128},{128,256},{256,384},{384,0},{1,129},{129,257},{257,385},{3... | collective-permute-start | bytes 1474568 | tf_op jit(solution)/shard_map/ppermute | solution.py:220
  37.1 29.8 %all-to-all-start.1 = ((f32[32,48,128]{2,1,0:T(8,128)}), f32[32,48,128]{2,1,0:T(8,128)S(1)}, u32[]{:S(2)}, u32[]{:S(2)}) async-start(f32[32,48,128]{2,1,0:T(8,128)} %get-tuple-element.10), calls=%async_computation.1 | async-start | bytes 1572864 | tf_op jit(solution)/shard_map/all_to_all | solution.py:226
  43.9 16.4 %collective-permute-start.1 = (f32[5,64,384]{2,1,0:T(8,128)S(1)}, f32[5,64,384]{2,1,0:T(8,128)S(1)}, u32[]{:S(2)}, u32[]{:S(2)}) collective-permute-start(f32[5,64,384]{2,1,0:T(8,128)S(1)} %get-tuple-element.11.refs_0_), channel_id=1, source_target_pairs={{0,8},{8,0},{1,9},{9,1},{2,10},{10,2},{3,11},{11,3},{4,12},{12,4},... | collective-permute-start | bytes 1474568 | tf_op jit(solution)/shard_map/ppermute | solution.py:222
  54.1 12.9 %collective-permute-start.3 = (f32[5,64,384]{2,1,0:T(8,128)S(1)}, f32[5,64,384]{2,1,0:T(8,128)}, u32[]{:S(2)}, u32[]{:S(2)}) collective-permute-start(f32[5,64,384]{2,1,0:T(8,128)S(1)} %collective-permute-done.2.refs_2_), channel_id=1, source_target_pairs={{0,8},{8,0},{1,9},{9,1},{2,10},{10,2},{3,11},{11,3},{4,12},{12,4},... | collective-permute-start | bytes 1474568 | tf_op jit(solution)/shard_map/ppermute | solution.py:222
  56.0 11.0 %collective-permute-start.5 = (f32[5,64,384]{2,1,0:T(8,128)S(1)}, f32[5,64,384]{2,1,0:T(8,128)}, u32[]{:S(2)}, u32[]{:S(2)}) collective-permute-start(f32[5,64,384]{2,1,0:T(8,128)S(1)} %collective-permute-done.4.refs_4_), channel_id=1, source_target_pairs={{0,8},{8,0},{1,9},{9,1},{2,10},{10,2},{3,11},{11,3},{4,12},{12,4},... | collective-permute-start | bytes 1474568 | tf_op jit(solution)/shard_map/ppermute | solution.py:222
  58.4 8.5 %collective-permute-start.7 = (f32[5,64,384]{2,1,0:T(8,128)S(1)}, f32[5,64,384]{2,1,0:T(8,128)}, u32[]{:S(2)}, u32[]{:S(2)}) collective-permute-start(f32[5,64,384]{2,1,0:T(8,128)S(1)} %collective-permute-done.6.refs_6_), channel_id=1, source_target_pairs={{0,8},{8,0},{1,9},{9,1},{2,10},{10,2},{3,11},{11,3},{4,12},{12,4},... | collective-permute-start | bytes 1474568 | tf_op jit(solution)/shard_map/ppermute | solution.py:222
  60.3 0.8 copy-start.1
  67.0 1.0 copy-start.2
  74.8 49.7 %copy-start.4 = (f32[3,5,1152]{2,0,1:T(4,128)S(1)}, f32[3,5,1152]{2,0,1:T(4,128)}, u32[]{:S(2)}) copy-start(f32[3,5,1152]{2,0,1:T(4,128)} %param.8) | copy-start | bytes 207364
  74.8 49.7 %all-to-all-start.2 = ((f32[64,1,2304]{2,1,0:T(1,128)}), f32[64,1,2304]{2,1,0:T(1,128)S(1)}, u32[]{:S(2)}, u32[]{:S(2)}) async-start(f32[64,1,2304]{2,1,0:T(1,128)} %bitcast.7), calls=%async_computation.2 | async-start | bytes 1179648 | tf_op jit(solution)/shard_map/all_to_all | solution.py:233
  124.5 0.7 copy-start.5
  124.5 0.7 copy-start.6

commit v3 on v2

--- a/solution.py
+++ b/solution.py
@@ -30,7 +30,7 @@
     n = index((1, 256), 1)
     q = n & 7
     zh = third(q, 2)
-    v = (n >> 6) * 48 + ((n >> 4) & 3) * 12 + zh * 6 + ((n >> 3) & 1) * 3 + q - zh * 3
+    v = ((n >> 4) & 3) * 48 + (n >> 6) * 12 + zh * 6 + ((n >> 3) & 1) * 3 + q - zh * 3
     v = jnp.where(q < 6, v, -1)
     return hot(index((256, 256), 0) == v)
 
@@ -114,8 +114,7 @@
             other = other_ref[k, :, p * 384:(p + 1) * 384]
             for zh, v in ((0, jnp.where(first, own, other)), (1, jnp.where(first, other, own))):
                 at = k * 24 + zh * 9 + p * 3
-                for y in range(4):
-                    one_ref[y, at:at + 3, :] = v
+                one_ref[at:at + 3, :] = v
                 at = k * 48 + p * 16 + zh * 3
                 rows[at:at + 3, :] = v[:, :256]
                 rows[at + 8:at + 11, :] = pltpu.roll(v[:, 128:], 192, 1)
@@ -126,15 +125,33 @@
         for k in range(5):
             v = pltpu.roll(chosen[k * 48:(k + 1) * 48, :], (k * 24 - n * 24) % 256, 1)[:, :128]
             part = jnp.where((lane >= k * 24) & (lane < k * 24 + 24), v, part)
-        for y in range(4):
-            two_ref[(n // 2 * 4 + y) * 2 + n % 2] = part
-
-
-def product_kernel(one_ref, two_ref, *refs):
-    weights, out_ref = refs[:8], refs[8]
-    two_high, two_low, mixed_high, mixed_low = refs[9:]
+        two_ref[n] = part
+
+
+def pack_kernel(one_ref, two_ref, out_ref):
+    for y in range(4):
+        for part in range(3):
+            out_ref[y, part * 120:(part + 1) * 120, :] = one_ref[:, part * 128:(part + 1) * 128]
+        out_ref[y, 360:, :] = two_ref[...].reshape(384, 128)
+
+
+def combine_kernel(*refs):
+    weights, high_ref, low_ref = refs[:8], refs[8], refs[9]
+    for z in range(4):
+        for k in range(5):
+            rows = [ref[k, z * 16:(z + 1) * 16, :] for ref in weights]
+            near = [v[:, :256] for v in rows]
+            far = [pltpu.roll(v[:, 128:], 192, 1) for v in rows]
+            high, low = split2(jnp.concatenate(near + far, 0))
+            high_ref[z, k] = high
+            low_ref[z, k] = low
+
+
+def product_kernel(got_ref, high_ref, low_ref, out_ref, two_high, two_low, mixed_high, mixed_low):
     for i in range(6):
-        high, low = split2(two_ref[:, i * 8:(i + 1) * 8, :].reshape(256, 128))
+        starts = [360 + s * 48 + i * 8 for s in range(8)]
+        part = jnp.concatenate([got_ref[y, at:at + 8, :] for y in range(4) for at in starts], 0)
+        high, low = split2(part)
         two_high[:, i * 128:(i + 1) * 128] = high
         two_low[:, i * 128:(i + 1) * 128] = low
     order, turn = order_matrix(), turn_matrix()
@@ -145,19 +162,18 @@
         swapped += dot(dot(turn_k, two_high[...], NT).astype(BF16), order, NT)
         straight = []
         for y in range(4):
-            v = one_ref[y, k * 24:(k + 1) * 24, :]
-            straight.append(jnp.where(lane < 192, v[:, :256], 0.0))
-            straight.append(jnp.where(lane < 192, pltpu.roll(v[:, 128:], 192, 1), 0.0))
+            v = [got_ref[y, part * 120 + k * 24:part * 120 + (k + 1) * 24, :] for part in range(3)]
+            near = jnp.concatenate(v[:2], 1)
+            far = pltpu.roll(jnp.concatenate(v[1:], 1), 192, 1)
+            straight.append(jnp.where(lane < 192, near, 0.0))
+            straight.append(jnp.where(lane < 192, far, 0.0))
         high, low = split2(2.0 * jnp.concatenate(straight, 0) - swapped)
         mixed_high[k] = high
         mixed_low[k] = low
     for z in range(4):
         total = jnp.zeros((192, 256), F32)
         for k in range(5):
-            rows = [ref[k, z * 16:(z + 1) * 16, :] for ref in weights]
-            near = [v[:, :256] for v in rows]
-            far = [pltpu.roll(v[:, 128:], 192, 1) for v in rows]
-            high, low = split2(jnp.concatenate(near + far, 0))
+            high, low = high_ref[z, k], low_ref[z, k]
             total += dot(mixed_high[k], low, NT) + dot(mixed_low[k], high, NT) + dot(mixed_high[k], high, NT)
         for yz in range(8):
             for half in range(2):
@@ -197,15 +213,16 @@
         inc_ref[j] = new / (den[...] - occ_ref[place_ref[3] + j])
 
 
-def call(kernel, n_smem, n_vmem, outs, scratch):
-    shapes = [jax.ShapeDtypeStruct(s, F32) for s in outs]
+def call(kernel, n_smem, n_vmem, outs, scratch, mib=8, dtype=F32, cost=1):
+    shapes = [jax.ShapeDtypeStruct(s, dtype) for s in outs]
     return pl.pallas_call(
         kernel,
         out_shape=shapes if len(shapes) > 1 else shapes[0],
         in_specs=[SMEM] * n_smem + [VMEM] * n_vmem,
         out_specs=[VMEM] * len(shapes) if len(shapes) > 1 else VMEM,
         scratch_shapes=scratch,
-        compiler_params=pltpu.CompilerParams(vmem_limit_bytes=48 * 1024 * 1024),
+        cost_estimate=pl.CostEstimate(flops=cost * 10**9, bytes_accessed=1000, transcendentals=0),
+        compiler_params=pltpu.CompilerParams(vmem_limit_bytes=mib * 1024 * 1024),
     )
 
 
@@ -220,16 +237,18 @@
         lax.ppermute(weights, "x", [(s, (s - d) % 4) for s in range(4)]) for d in (1, 2, 3)
     ]
     across = [lax.ppermute(w, "core", [(0, 1), (1, 0)]) for w in along]
-    one, two = call(amps_kernel, 1, 3, [(4, 120, 384), (32, 48, 128)], [pltpu.VMEM((240, 256), F32)])(
+    one, two = call(amps_kernel, 1, 3, [(120, 384), (8, 48, 128)], [pltpu.VMEM((240, 256), F32)])(
         zh.reshape(1), amps, other, mark
     )
-    two = lax.all_to_all(two, ("x", "y", "core"), 0, 0, tiled=True)
-    one = lax.all_to_all(one, "y", 0, 0, tiled=True)
+    two = lax.all_to_all(two, ("x", "core"), 0, 0, tiled=True)
+    both = call(pack_kernel, 0, 2, [(4, 744, 128)], [])(one, two)
+    both = lax.all_to_all(both, "y", 0, 0, tiled=True)
     ordered = [w for pair in zip(along, across) for w in pair]
+    high, low = call(combine_kernel, 0, 8, [(4, 5, 256, 256)] * 2, [], 24, BF16, 5)(*ordered)
     partial = call(
-        product_kernel, 0, 10, [(1152, 128)],
-        [pltpu.VMEM((256, 768), BF16)] * 2 + [pltpu.VMEM((5, 192, 256), BF16)] * 2,
-    )(one, two, *ordered)
+        product_kernel, 0, 3, [(1152, 128)],
+        [pltpu.VMEM((256, 768), BF16)] * 2 + [pltpu.VMEM((5, 192, 256), BF16)] * 2, 24,
+    )(both, high, low)
     got = lax.all_to_all(partial.reshape(64, 1, 2304), ("y", "zh", "col"), 0, 0, tiled=True).reshape(1152, 128)
     r = ((x * 4 + y) * 2 + zh) * 2 + core
     place = jnp.stack([x, core, r * 3, col * 5, window_start[0]])

time: 128 us -> 130 us (1.016)
  blocking collectives: 0 us -> 22.1 us
  starting transfers between devices: 60.7 us -> 47.1 us
  waiting for transfers between devices: 48 us -> 37.4 us
  local copies, waits for them, and re-layouts: 3.65 us -> 7.71 us
    all_to_all x0 -> x1, blocking collectives: none -> 22.1 us  [body(): two = lax.all_to_all(two, ('x', 'core'), 0, 0, tiled=True)]
    ppermute x3, waiting for transfers between devices: 8.1 us -> 0.01 us  [body(): lax.ppermute(weights, 'x', [(s, (s - d) % 4) for s in range(4)])]
    all_to_all x1, starting transfers between devices: 14.8 us -> 7.66 us  [body(): lax.all_to_all(partial.reshape(64, 1, 2304), ('y', 'zh', 'col'), 0, 0, ti...]
    all_to_all x2 -> x1, starting transfers between devices: 12 us -> 4.91 us  [body(): both = lax.all_to_all(both, 'y', 0, 0, tiled=True)]
    unnamed x14 -> x18, local copies, waits for them, and re-layouts: 3.56 us -> 7.63 us
    all_to_all x1, waiting for transfers between devices: 34.1 us -> 31.5 us  [body(): lax.all_to_all(partial.reshape(64, 1, 2304), ('y', 'zh', 'col'), 0, 0, ti...]
    ppermute x4, waiting for transfers between devices: 0.01 us -> 1.44 us  [body(): across = [lax.ppermute(w, 'core', [(0, 1), (1, 0)]) for w in along]]
    all_to_all x2 -> x1, waiting for transfers between devices: 5.8 us -> 4.44 us  [body(): both = lax.all_to_all(both, 'y', 0, 0, tiled=True)]
  transfers between devices with their start and end apart: 11 -> 10, of which waited for: 3 -> 3; matrix products, arithmetic and copies ran while one was open for 0% -> 0% of each run, Pallas kernels for 2% -> 4%
where the time goes in v3:
time: 130 us; the launch traced here: 129 us
  starting transfers between devices  47.1 us (36%)
  waiting for transfers between devices  37.4 us (29%)
  blocking collectives  22.1 us (17%)
  Pallas kernels  13.2 us (10%)
  local copies, waits for them, and re-layouts  7.71 us (6%)
  between operations  1.48 us (1%)
    all_to_all x1, waiting for transfers between devices, body(): lax.all_to_all(partial.reshape(64, 1, 2304), ('y', 'zh', 'col'), 0, 0, ti...  31.5 us
    all_to_all x1, blocking collectives, body(): two = lax.all_to_all(two, ('x', 'core'), 0, 0, tiled=True)  22.1 us
    ppermute x1, starting transfers between devices, body(): other = lax.ppermute(amps, 'zh', [(0, 1), (1, 0)])  15.7 us
    ppermute x3, starting transfers between devices, body(): lax.ppermute(weights, 'x', [(s, (s - d) % 4) for s in range(4)])  10.2 us
    ppermute x4, starting transfers between devices, body(): across = [lax.ppermute(w, 'core', [(0, 1), (1, 0)]) for w in along]  8.64 us
    all_to_all x1, starting transfers between devices, body(): lax.all_to_all(partial.reshape(64, 1, 2304), ('y', 'zh', 'col'), 0, 0, ti...  7.66 us
    unnamed x18, local copies, waits for them, and re-layouts  7.63 us
    pallas_call x1, Pallas kernels, body(): call(product_kernel, 0, 3, [(1152, 128)], [pltpu.VMEM((256, 768), BF16)]...  5.44 us
  transfers between devices with their start and end apart: 10, of which 3 were waited for; matrix products, arithmetic and copies ran while one was open for 0% of the time, Pallas kernels for 4%

profile of v3, /device:TPU:8, one launch (start us, length us, event | category | flops | bytes accessed | tf_op | source)
XLA Modules:
  0.0 129.0 jit_solution(8479622597961090943)
XLA Ops:
  0.6 15.7 %collective-permute-start = (f32[5,3,1152]{2,1,0:T(4,128)}, f32[5,3,1152]{2,1,0:T(4,128)S(1)}, u32[]{:S(2)}, u32[]{:S(2)}) collective-permute-start(f32[5,3,1152]{2,1,0:T(4,128)} %bitcast.15), channel_id=1, source_target_pairs={{0,16},{16,0},{1,17},{17,1},{2,18},{18,2},{3,19},{19,3},{4,20},{20... | collective-permute-start | bytes 207368 | tf_op jit(solution)/shard_map/ppermute | solution.py:234
  16.4 1.1 copy-done.4
  17.4 2.8 %shard_map.77 = (f32[5,64,384]{2,1,0:T(8,128)S(1)}, f32[8,128]{1,0:T(8,128)S(1)}) custom-call(f32[5,3,7680]{2,1,0:T(4,128)S(1)} %bitcast.14), custom_call_target="tpu_custom_call" | custom-call | flops 1000000000 | bytes 1000 | tf_op jit(solution)/shard_map/pallas_call | solution.py:235
  20.2 4.7 %collective-permute-start.2 = (f32[5,64,384]{2,1,0:T(8,128)S(1)}, f32[5,64,384]{2,1,0:T(8,128)S(1)}, u32[]{:S(2)}, u32[]{:S(2)}) collective-permute-start(f32[5,64,384]{2,1,0:T(8,128)S(1)} %get-tuple-element.13.refs_0_), channel_id=1, source_target_pairs={{0,384},{128,0},{256,128},{384,256},{1,385},{129,1},{257,129},{385... | collective-permute-start | bytes 1474568 | tf_op jit(solution)/shard_map/ppermute | solution.py:237
  24.9 2.7 %collective-permute-start.4 = (f32[5,64,384]{2,1,0:T(8,128)S(1)}, f32[5,64,384]{2,1,0:T(8,128)S(1)}, u32[]{:S(2)}, u32[]{:S(2)}) collective-permute-start(f32[5,64,384]{2,1,0:T(8,128)S(1)} %get-tuple-element.13.refs_0_), channel_id=1, source_target_pairs={{0,256},{128,384},{256,0},{384,128},{1,257},{129,385},{257,1},{385... | collective-permute-start | bytes 1474568 | tf_op jit(solution)/shard_map/ppermute | solution.py:237
  27.6 2.8 %collective-permute-start.6 = (f32[5,64,384]{2,1,0:T(8,128)S(1)}, f32[5,64,384]{2,1,0:T(8,128)S(1)}, u32[]{:S(2)}, u32[]{:S(2)}) collective-permute-start(f32[5,64,384]{2,1,0:T(8,128)S(1)} %get-tuple-element.13.refs_0_), channel_id=1, source_target_pairs={{0,128},{128,256},{256,384},{384,0},{1,129},{129,257},{257,385},{3... | collective-permute-start | bytes 1474568 | tf_op jit(solution)/shard_map/ppermute | solution.py:237
  30.4 0.8 shard_map.78
  31.2 22.1 %all_to_all.15.two_ref = f32[8,48,128]{2,1,0:T(8,128)S(1)} all-to-all(f32[8,48,128]{2,1,0:T(8,128)S(1)} %get-tuple-element.12), channel_id=1, replica_groups=mesh['x'=4,'y'=4,'zh'=2,'core'=2,'col'=8] {'x','core'}, dimensions={0} | all-to-all | bytes 393216 | tf_op jit(solution)/shard_map/all_to_all | solution.py:243
  53.4 1.2 shard_map.79
  54.6 4.9 %all-to-all-start.1 = ((f32[4,744,128]{2,1,0:T(8,128)}), f32[4,744,128]{2,1,0:T(8,128)S(1)}, u32[]{:S(2)}, u32[]{:S(2)}) async-start(f32[4,744,128]{2,1,0:T(8,128)} %shard_map.79), calls=%async_computation.1 | async-start | bytes 3047424 | tf_op jit(solution)/shard_map/all_to_all | solution.py:245
  59.5 1.9 %collective-permute-start.1 = (f32[5,64,384]{2,1,0:T(8,128)S(1)}, f32[5,64,384]{2,1,0:T(8,128)S(1)}, u32[]{:S(2)}, u32[]{:S(2)}) collective-permute-start(f32[5,64,384]{2,1,0:T(8,128)S(1)} %get-tuple-element.13.refs_0_), channel_id=1, source_target_pairs={{0,8},{8,0},{1,9},{9,1},{2,10},{10,2},{3,11},{11,3},{4,12},{12,4},... | collective-permute-start | bytes 1474568 | tf_op jit(solution)/shard_map/ppermute | solution.py:239
  61.4 2.4 %collective-permute-start.3 = (f32[5,64,384]{2,1,0:T(8,128)S(1)}, f32[5,64,384]{2,1,0:T(8,128)S(1)}, u32[]{:S(2)}, u32[]{:S(2)}) collective-permute-start(f32[5,64,384]{2,1,0:T(8,128)S(1)} %collective-permute-done.2.refs_2_), channel_id=1, source_target_pairs={{0,8},{8,0},{1,9},{9,1},{2,10},{10,2},{3,11},{11,3},{4,12},{12,4},... | collective-permute-start | bytes 1474568 | tf_op jit(solution)/shard_map/ppermute | solution.py:239
  63.9 1.9 %collective-permute-start.5 = (f32[5,64,384]{2,1,0:T(8,128)S(1)}, f32[5,64,384]{2,1,0:T(8,128)S(1)}, u32[]{:S(2)}, u32[]{:S(2)}) collective-permute-start(f32[5,64,384]{2,1,0:T(8,128)S(1)} %collective-permute-done.4.refs_4_), channel_id=1, source_target_pairs={{0,8},{8,0},{1,9},{9,1},{2,10},{10,2},{3,11},{11,3},{4,12},{12,4},... | collective-permute-start | bytes 1474568 | tf_op jit(solution)/shard_map/ppermute | solution.py:239
  65.8 2.4 %collective-permute-start.7 = (f32[5,64,384]{2,1,0:T(8,128)S(1)}, f32[5,64,384]{2,1,0:T(8,128)S(1)}, u32[]{:S(2)}, u32[]{:S(2)}) collective-permute-start(f32[5,64,384]{2,1,0:T(8,128)S(1)} %collective-permute-done.6.refs_6_), channel_id=1, source_target_pairs={{0,8},{8,0},{1,9},{9,1},{2,10},{10,2},{3,11},{11,3},{4,12},{12,4},... | collective-permute-start | bytes 1474568 | tf_op jit(solution)/shard_map/ppermute | solution.py:239
  68.2 1.4 %collective-permute-done.7.refs_7_ = f32[5,64,384]{2,1,0:T(8,128)S(1)} collective-permute-done((f32[5,64,384]{2,1,0:T(8,128)S(1)}, f32[5,64,384]{2,1,0:T(8,128)S(1)}, u32[]{:S(2)}, u32[]{:S(2)}) %collective-permute-start.7) | collective-permute-done | bytes 491552 | tf_op jit(solution)/shard_map/ppermute | solution.py:239
  70.5 1.5 %copy-done = bf16[4,5,256,256]{3,2,1,0:T(8,128)(2,1)} copy-done((bf16[4,5,256,256]{3,2,1,0:T(8,128)(2,1)}, bf16[4,5,256,256]{3,2,1,0:T(8,128)(2,1)S(1)}, u32[]{:S(2)}) %copy-start) | copy-done | bytes 2621464
  72.0 1.6 %copy-done.2 = bf16[4,5,256,256]{3,2,1,0:T(8,128)(2,1)} copy-done((bf16[4,5,256,256]{3,2,1,0:T(8,128)(2,1)}, bf16[4,5,256,256]{3,2,1,0:T(8,128)(2,1)S(1)}, u32[]{:S(2)}) %copy-start.2) | copy-done | bytes 2621464
  73.5 4.4 %all-to-all-done.1.got_ref = f32[4,744,128]{2,1,0:T(8,128)S(1)} async-done(((f32[4,744,128]{2,1,0:T(8,128)}), f32[4,744,128]{2,1,0:T(8,128)S(1)}, u32[]{:S(2)}, u32[]{:S(2)}) %all-to-all-start.1) | async-done | bytes 1523744 | tf_op jit(solution)/shard_map/all_to_all | solution.py:245
  78.0 1.7 %copy-done.1 = bf16[4,5,256,256]{3,2,1,0:T(8,128)(2,1)S(1)} copy-done((bf16[4,5,256,256]{3,2,1,0:T(8,128)(2,1)S(1)}, bf16[4,5,256,256]{3,2,1,0:T(8,128)(2,1)}, u32[]{:S(2)}) %copy-start.1) | copy-done | bytes 2621464
  79.7 1.7 %copy-done.3 = bf16[4,5,256,256]{3,2,1,0:T(8,128)(2,1)S(1)} copy-done((bf16[4,5,256,256]{3,2,1,0:T(8,128)(2,1)S(1)}, bf16[4,5,256,256]{3,2,1,0:T(8,128)(2,1)}, u32[]{:S(2)}) %copy-start.3) | copy-done | bytes 2621464
  81.5 5.4 %shard_map.81 = f32[1152,128]{1,0:T(8,128)} custom-call(f32[4,744,128]{2,1,0:T(8,128)S(1)} %all-to-all-done.1.got_ref, bf16[4,5,256,256]{3,2,1,0:T(8,128)(2,1)S(1)} %copy-done.1, bf16[4,5,256,256]{3,2,1,0:T(8,128)(2,1)S(1)} %copy-done.3), custom_call_target="tpu_custom_call" | custom-call | flops 1000000000 | bytes 1000 | tf_op jit(solution)/shard_map/pallas_call | solution.py:248
  86.9 7.7 %all-to-all-start.2 = ((f32[64,1,2304]{2,1,0:T(1,128)}), f32[64,1,2304]{2,1,0:T(1,128)S(1)}, u32[]{:S(2)}, u32[]{:S(2)}) async-start(f32[64,1,2304]{2,1,0:T(1,128)} %bitcast.7), calls=%async_computation.2 | async-start | bytes 1179648 | tf_op jit(solution)/shard_map/all_to_all | solution.py:252
  95.3 31.5 %all-to-all-done.2 = f32[64,1,2304]{2,1,0:T(1,128)S(1)} async-done(((f32[64,1,2304]{2,1,0:T(1,128)}), f32[64,1,2304]{2,1,0:T(1,128)S(1)}, u32[]{:S(2)}, u32[]{:S(2)}) %all-to-all-start.2) | async-done | bytes 589856 | tf_op jit(solution)/shard_map/all_to_all | solution.py:252
  126.8 2.2 %shard_map.82 = (f32[5,3,1152]{2,1,0:T(4,128)}, f32[5,3,1152]{2,1,0:T(4,128)}) custom-call(s32[5]{0:T(128)S(1)} %stack.19.place_ref, f32[40]{0:T(128)S(1)} %copy-done.8, f32[192]{0:T(256)S(1)} %copy-done.7, f32[1152,128]{1,0:T(8,128)S(1)} %bitcast.13, f32[1,192]{1,0:T(1,128)S(1)} %bitcast.18, f32[5,3,1152]{2,1,0:T(4,128)S(1)} %bitcast.17), custom_call_target="tpu_custom_call" | custom-call | flops 1000000000 | bytes 1000 | tf_op jit(solution)/shard_map/pallas_call | solution.py:255
  (22 shorter events, 0.9 us)
Async XLA Ops:
  0.6 29.8 %collective-permute-start = (f32[5,3,1152]{2,1,0:T(4,128)}, f32[5,3,1152]{2,1,0:T(4,128)S(1)}, u32[]{:S(2)}, u32[]{:S(2)}) collective-permute-start(f32[5,3,1152]{2,1,0:T(4,128)} %bitcast.15), channel_id=1, source_target_pairs={{0,16},{16,0},{1,17},{17,1},{2,18},{18,2},{3,19},{19,3},{4,20},{20... | collective-permute-start | bytes 207368 | tf_op jit(solution)/shard_map/ppermute | solution.py:234
  16.4 1.1 copy-start.4
  17.4 13.0 %copy-start.5 = (f32[3,5,1152]{2,0,1:T(4,128)S(1)}, f32[3,5,1152]{2,0,1:T(4,128)}, u32[]{:S(2)}) copy-start(f32[3,5,1152]{2,0,1:T(4,128)} %param.6) | copy-start | bytes 207364
  20.2 41.2 %collective-permute-start.2 = (f32[5,64,384]{2,1,0:T(8,128)S(1)}, f32[5,64,384]{2,1,0:T(8,128)S(1)}, u32[]{:S(2)}, u32[]{:S(2)}) collective-permute-start(f32[5,64,384]{2,1,0:T(8,128)S(1)} %get-tuple-element.13.refs_0_), channel_id=1, source_target_pairs={{0,384},{128,0},{256,128},{384,256},{1,385},{129,1},{257,129},{385... | collective-permute-start | bytes 1474568 | tf_op jit(solution)/shard_map/ppermute | solution.py:237
  24.9 39.0 %collective-permute-start.4 = (f32[5,64,384]{2,1,0:T(8,128)S(1)}, f32[5,64,384]{2,1,0:T(8,128)S(1)}, u32[]{:S(2)}, u32[]{:S(2)}) collective-permute-start(f32[5,64,384]{2,1,0:T(8,128)S(1)} %get-tuple-element.13.refs_0_), channel_id=1, source_target_pairs={{0,256},{128,384},{256,0},{384,128},{1,257},{129,385},{257,1},{385... | collective-permute-start | bytes 1474568 | tf_op jit(solution)/shard_map/ppermute | solution.py:237
  27.6 38.2 %collective-permute-start.6 = (f32[5,64,384]{2,1,0:T(8,128)S(1)}, f32[5,64,384]{2,1,0:T(8,128)S(1)}, u32[]{:S(2)}, u32[]{:S(2)}) collective-permute-start(f32[5,64,384]{2,1,0:T(8,128)S(1)} %get-tuple-element.13.refs_0_), channel_id=1, source_target_pairs={{0,128},{128,256},{256,384},{384,0},{1,129},{129,257},{257,385},{3... | collective-permute-start | bytes 1474568 | tf_op jit(solution)/shard_map/ppermute | solution.py:237
  54.6 23.4 %all-to-all-start.1 = ((f32[4,744,128]{2,1,0:T(8,128)}), f32[4,744,128]{2,1,0:T(8,128)S(1)}, u32[]{:S(2)}, u32[]{:S(2)}) async-start(f32[4,744,128]{2,1,0:T(8,128)} %shard_map.79), calls=%async_computation.1 | async-start | bytes 3047424 | tf_op jit(solution)/shard_map/all_to_all | solution.py:245
  59.5 8.7 %collective-permute-start.1 = (f32[5,64,384]{2,1,0:T(8,128)S(1)}, f32[5,64,384]{2,1,0:T(8,128)S(1)}, u32[]{:S(2)}, u32[]{:S(2)}) collective-permute-start(f32[5,64,384]{2,1,0:T(8,128)S(1)} %get-tuple-element.13.refs_0_), channel_id=1, source_target_pairs={{0,8},{8,0},{1,9},{9,1},{2,10},{10,2},{3,11},{11,3},{4,12},{12,4},... | collective-permute-start | bytes 1474568 | tf_op jit(solution)/shard_map/ppermute | solution.py:239
  61.4 6.8 %collective-permute-start.3 = (f32[5,64,384]{2,1,0:T(8,128)S(1)}, f32[5,64,384]{2,1,0:T(8,128)S(1)}, u32[]{:S(2)}, u32[]{:S(2)}) collective-permute-start(f32[5,64,384]{2,1,0:T(8,128)S(1)} %collective-permute-done.2.refs_2_), channel_id=1, source_target_pairs={{0,8},{8,0},{1,9},{9,1},{2,10},{10,2},{3,11},{11,3},{4,12},{12,4},... | collective-permute-start | bytes 1474568 | tf_op jit(solution)/shard_map/ppermute | solution.py:239
  63.9 4.4 %collective-permute-start.5 = (f32[5,64,384]{2,1,0:T(8,128)S(1)}, f32[5,64,384]{2,1,0:T(8,128)S(1)}, u32[]{:S(2)}, u32[]{:S(2)}) collective-permute-start(f32[5,64,384]{2,1,0:T(8,128)S(1)} %collective-permute-done.4.refs_4_), channel_id=1, source_target_pairs={{0,8},{8,0},{1,9},{9,1},{2,10},{10,2},{3,11},{11,3},{4,12},{12,4},... | collective-permute-start | bytes 1474568 | tf_op jit(solution)/shard_map/ppermute | solution.py:239
  65.8 3.9 %collective-permute-start.7 = (f32[5,64,384]{2,1,0:T(8,128)S(1)}, f32[5,64,384]{2,1,0:T(8,128)S(1)}, u32[]{:S(2)}, u32[]{:S(2)}) collective-permute-start(f32[5,64,384]{2,1,0:T(8,128)S(1)} %collective-permute-done.6.refs_6_), channel_id=1, source_target_pairs={{0,8},{8,0},{1,9},{9,1},{2,10},{10,2},{3,11},{11,3},{4,12},{12,4},... | collective-permute-start | bytes 1474568 | tf_op jit(solution)/shard_map/ppermute | solution.py:239
  70.5 1.5 %copy-start = (bf16[4,5,256,256]{3,2,1,0:T(8,128)(2,1)}, bf16[4,5,256,256]{3,2,1,0:T(8,128)(2,1)S(1)}, u32[]{:S(2)}) copy-start(bf16[4,5,256,256]{3,2,1,0:T(8,128)(2,1)S(1)} %get-tuple-element.14.high_ref) | copy-start | bytes 7864324
  72.0 1.6 %copy-start.2 = (bf16[4,5,256,256]{3,2,1,0:T(8,128)(2,1)}, bf16[4,5,256,256]{3,2,1,0:T(8,128)(2,1)S(1)}, u32[]{:S(2)}) copy-start(bf16[4,5,256,256]{3,2,1,0:T(8,128)(2,1)S(1)} %get-tuple-element.15.low_ref) | copy-start | bytes 7864324
  78.0 1.7 %copy-start.1 = (bf16[4,5,256,256]{3,2,1,0:T(8,128)(2,1)S(1)}, bf16[4,5,256,256]{3,2,1,0:T(8,128)(2,1)}, u32[]{:S(2)}) copy-start(bf16[4,5,256,256]{3,2,1,0:T(8,128)(2,1)} %copy-done) | copy-start | bytes 7864324
  79.7 1.7 %copy-start.3 = (bf16[4,5,256,256]{3,2,1,0:T(8,128)(2,1)S(1)}, bf16[4,5,256,256]{3,2,1,0:T(8,128)(2,1)}, u32[]{:S(2)}) copy-start(bf16[4,5,256,256]{3,2,1,0:T(8,128)(2,1)} %copy-done.2) | copy-start | bytes 7864324
  81.4 45.4 %copy-start.6 = (f32[3,5,1152]{2,0,1:T(4,128)S(1)}, f32[3,5,1152]{2,0,1:T(4,128)}, u32[]{:S(2)}) copy-start(f32[3,5,1152]{2,0,1:T(4,128)} %param.8) | copy-start | bytes 207364
  81.4 45.4 %copy-start.7 = (f32[192]{0:T(256)S(1)}, f32[192]{0:T(256)}, u32[]{:S(2)}) copy-start(f32[192]{0:T(256)} %va_ref.1) | copy-start | bytes 2308
  81.4 45.4 %copy-start.8 = (f32[40]{0:T(128)S(1)}, f32[40]{0:T(128)}, u32[]{:S(2)}) copy-start(f32[40]{0:T(128)} %occ_ref.1) | copy-start | bytes 484
  86.9 39.9 %all-to-all-start.2 = ((f32[64,1,2304]{2,1,0:T(1,128)}), f32[64,1,2304]{2,1,0:T(1,128)S(1)}, u32[]{:S(2)}, u32[]{:S(2)}) async-start(f32[64,1,2304]{2,1,0:T(1,128)} %bitcast.7), calls=%async_computation.2 | async-start | bytes 1179648 | tf_op jit(solution)/shard_map/all_to_all | solution.py:252

commit v4 on v2

--- a/solution.py
+++ b/solution.py
@@ -26,13 +26,11 @@
     return jnp.where(mask, 1.0, 0.0).astype(BF16)
 
 
-def order_matrix():
-    n = index((1, 256), 1)
-    q = n & 7
-    zh = third(q, 2)
-    v = (n >> 6) * 48 + ((n >> 4) & 3) * 12 + zh * 6 + ((n >> 3) & 1) * 3 + q - zh * 3
-    v = jnp.where(q < 6, v, -1)
-    return hot(index((256, 256), 0) == v)
+def order_matrix(e):
+    n = index((1, 512), 1)
+    v = ((n >> 5) & 3) * 48 + (n >> 7) * 12 + ((n >> 4) & 1) * 6 + ((n >> 3) & 1) * 3 + (n & 3)
+    v = jnp.where(((n & 3) < 3) & (((n >> 2) & 1) == e), v, -1)
+    return hot(index((256, 512), 0) == v)
 
 
 def choose_matrix():
@@ -46,14 +44,14 @@
 
 
 def turn_matrix():
-    n = index((1, 768), 1)
-    i, q = n >> 7, n & 127
+    n = index((1, 384), 1)
+    p, q = n >> 7, n & 127
     k = sum((q >= 24 * s).astype(jnp.int32) for s in range(1, 6))
     q = q - k * 24
     yz = third(q, 8)
-    row = k * 192 + (yz >> 1) * 48 + (i & 1) * 24 + (yz & 1) * 9 + (i >> 1) * 3 + q - yz * 3
+    row = k * 96 + (yz >> 1) * 24 + (yz & 1) * 9 + p * 3 + q - yz * 3
     row = jnp.where(k < 5, row, -1)
-    return hot(index((960, 768), 0) == row)
+    return hot(index((480, 384), 0) == row)
 
 
 def spread_matrix():
@@ -90,9 +88,8 @@
     return pltpu.roll(ref[lead, :, n * 192 - 64:n * 192 + 192], 192, 1)
 
 
-def weights_kernel(ints_ref, out_ref, mark_ref):
+def weights_kernel(ints_ref, out_ref):
     out_ref[...] = jnp.zeros_like(out_ref)
-    mark_ref[...] = jnp.zeros_like(mark_ref)
     lane = index((3, 128), 1)
     for k in range(5):
         for j in range(20):
@@ -104,57 +101,80 @@
             out_ref[k, at:at + 3, 256:] = far[:, 128:]
 
 
-def amps_kernel(zh_ref, own_ref, other_ref, mark_ref, one_ref, two_ref, rows):
+def swap_kernel(own_ref, two_ref, rows):
+    rows[...] = jnp.zeros_like(rows)
+    for k in range(5):
+        for p in range(3):
+            v = own_ref[k, :, p * 384:(p + 1) * 384]
+            at = k * 24 + p * 8
+            rows[at:at + 3, :] = v[:, :256]
+            rows[at + 4:at + 7, :] = pltpu.roll(v[:, 128:], 192, 1)
+    chosen = moved(rows[...], choose_matrix())
+    lane = index((24, 128), 1)
+    for n in range(8):
+        part = jnp.zeros((24, 128), F32)
+        for k in range(5):
+            v = pltpu.roll(chosen[k * 24:(k + 1) * 24, :], (k * 24 - n * 24) % 256, 1)[:, :128]
+            part = jnp.where((lane >= k * 24) & (lane < k * 24 + 24), v, part)
+        for zh in range(2):
+            two_ref[n // 2 * 4 + zh * 2 + n % 2] = part
+
+
+def pack_kernel(zh_ref, own_ref, other_ref, two_ref, out_ref, rows):
     first = zh_ref[0] == 0
     rows[...] = jnp.zeros_like(rows)
-    one_ref[...] = jnp.zeros_like(one_ref)
     for k in range(5):
         for p in range(3):
             own = own_ref[k, :, p * 384:(p + 1) * 384]
             other = other_ref[k, :, p * 384:(p + 1) * 384]
-            for zh, v in ((0, jnp.where(first, own, other)), (1, jnp.where(first, other, own))):
-                at = k * 24 + zh * 9 + p * 3
-                for y in range(4):
-                    one_ref[y, at:at + 3, :] = v
-                at = k * 48 + p * 16 + zh * 3
-                rows[at:at + 3, :] = v[:, :256]
-                rows[at + 8:at + 11, :] = pltpu.roll(v[:, 128:], 192, 1)
-    chosen = moved(rows[...], choose_matrix())
-    lane = index((48, 128), 1)
-    for n in range(8):
-        part = jnp.zeros((48, 128), F32)
-        for k in range(5):
-            v = pltpu.roll(chosen[k * 48:(k + 1) * 48, :], (k * 24 - n * 24) % 256, 1)[:, :128]
-            part = jnp.where((lane >= k * 24) & (lane < k * 24 + 24), v, part)
+            at = k * 18 + p * 3
+            rows[at:at + 3, :] = jnp.where(first, own, other)
+            rows[at + 9:at + 12, :] = jnp.where(first, other, own)
+    for y in range(4):
+        for part in range(3):
+            out_ref[y, part * 96:(part + 1) * 96, :] = rows[:, part * 128:(part + 1) * 128]
+        out_ref[y, 288:, :] = two_ref[...].reshape(384, 128)
+
+
+def mark_kernel(*refs):
+    refs[-1][...] = jnp.zeros_like(refs[-1])
+
+
+def product_kernel(got_ref, *refs):
+    away, out_ref = refs[:8], refs[9]
+    two_high, two_low, mixed_high, mixed_low, weights, arrived = refs[10:]
+    copies = [pltpu.make_async_copy(away[n], weights.at[n], arrived.at[n]) for n in range(8)]
+    for copy in copies:
+        copy.start()
+    for p in range(3):
+        starts = [288 + s * 24 + p * 8 for s in range(16)]
+        part = jnp.concatenate([got_ref[y, at:at + 8, :] for y in range(4) for at in starts], 0)
+        high, low = split2(part)
+        two_high[:, p * 128:(p + 1) * 128] = high
+        two_low[:, p * 128:(p + 1) * 128] = low
+    orders, turn = [order_matrix(0), order_matrix(1)], turn_matrix()
+    lane = index((24, 256), 1)
+    for k in range(5):
+        turn_k = turn[k * 96:(k + 1) * 96, :]
+        high = dot(turn_k, two_high[...], NT).astype(BF16)
+        low = dot(turn_k, two_low[...], NT).astype(BF16)
+        swapped = [dot(low, o, NT) + dot(high, o, NT) for o in orders]
+        mixed = []
         for y in range(4):
-            two_ref[(n // 2 * 4 + y) * 2 + n % 2] = part
-
-
-def product_kernel(one_ref, two_ref, *refs):
-    weights, out_ref = refs[:8], refs[8]
-    two_high, two_low, mixed_high, mixed_low = refs[9:]
-    for i in range(6):
-        high, low = split2(two_ref[:, i * 8:(i + 1) * 8, :].reshape(256, 128))
-        two_high[:, i * 128:(i + 1) * 128] = high
-        two_low[:, i * 128:(i + 1) * 128] = low
-    order, turn = order_matrix(), turn_matrix()
-    lane = index((24, 256), 1)
-    for k in range(5):
-        turn_k = turn[k * 192:(k + 1) * 192, :]
-        swapped = dot(dot(turn_k, two_low[...], NT).astype(BF16), order, NT)
-        swapped += dot(dot(turn_k, two_high[...], NT).astype(BF16), order, NT)
-        straight = []
-        for y in range(4):
-            v = one_ref[y, k * 24:(k + 1) * 24, :]
-            straight.append(jnp.where(lane < 192, v[:, :256], 0.0))
-            straight.append(jnp.where(lane < 192, pltpu.roll(v[:, 128:], 192, 1), 0.0))
-        high, low = split2(2.0 * jnp.concatenate(straight, 0) - swapped)
+            v = [got_ref[y, part * 96 + k * 18:part * 96 + k * 18 + 24, :] for part in range(3)]
+            near = jnp.concatenate(v[:2], 1)
+            far = pltpu.roll(jnp.concatenate(v[1:], 1), 192, 1)
+            for e, straight in enumerate((near, far)):
+                mixed.append(2.0 * jnp.where(lane < 192, straight, 0.0) - swapped[e][y * 24:(y + 1) * 24, :])
+        high, low = split2(jnp.concatenate(mixed, 0))
         mixed_high[k] = high
         mixed_low[k] = low
+    for copy in copies:
+        copy.wait()
     for z in range(4):
         total = jnp.zeros((192, 256), F32)
         for k in range(5):
-            rows = [ref[k, z * 16:(z + 1) * 16, :] for ref in weights]
+            rows = [weights[n, k, z * 16:(z + 1) * 16, :] for n in range(8)]
             near = [v[:, :256] for v in rows]
             far = [pltpu.roll(v[:, 128:], 192, 1) for v in rows]
             high, low = split2(jnp.concatenate(near + far, 0))
@@ -197,15 +217,16 @@
         inc_ref[j] = new / (den[...] - occ_ref[place_ref[3] + j])
 
 
-def call(kernel, n_smem, n_vmem, outs, scratch):
-    shapes = [jax.ShapeDtypeStruct(s, F32) for s in outs]
+def call(kernel, n_smem, n_vmem, outs, scratch, mib=8, dtype=F32, cost=1, space=pltpu.VMEM):
+    shapes = [jax.ShapeDtypeStruct(s, dtype) for s in outs]
     return pl.pallas_call(
         kernel,
         out_shape=shapes if len(shapes) > 1 else shapes[0],
-        in_specs=[SMEM] * n_smem + [VMEM] * n_vmem,
+        in_specs=[SMEM] * n_smem + [pl.BlockSpec(memory_space=space)] * n_vmem,
         out_specs=[VMEM] * len(shapes) if len(shapes) > 1 else VMEM,
         scratch_shapes=scratch,
-        compiler_params=pltpu.CompilerParams(vmem_limit_bytes=48 * 1024 * 1024),
+        cost_estimate=pl.CostEstimate(flops=cost * 10**9, bytes_accessed=1000, transcendentals=0),
+        compiler_params=pltpu.CompilerParams(vmem_limit_bytes=mib * 1024 * 1024),
     )
 
 
@@ -215,21 +236,27 @@
     ints = jnp.transpose(integrals, (1, 0, 2))
     res = jnp.transpose(residual, (1, 0, 2))
     other = lax.ppermute(amps, "zh", [(0, 1), (1, 0)])
-    weights, mark = call(weights_kernel, 0, 1, [(5, 64, 384), (8, 128)], [])(ints)
+    weights = call(weights_kernel, 0, 1, [(5, 64, 384)], [])(ints)
     along = [weights] + [
         lax.ppermute(weights, "x", [(s, (s - d) % 4) for s in range(4)]) for d in (1, 2, 3)
     ]
     across = [lax.ppermute(w, "core", [(0, 1), (1, 0)]) for w in along]
-    one, two = call(amps_kernel, 1, 3, [(4, 120, 384), (32, 48, 128)], [pltpu.VMEM((240, 256), F32)])(
-        zh.reshape(1), amps, other, mark
-    )
-    two = lax.all_to_all(two, ("x", "y", "core"), 0, 0, tiled=True)
-    one = lax.all_to_all(one, "y", 0, 0, tiled=True)
+    two = call(swap_kernel, 0, 1, [(16, 24, 128)], [pltpu.VMEM((120, 256), F32)])(amps)
+    two = lax.all_to_all(two, ("x", "zh", "core"), 0, 0, tiled=True)
+    both = call(pack_kernel, 1, 3, [(4, 672, 128)], [pltpu.VMEM((96, 384), F32)])(zh.reshape(1), amps, other, two)
+    both = lax.all_to_all(both, "y", 0, 0, tiled=True)
     ordered = [w for pair in zip(along, across) for w in pair]
-    partial = call(
-        product_kernel, 0, 10, [(1152, 128)],
-        [pltpu.VMEM((256, 768), BF16)] * 2 + [pltpu.VMEM((5, 192, 256), BF16)] * 2,
-    )(one, two, *ordered)
+    mark = call(mark_kernel, 0, 8, [(8, 128)], [], 8, F32, 1, pl.ANY)(*ordered)
+    partial = pl.pallas_call(
+        product_kernel,
+        out_shape=jax.ShapeDtypeStruct((1152, 128), F32),
+        in_specs=[VMEM] + [pl.BlockSpec(memory_space=pl.ANY)] * 9,
+        out_specs=VMEM,
+        scratch_shapes=[pltpu.VMEM((512, 384), BF16)] * 2 + [pltpu.VMEM((5, 192, 256), BF16)] * 2
+        + [pltpu.VMEM((8, 5, 64, 384), F32), pltpu.SemaphoreType.DMA((8,))],
+        cost_estimate=pl.CostEstimate(flops=10**9, bytes_accessed=1000, transcendentals=0),
+        compiler_params=pltpu.CompilerParams(vmem_limit_bytes=52 * 1024 * 1024),
+    )(both, *ordered, mark)
     got = lax.all_to_all(partial.reshape(64, 1, 2304), ("y", "zh", "col"), 0, 0, tiled=True).reshape(1152, 128)
     r = ((x * 4 + y) * 2 + zh) * 2 + core
     place = jnp.stack([x, core, r * 3, col * 5, window_start[0]])

time: 128 us -> 127 us (level)
  waiting for transfers between devices: 48 us -> 44.5 us
  Pallas kernels: 13.5 us -> 16.6 us
  local copies, waits for them, and re-layouts: 3.65 us -> 1.78 us
  starting transfers between devices: 60.7 us -> 62 us
    all_to_all x2, starting transfers between devices: 12 us -> 22.6 us  [the longest x1 17.7 us: body(): two = lax.all_to_all(two, ('x', 'zh', 'core'), 0, 0, tiled=True)]
    all_to_all x1, starting transfers between devices: 14.8 us -> 8.67 us  [body(): lax.all_to_all(partial.reshape(64, 1, 2304), ('y', 'zh', 'col'), 0, 0, ti...]
    all_to_all x2, waiting for transfers between devices: 5.8 us -> 0.01 us  [the longest x1 0.01 us: body(): two = lax.all_to_all(two, ('x', 'zh', 'core'), 0, 0, tiled=True)]
    ppermute x1, starting transfers between devices: 15.7 us -> 12.5 us  [body(): other = lax.ppermute(amps, 'zh', [(0, 1), (1, 0)])]
    pallas_call x3 -> x5, Pallas kernels: 11.4 us -> 14.4 us  [the longest x1 9.21 us: body(): pl.pallas_call(product_kernel, out_shape=jax.ShapeDtypeStruct((1152, 128)...]
    unnamed x14 -> x20, local copies, waits for them, and re-layouts: 3.56 us -> 1.7 us
    ppermute x4, waiting for transfers between devices: 0.01 us -> 1.79 us  [body(): across = [lax.ppermute(w, 'core', [(0, 1), (1, 0)]) for w in along]]
  transfers between devices with their start and end apart: 11 -> 11, of which waited for: 3 -> 4; matrix products, arithmetic and copies ran while one was open for 0% -> 0% of each run, Pallas kernels for 2% -> 3%
where the time goes in v4:
time: 127 us; the launch traced here: 126 us
  starting transfers between devices  62 us (49%)
  waiting for transfers between devices  44.5 us (35%)
  Pallas kernels  16.6 us (13%)
  local copies, waits for them, and re-layouts  1.78 us (1%)
  between operations  1.51 us (1%)
    all_to_all x1, waiting for transfers between devices, body(): lax.all_to_all(partial.reshape(64, 1, 2304), ('y', 'zh', 'col'), 0, 0, ti...  34.1 us
    all_to_all x1, starting transfers between devices, body(): two = lax.all_to_all(two, ('x', 'zh', 'core'), 0, 0, tiled=True)  17.7 us
    ppermute x1, starting transfers between devices, body(): other = lax.ppermute(amps, 'zh', [(0, 1), (1, 0)])  12.5 us
    ppermute x3, starting transfers between devices, body(): lax.ppermute(weights, 'x', [(s, (s - d) % 4) for s in range(4)])  10.1 us
    pallas_call x1, Pallas kernels, body(): pl.pallas_call(product_kernel, out_shape=jax.ShapeDtypeStruct((1152, 128)...  9.21 us
    all_to_all x1, starting transfers between devices, body(): lax.all_to_all(partial.reshape(64, 1, 2304), ('y', 'zh', 'col'), 0, 0, ti...  8.67 us
    ppermute x3, waiting for transfers between devices, body(): lax.ppermute(weights, 'x', [(s, (s - d) % 4) for s in range(4)])  8.65 us
    ppermute x4, starting transfers between devices, body(): across = [lax.ppermute(w, 'core', [(0, 1), (1, 0)]) for w in along]  8.14 us
  transfers between devices with their start and end apart: 11, of which 4 were waited for; matrix products, arithmetic and copies ran while one was open for 0% of the time, Pallas kernels for 3%

profile of v4, /device:TPU:8, one launch (start us, length us, event | category | flops | bytes accessed | tf_op | source)
XLA Modules:
  0.0 126.5 jit_solution(17670390679256953792)
XLA Ops:
  0.6 0.9 copy-done.5
  1.5 1.2 shard_map.77
  2.7 17.7 %all-to-all-start = ((f32[16,24,128]{2,1,0:T(8,128)}), f32[16,24,128]{2,1,0:T(8,128)S(1)}, u32[]{:S(2)}, u32[]{:S(2)}) async-start(f32[16,24,128]{2,1,0:T(8,128)} %shard_map.77), calls=%async_computation | async-start | bytes 393216 | tf_op jit(solution)/shard_map/all_to_all | solution.py:245
  20.4 12.5 %collective-permute-start = (f32[5,3,1152]{2,1,0:T(4,128)S(1)}, f32[5,3,1152]{2,1,0:T(4,128)S(1)}, u32[]{:S(2)}, u32[]{:S(2)}) collective-permute-start(f32[5,3,1152]{2,1,0:T(4,128)S(1)} %bitcast.16), channel_id=1, source_target_pairs={{0,16},{16,0},{1,17},{17,1},{2,18},{18,2},{3,19},{19,3},{4,20},{20... | collective-permute-start | bytes 207368 | tf_op jit(solution)/shard_map/ppermute | solution.py:238
  33.0 2.8 %shard_map.79.refs_0_ = f32[5,64,384]{2,1,0:T(8,128)S(1)} custom-call(f32[5,3,7680]{2,1,0:T(4,128)S(1)} %bitcast.14), custom_call_target="tpu_custom_call" | custom-call | flops 1000000000 | bytes 1000 | tf_op jit(solution)/shard_map/pallas_call | solution.py:239
  35.7 4.6 %collective-permute-start.2 = (f32[5,64,384]{2,1,0:T(8,128)S(1)}, f32[5,64,384]{2,1,0:T(8,128)S(1)}, u32[]{:S(2)}, u32[]{:S(2)}) collective-permute-start(f32[5,64,384]{2,1,0:T(8,128)S(1)} %shard_map.79.refs_0_), channel_id=1, source_target_pairs={{0,384},{128,0},{256,128},{384,256},{1,385},{129,1},{257,129},{385... | collective-permute-start | bytes 1474568 | tf_op jit(solution)/shard_map/ppermute | solution.py:241
  40.3 2.8 %collective-permute-start.4 = (f32[5,64,384]{2,1,0:T(8,128)S(1)}, f32[5,64,384]{2,1,0:T(8,128)S(1)}, u32[]{:S(2)}, u32[]{:S(2)}) collective-permute-start(f32[5,64,384]{2,1,0:T(8,128)S(1)} %shard_map.79.refs_0_), channel_id=1, source_target_pairs={{0,256},{128,384},{256,0},{384,128},{1,257},{129,385},{257,1},{385... | collective-permute-start | bytes 1474568 | tf_op jit(solution)/shard_map/ppermute | solution.py:241
  43.1 2.8 %collective-permute-start.6 = (f32[5,64,384]{2,1,0:T(8,128)S(1)}, f32[5,64,384]{2,1,0:T(8,128)S(1)}, u32[]{:S(2)}, u32[]{:S(2)}) collective-permute-start(f32[5,64,384]{2,1,0:T(8,128)S(1)} %shard_map.79.refs_0_), channel_id=1, source_target_pairs={{0,128},{128,256},{256,384},{384,0},{1,129},{129,257},{257,385},{3... | collective-permute-start | bytes 1474568 | tf_op jit(solution)/shard_map/ppermute | solution.py:241
  45.9 0.0 collective-permute-done.other_ref
  45.9 1.2 shard_map.78
  47.2 4.9 %all-to-all-start.1 = ((f32[4,672,128]{2,1,0:T(8,128)}), f32[4,672,128]{2,1,0:T(8,128)}, u32[]{:S(2)}, u32[]{:S(2)}) async-start(f32[4,672,128]{2,1,0:T(8,128)} %shard_map.78), calls=%async_computation.1 | async-start | bytes 2752512 | tf_op jit(solution)/shard_map/all_to_all | solution.py:247
  52.1 1.9 %collective-permute-start.1 = (f32[5,64,384]{2,1,0:T(8,128)S(1)}, f32[5,64,384]{2,1,0:T(8,128)S(1)}, u32[]{:S(2)}, u32[]{:S(2)}) collective-permute-start(f32[5,64,384]{2,1,0:T(8,128)S(1)} %shard_map.79.refs_0_), channel_id=1, source_target_pairs={{0,8},{8,0},{1,9},{9,1},{2,10},{10,2},{3,11},{11,3},{4,12},{12,4},... | collective-permute-start | bytes 1474568 | tf_op jit(solution)/shard_map/ppermute | solution.py:243
  54.0 7.4 %collective-permute-done.2.refs_2_ = f32[5,64,384]{2,1,0:T(8,128)S(1)} collective-permute-done((f32[5,64,384]{2,1,0:T(8,128)S(1)}, f32[5,64,384]{2,1,0:T(8,128)S(1)}, u32[]{:S(2)}, u32[]{:S(2)}) %collective-permute-start.2) | collective-permute-done | bytes 491552 | tf_op jit(solution)/shard_map/ppermute | solution.py:241
  61.4 1.9 %collective-permute-start.3 = (f32[5,64,384]{2,1,0:T(8,128)S(1)}, f32[5,64,384]{2,1,0:T(8,128)S(1)}, u32[]{:S(2)}, u32[]{:S(2)}) collective-permute-start(f32[5,64,384]{2,1,0:T(8,128)S(1)} %collective-permute-done.2.refs_2_), channel_id=1, source_target_pairs={{0,8},{8,0},{1,9},{9,1},{2,10},{10,2},{3,11},{11,3},{4,12},{12,4},... | collective-permute-start | bytes 1474568 | tf_op jit(solution)/shard_map/ppermute | solution.py:243
  63.3 2.4 %collective-permute-start.5 = (f32[5,64,384]{2,1,0:T(8,128)S(1)}, f32[5,64,384]{2,1,0:T(8,128)S(1)}, u32[]{:S(2)}, u32[]{:S(2)}) collective-permute-start(f32[5,64,384]{2,1,0:T(8,128)S(1)} %collective-permute-done.4.refs_4_), channel_id=1, source_target_pairs={{0,8},{8,0},{1,9},{9,1},{2,10},{10,2},{3,11},{11,3},{4,12},{12,4},... | collective-permute-start | bytes 1474568 | tf_op jit(solution)/shard_map/ppermute | solution.py:243
  65.8 1.2 collective-permute-done.6.refs_6_
  67.0 1.9 %collective-permute-start.7 = (f32[5,64,384]{2,1,0:T(8,128)S(1)}, f32[5,64,384]{2,1,0:T(8,128)S(1)}, u32[]{:S(2)}, u32[]{:S(2)}) collective-permute-start(f32[5,64,384]{2,1,0:T(8,128)S(1)} %collective-permute-done.6.refs_6_), channel_id=1, source_target_pairs={{0,8},{8,0},{1,9},{9,1},{2,10},{10,2},{3,11},{11,3},{4,12},{12,4},... | collective-permute-start | bytes 1474568 | tf_op jit(solution)/shard_map/ppermute | solution.py:243
  69.0 1.8 %collective-permute-done.7.refs_7_ = f32[5,64,384]{2,1,0:T(8,128)S(1)} collective-permute-done((f32[5,64,384]{2,1,0:T(8,128)S(1)}, f32[5,64,384]{2,1,0:T(8,128)S(1)}, u32[]{:S(2)}, u32[]{:S(2)}) %collective-permute-start.7) | collective-permute-done | bytes 491552 | tf_op jit(solution)/shard_map/ppermute | solution.py:243
  70.8 0.8 copy-done.3
  71.6 9.2 %shard_map.81 = f32[1152,128]{1,0:T(8,128)} custom-call(f32[4,672,128]{2,1,0:T(8,128)} %all-to-all-done.1.got_ref, f32[5,64,384]{2,1,0:T(8,128)S(1)} %shard_map.79.refs_0_, f32[5,64,384]{2,1,0:T(8,128)S(1)} %collective-permute-done.1.refs_1_, f32[5,64,384]{2,1,0:T(8,128)S(1)} %collective-permute-done.2.refs_2_, ...), custom_call_target="tpu_custom_call" | custom-call | flops 1000000000 | bytes 1000 | tf_op jit(solution)/shard_map/pallas_call | solution.py:250
  80.8 8.7 %all-to-all-start.2 = ((f32[64,1,2304]{2,1,0:T(1,128)}), f32[64,1,2304]{2,1,0:T(1,128)S(1)}, u32[]{:S(2)}, u32[]{:S(2)}) async-start(f32[64,1,2304]{2,1,0:T(1,128)} %bitcast.20), calls=%async_computation.2 | async-start | bytes 1179648 | tf_op jit(solution)/shard_map/all_to_all | solution.py:260
  90.1 0.1 stack.19.place_ref
  90.2 34.1 %all-to-all-done.2 = f32[64,1,2304]{2,1,0:T(1,128)S(1)} async-done(((f32[64,1,2304]{2,1,0:T(1,128)}), f32[64,1,2304]{2,1,0:T(1,128)S(1)}, u32[]{:S(2)}, u32[]{:S(2)}) %all-to-all-start.2) | async-done | bytes 589856 | tf_op jit(solution)/shard_map/all_to_all | solution.py:260
  124.3 2.1 %shard_map.82 = (f32[5,3,1152]{2,1,0:T(4,128)}, f32[5,3,1152]{2,1,0:T(4,128)}) custom-call(s32[5]{0:T(128)S(1)} %stack.19.place_ref, f32[40]{0:T(128)S(1)} %copy-done.9, f32[192]{0:T(256)S(1)} %copy-done.8, f32[1152,128]{1,0:T(8,128)S(1)} %bitcast.13, f32[1,192]{1,0:T(1,128)S(1)} %bitcast.19, f32[5,3,1152]{2,1,0:T(4,128)S(1)} %bitcast.18), custom_call_target="tpu_custom_call" | custom-call | flops 1000000000 | bytes 1000 | tf_op jit(solution)/shard_map/pallas_call | solution.py:263
  (25 shorter events, 0.1 us)
Async XLA Ops:
  0.6 0.9 copy-start.5
  1.5 18.9 %copy-start.6 = (f32[3,5,1152]{2,0,1:T(4,128)S(1)}, f32[3,5,1152]{2,0,1:T(4,128)}, u32[]{:S(2)}) copy-start(f32[3,5,1152]{2,0,1:T(4,128)} %param.6) | copy-start | bytes 207364
  1.5 31.4 %copy-start.4 = (f32[3,5,7680]{2,0,1:T(4,128)S(1)}, f32[3,5,7680]{2,0,1:T(4,128)}, u32[]{:S(2)}) copy-start(f32[3,5,7680]{2,0,1:T(4,128)} %param.7) | copy-start | bytes 1382404
  2.7 43.2 %all-to-all-start = ((f32[16,24,128]{2,1,0:T(8,128)}), f32[16,24,128]{2,1,0:T(8,128)S(1)}, u32[]{:S(2)}, u32[]{:S(2)}) async-start(f32[16,24,128]{2,1,0:T(8,128)} %shard_map.77), calls=%async_computation | async-start | bytes 393216 | tf_op jit(solution)/shard_map/all_to_all | solution.py:245
  20.4 25.5 %collective-permute-start = (f32[5,3,1152]{2,1,0:T(4,128)S(1)}, f32[5,3,1152]{2,1,0:T(4,128)S(1)}, u32[]{:S(2)}, u32[]{:S(2)}) collective-permute-start(f32[5,3,1152]{2,1,0:T(4,128)S(1)} %bitcast.16), channel_id=1, source_target_pairs={{0,16},{16,0},{1,17},{17,1},{2,18},{18,2},{3,19},{19,3},{4,20},{20... | collective-permute-start | bytes 207368 | tf_op jit(solution)/shard_map/ppermute | solution.py:238
  35.7 25.7 %collective-permute-start.2 = (f32[5,64,384]{2,1,0:T(8,128)S(1)}, f32[5,64,384]{2,1,0:T(8,128)S(1)}, u32[]{:S(2)}, u32[]{:S(2)}) collective-permute-start(f32[5,64,384]{2,1,0:T(8,128)S(1)} %shard_map.79.refs_0_), channel_id=1, source_target_pairs={{0,384},{128,0},{256,128},{384,256},{1,385},{129,1},{257,129},{385... | collective-permute-start | bytes 1474568 | tf_op jit(solution)/shard_map/ppermute | solution.py:241
  40.3 23.0 %collective-permute-start.4 = (f32[5,64,384]{2,1,0:T(8,128)S(1)}, f32[5,64,384]{2,1,0:T(8,128)S(1)}, u32[]{:S(2)}, u32[]{:S(2)}) collective-permute-start(f32[5,64,384]{2,1,0:T(8,128)S(1)} %shard_map.79.refs_0_), channel_id=1, source_target_pairs={{0,256},{128,384},{256,0},{384,128},{1,257},{129,385},{257,1},{385... | collective-permute-start | bytes 1474568 | tf_op jit(solution)/shard_map/ppermute | solution.py:241
  43.1 23.9 %collective-permute-start.6 = (f32[5,64,384]{2,1,0:T(8,128)S(1)}, f32[5,64,384]{2,1,0:T(8,128)S(1)}, u32[]{:S(2)}, u32[]{:S(2)}) collective-permute-start(f32[5,64,384]{2,1,0:T(8,128)S(1)} %shard_map.79.refs_0_), channel_id=1, source_target_pairs={{0,128},{128,256},{256,384},{384,0},{1,129},{129,257},{257,385},{3... | collective-permute-start | bytes 1474568 | tf_op jit(solution)/shard_map/ppermute | solution.py:241
  47.2 24.4 %all-to-all-start.1 = ((f32[4,672,128]{2,1,0:T(8,128)}), f32[4,672,128]{2,1,0:T(8,128)}, u32[]{:S(2)}, u32[]{:S(2)}) async-start(f32[4,672,128]{2,1,0:T(8,128)} %shard_map.78), calls=%async_computation.1 | async-start | bytes 2752512 | tf_op jit(solution)/shard_map/all_to_all | solution.py:247
  52.1 16.8 %collective-permute-start.1 = (f32[5,64,384]{2,1,0:T(8,128)S(1)}, f32[5,64,384]{2,1,0:T(8,128)S(1)}, u32[]{:S(2)}, u32[]{:S(2)}) collective-permute-start(f32[5,64,384]{2,1,0:T(8,128)S(1)} %shard_map.79.refs_0_), channel_id=1, source_target_pairs={{0,8},{8,0},{1,9},{9,1},{2,10},{10,2},{3,11},{11,3},{4,12},{12,4},... | collective-permute-start | bytes 1474568 | tf_op jit(solution)/shard_map/ppermute | solution.py:243
  61.4 7.5 %collective-permute-start.3 = (f32[5,64,384]{2,1,0:T(8,128)S(1)}, f32[5,64,384]{2,1,0:T(8,128)S(1)}, u32[]{:S(2)}, u32[]{:S(2)}) collective-permute-start(f32[5,64,384]{2,1,0:T(8,128)S(1)} %collective-permute-done.2.refs_2_), channel_id=1, source_target_pairs={{0,8},{8,0},{1,9},{9,1},{2,10},{10,2},{3,11},{11,3},{4,12},{12,4},... | collective-permute-start | bytes 1474568 | tf_op jit(solution)/shard_map/ppermute | solution.py:243
  63.3 7.4 %copy-start = (f32[5,64,384]{2,1,0:T(8,128)}, f32[5,64,384]{2,1,0:T(8,128)S(1)}, u32[]{:S(2)}) copy-start(f32[5,64,384]{2,1,0:T(8,128)S(1)} %collective-permute-done.4.refs_4_) | copy-start | bytes 1474564
  63.3 5.6 %collective-permute-start.5 = (f32[5,64,384]{2,1,0:T(8,128)S(1)}, f32[5,64,384]{2,1,0:T(8,128)S(1)}, u32[]{:S(2)}, u32[]{:S(2)}) collective-permute-start(f32[5,64,384]{2,1,0:T(8,128)S(1)} %collective-permute-done.4.refs_4_), channel_id=1, source_target_pairs={{0,8},{8,0},{1,9},{9,1},{2,10},{10,2},{3,11},{11,3},{4,12},{12,4},... | collective-permute-start | bytes 1474568 | tf_op jit(solution)/shard_map/ppermute | solution.py:243
  67.0 3.8 %copy-start.1 = (f32[5,64,384]{2,1,0:T(8,128)}, f32[5,64,384]{2,1,0:T(8,128)S(1)}, u32[]{:S(2)}) copy-start(f32[5,64,384]{2,1,0:T(8,128)S(1)} %collective-permute-done.6.refs_6_) | copy-start | bytes 1474564
  67.0 3.7 %collective-permute-start.7 = (f32[5,64,384]{2,1,0:T(8,128)S(1)}, f32[5,64,384]{2,1,0:T(8,128)S(1)}, u32[]{:S(2)}, u32[]{:S(2)}) collective-permute-start(f32[5,64,384]{2,1,0:T(8,128)S(1)} %collective-permute-done.6.refs_6_), channel_id=1, source_target_pairs={{0,8},{8,0},{1,9},{9,1},{2,10},{10,2},{3,11},{11,3},{4,12},{12,4},... | collective-permute-start | bytes 1474568 | tf_op jit(solution)/shard_map/ppermute | solution.py:243
  68.9 1.8 %copy-start.2 = (f32[5,64,384]{2,1,0:T(8,128)}, f32[5,64,384]{2,1,0:T(8,128)S(1)}, u32[]{:S(2)}) copy-start(f32[5,64,384]{2,1,0:T(8,128)S(1)} %collective-permute-done.5.refs_5_) | copy-start | bytes 1474564
  70.8 0.8 copy-start.3
  71.5 52.8 %copy-start.7 = (f32[3,5,1152]{2,0,1:T(4,128)S(1)}, f32[3,5,1152]{2,0,1:T(4,128)}, u32[]{:S(2)}) copy-start(f32[3,5,1152]{2,0,1:T(4,128)} %param.8) | copy-start | bytes 207364
  71.5 52.8 %copy-start.8 = (f32[192]{0:T(256)S(1)}, f32[192]{0:T(256)}, u32[]{:S(2)}) copy-start(f32[192]{0:T(256)} %va_ref.1) | copy-start | bytes 2308
  71.5 52.8 %copy-start.9 = (f32[40]{0:T(128)S(1)}, f32[40]{0:T(128)}, u32[]{:S(2)}) copy-start(f32[40]{0:T(128)} %occ_ref.1) | copy-start | bytes 484
  80.8 43.5 %all-to-all-start.2 = ((f32[64,1,2304]{2,1,0:T(1,128)}), f32[64,1,2304]{2,1,0:T(1,128)S(1)}, u32[]{:S(2)}, u32[]{:S(2)}) async-start(f32[64,1,2304]{2,1,0:T(1,128)} %bitcast.20), calls=%async_computation.2 | async-start | bytes 1179648 | tf_op jit(solution)/shard_map/all_to_all | solution.py:260

commit v5 on v4

--- a/solution.py
+++ b/solution.py
@@ -5,8 +5,8 @@
 from jax.experimental.pallas import tpu as pltpu
 from jax.sharding import Mesh, PartitionSpec as P
 
-AXES = ("x", "y", "zh", "core", "col")
-SIZES = (4, 4, 2, 2, 8)
+AXES = ("x", "y", "zh", "core", "pair", "par")
+SIZES = (4, 4, 2, 2, 4, 2)
 F32, BF16 = jnp.float32, jnp.bfloat16
 VMEM = pl.BlockSpec(memory_space=pltpu.VMEM)
 SMEM = pl.BlockSpec(memory_space=pltpu.SMEM)
@@ -54,13 +54,14 @@
     return hot(index((480, 384), 0) == row)
 
 
-def spread_matrix():
+def spread_matrix(par):
     n = index((1, 1280), 1)
     j, q = n >> 8, n & 255
+    slot = jnp.where((j & 1) == par, (j - par) >> 1, (j >> 1) + 3 - par)
     x = sum((q >= 48 * s).astype(jnp.int32) for s in range(1, 6))
     q = q - x * 48
     core = third(q, 2)
-    row = (x * 2 + core) * 16 + j * 3 + q - core * 3
+    row = (x * 2 + core) * 16 + slot * 3 + q - core * 3
     row = jnp.where((x < 4) & (q < 6), row, -1)
     return hot(index((128, 1280), 0) == row)
 
@@ -82,26 +83,15 @@
     return (dot(low, hot) + dot(mid, hot)) + dot(high, hot)
 
 
-def lanes192(ref, lead, n):
-    if n % 2 == 0:
-        return ref[lead, :, n * 192:n * 192 + 256]
-    return pltpu.roll(ref[lead, :, n * 192 - 64:n * 192 + 192], 192, 1)
-
-
 def weights_kernel(ints_ref, out_ref):
     out_ref[...] = jnp.zeros_like(out_ref)
-    lane = index((3, 128), 1)
-    for k in range(5):
-        for j in range(20):
-            at = j // 5 * 16 + j % 5 * 3
-            near = lanes192(ints_ref, k, j)
-            far = pltpu.roll(lanes192(ints_ref, k, j + 20), 64, 1)
-            out_ref[k, at:at + 3, :128] = near[:, :128]
-            out_ref[k, at:at + 3, 128:256] = jnp.where(lane < 64, near[:, 128:], far[:, :128])
-            out_ref[k, at:at + 3, 256:] = far[:, 128:]
-
-
-def swap_kernel(own_ref, two_ref, rows):
+    for k in range(5):
+        for n in range(20):
+            at = n // 5 * 16 + n % 5 * 3
+            out_ref[k, at:at + 3, :] = ints_ref[k, :, n * 384:(n + 1) * 384]
+
+
+def swap_kernel(own_ref, token_ref, two_ref, rows):
     rows[...] = jnp.zeros_like(rows)
     for k in range(5):
         for p in range(3):
@@ -140,9 +130,9 @@
     refs[-1][...] = jnp.zeros_like(refs[-1])
 
 
-def product_kernel(got_ref, *refs):
-    away, out_ref = refs[:8], refs[9]
-    two_high, two_low, mixed_high, mixed_low, weights, arrived = refs[10:]
+def product_kernel(par_ref, got_ref, *refs):
+    away, (keep_ref, send_ref) = refs[:8], refs[9:11]
+    two_high, two_low, swapped, whole, mixed, weights, arrived = refs[11:]
     copies = [pltpu.make_async_copy(away[n], weights.at[n], arrived.at[n]) for n in range(8)]
     for copy in copies:
         copy.start()
@@ -152,54 +142,63 @@
         high, low = split2(part)
         two_high[:, p * 128:(p + 1) * 128] = high
         two_low[:, p * 128:(p + 1) * 128] = low
-    orders, turn = [order_matrix(0), order_matrix(1)], turn_matrix()
+    turn = turn_matrix()
+    parts = [dot(turn, two[...], NT).astype(BF16) for two in (two_high, two_low)]
+    parts = jnp.concatenate(parts, 0)
+    for e in range(2):
+        moved_parts = dot(parts, order_matrix(e), NT)
+        swapped[e] = moved_parts[:480] + moved_parts[480:]
     lane = index((24, 256), 1)
     for k in range(5):
-        turn_k = turn[k * 96:(k + 1) * 96, :]
-        high = dot(turn_k, two_high[...], NT).astype(BF16)
-        low = dot(turn_k, two_low[...], NT).astype(BF16)
-        swapped = [dot(low, o, NT) + dot(high, o, NT) for o in orders]
-        mixed = []
         for y in range(4):
             v = [got_ref[y, part * 96 + k * 18:part * 96 + k * 18 + 24, :] for part in range(3)]
             near = jnp.concatenate(v[:2], 1)
             far = pltpu.roll(jnp.concatenate(v[1:], 1), 192, 1)
             for e, straight in enumerate((near, far)):
-                mixed.append(2.0 * jnp.where(lane < 192, straight, 0.0) - swapped[e][y * 24:(y + 1) * 24, :])
-        high, low = split2(jnp.concatenate(mixed, 0))
-        mixed_high[k] = high
-        mixed_low[k] = low
+                at = (k * 4 + y) * 24
+                value = 2.0 * jnp.where(lane < 192, straight, 0.0) - swapped[e, at:at + 24, :]
+                whole[y * 48 + e * 24:y * 48 + e * 24 + 24, :] = value
+        high, low = split2(whole[...])
+        mixed[k, :192] = high
+        mixed[k, 192:] = low
     for copy in copies:
         copy.wait()
-    for z in range(4):
+    even = par_ref[0] == 0
+    slot = index((192, 128), 1) & 15
+    for q in range(4):
         total = jnp.zeros((192, 256), F32)
         for k in range(5):
-            rows = [weights[n, k, z * 16:(z + 1) * 16, :] for n in range(8)]
+            rows = [weights[n, k, q * 16:(q + 1) * 16, :] for n in range(8)]
             near = [v[:, :256] for v in rows]
             far = [pltpu.roll(v[:, 128:], 192, 1) for v in rows]
             high, low = split2(jnp.concatenate(near + far, 0))
-            total += dot(mixed_high[k], low, NT) + dot(mixed_low[k], high, NT) + dot(mixed_high[k], high, NT)
-        for yz in range(8):
-            for half in range(2):
+            both = dot(mixed[k], high, NT)
+            total += dot(mixed[k, :192], low, NT) + both[192:]
+            total += both[:192]
+        near, far = total[:, :128], total[:, 128:]
+        first = jnp.where(slot < 9, near, pltpu.roll(far, 9, 1))
+        second = jnp.where(slot < 6, pltpu.roll(near, 119, 1), far)
+        for ref, v in ((keep_ref, jnp.where(even, first, second)), (send_ref, jnp.where(even, second, first))):
+            for yz in range(8):
                 for e in range(2):
-                    to = (yz * 8 + z + 4 * half) * 18 + e * 9
+                    to = (yz * 4 + q) * 18 + e * 9
                     at = yz // 2 * 48 + e * 24 + yz % 2 * 9
-                    out_ref[to:to + 9, :] = total[at:at + 9, half * 128:(half + 1) * 128]
+                    ref[to:to + 9, :] = v[at:at + 9, :]
 
 
 def final_kernel(place_ref, occ_ref, va_ref, got_ref, vb_ref, res_ref, new_ref, inc_ref, sums, cyc, den):
     sums[...] = jnp.zeros_like(sums)
     for yz in range(8):
-        total = got_ref[yz * 144:yz * 144 + 18, :]
-        for z in range(1, 8):
-            at = (yz * 8 + z) * 18
+        total = got_ref[yz * 72:yz * 72 + 18, :]
+        for z in range(1, 4):
+            at = (yz * 4 + z) * 18
             total += got_ref[at:at + 18, :]
         sums[yz * 24:yz * 24 + 18, :] = total
     v = pltpu.roll(sums[...], place_ref[0] * 32, 1)
     lane = lax.broadcasted_iota(jnp.int32, v.shape, 1)
     other = jnp.where((lane & 16) == 0, pltpu.roll(v, 112, 1), pltpu.roll(v, 16, 1))
     v = jnp.where(place_ref[1] == 0, v, other)
-    wide = moved(v, spread_matrix())
+    wide = moved(v, spread_matrix(place_ref[5]))
     row = lax.broadcasted_iota(jnp.int32, (3, 192), 0)
     va = [va_ref[place_ref[2] + m] for m in range(3)]
     va = jnp.where(row == 0, va[0], jnp.where(row == 1, va[1], va[2]))
@@ -231,7 +230,7 @@
 
 
 def body(amplitudes, integrals, residual, occupied_energy, virtual_energy, window_start):
-    x, y, zh, core, col = [lax.axis_index(a).astype(jnp.int32) for a in AXES]
+    x, y, zh, core, pair, par = [lax.axis_index(a).astype(jnp.int32) for a in AXES]
     amps = jnp.transpose(amplitudes, (1, 0, 2))
     ints = jnp.transpose(integrals, (1, 0, 2))
     res = jnp.transpose(residual, (1, 0, 2))
@@ -241,25 +240,27 @@
         lax.ppermute(weights, "x", [(s, (s - d) % 4) for s in range(4)]) for d in (1, 2, 3)
     ]
     across = [lax.ppermute(w, "core", [(0, 1), (1, 0)]) for w in along]
-    two = call(swap_kernel, 0, 1, [(16, 24, 128)], [pltpu.VMEM((120, 256), F32)])(amps)
+    two = call(swap_kernel, 0, 2, [(16, 24, 128)], [pltpu.VMEM((120, 256), F32)])(amps, weights)
     two = lax.all_to_all(two, ("x", "zh", "core"), 0, 0, tiled=True)
     both = call(pack_kernel, 1, 3, [(4, 672, 128)], [pltpu.VMEM((96, 384), F32)])(zh.reshape(1), amps, other, two)
     both = lax.all_to_all(both, "y", 0, 0, tiled=True)
     ordered = [w for pair in zip(along, across) for w in pair]
     mark = call(mark_kernel, 0, 8, [(8, 128)], [], 8, F32, 1, pl.ANY)(*ordered)
-    partial = pl.pallas_call(
+    keep, send = pl.pallas_call(
         product_kernel,
-        out_shape=jax.ShapeDtypeStruct((1152, 128), F32),
-        in_specs=[VMEM] + [pl.BlockSpec(memory_space=pl.ANY)] * 9,
-        out_specs=VMEM,
-        scratch_shapes=[pltpu.VMEM((512, 384), BF16)] * 2 + [pltpu.VMEM((5, 192, 256), BF16)] * 2
+        out_shape=[jax.ShapeDtypeStruct((576, 128), F32)] * 2,
+        in_specs=[SMEM, VMEM] + [pl.BlockSpec(memory_space=pl.ANY)] * 9,
+        out_specs=[VMEM] * 2,
+        scratch_shapes=[pltpu.VMEM((512, 384), BF16)] * 2
+        + [pltpu.VMEM((2, 480, 256), F32), pltpu.VMEM((192, 256), F32), pltpu.VMEM((5, 384, 256), BF16)]
         + [pltpu.VMEM((8, 5, 64, 384), F32), pltpu.SemaphoreType.DMA((8,))],
         cost_estimate=pl.CostEstimate(flops=10**9, bytes_accessed=1000, transcendentals=0),
         compiler_params=pltpu.CompilerParams(vmem_limit_bytes=52 * 1024 * 1024),
-    )(both, *ordered, mark)
-    got = lax.all_to_all(partial.reshape(64, 1, 2304), ("y", "zh", "col"), 0, 0, tiled=True).reshape(1152, 128)
+    )(par.reshape(1), both, *ordered, mark)
+    half = keep + lax.ppermute(send, "par", [(0, 1), (1, 0)])
+    got = lax.all_to_all(half.reshape(32, 1, 2304), ("y", "zh", "pair"), 0, 0, tiled=True).reshape(576, 128)
     r = ((x * 4 + y) * 2 + zh) * 2 + core
-    place = jnp.stack([x, core, r * 3, col * 5, window_start[0]])
+    place = jnp.stack([x, core, r * 3, (pair * 2 + par) * 5, window_start[0], par])
     new, inc = call(
         final_kernel, 3, 3, [(5, 3, 1152)] * 2,
         [pltpu.VMEM((192, 128), F32), pltpu.VMEM((3, 1152), F32), pltpu.VMEM((3, 1152), F32)],
@@ -269,7 +270,7 @@
 
 def solution(mesh):
     fine = Mesh(mesh.devices.reshape(SIZES), AXES)
-    split = P(("x", "y", "zh", "core"), "col", None)
+    split = P(("x", "y", "zh", "core"), ("pair", "par"), None)
     return jax.shard_map(
         body, mesh=fine, in_specs=(split, split, split, P(), P(), P()), out_specs=(split, split), check_vma=False
     )

time: 127 us -> 119 us (0.937)
  the two profiles are of different devices: /device:TPU:8 before, /device:TPU:64 now
where the time goes in v5:
time: 119 us
  starting transfers between devices  65.9 us (55%)
  waiting for transfers between devices  37.6 us (32%)
  Pallas kernels  10.9 us (9%)
  local copies, waits for them, and re-layouts  1.94 us (2%)
  between operations  1.52 us (1%)
    all_to_all x1, waiting for transfers between devices, body(): lax.all_to_all(half.reshape(32, 1, 2304), ('y', 'zh', 'pair'), 0, 0, tile...  20.4 us
    all_to_all x1, starting transfers between devices, body(): two = lax.all_to_all(two, ('x', 'zh', 'core'), 0, 0, tiled=True)  15.9 us
    ppermute x1, starting transfers between devices, body(): other = lax.ppermute(amps, 'zh', [(0, 1), (1, 0)])  12.5 us
    ppermute x3, starting transfers between devices, body(): lax.ppermute(weights, 'x', [(s, (s - d) % 4) for s in range(4)])  10.1 us
    all_to_all x1, starting transfers between devices, body(): lax.all_to_all(half.reshape(32, 1, 2304), ('y', 'zh', 'pair'), 0, 0, tile...  9.5 us
    ppermute x4, starting transfers between devices, body(): across = [lax.ppermute(w, 'core', [(0, 1), (1, 0)]) for w in along]  8.24 us
    ppermute x3, waiting for transfers between devices, body(): lax.ppermute(weights, 'x', [(s, (s - d) % 4) for s in range(4)])  7.52 us
    pallas_call x1, Pallas kernels, body(): pl.pallas_call(product_kernel, out_shape=[jax.ShapeDtypeStruct((576, 128)...  6.15 us
  transfers between devices with their start and end apart: 12, of which 7 were waited for; matrix products, arithmetic and copies ran while one was open for 0% of the time, Pallas kernels for 1%

profile of v5, /device:TPU:64, one launch (start us, length us, event | category | flops | bytes accessed | tf_op | source)
XLA Modules:
  0.0 118.7 jit_solution(13039121265967505040)
XLA Ops:
  0.6 1.1 copy-done.5
  1.8 0.7 copy-done.6
  2.6 1.2 %shard_map.78 = f32[16,24,128]{2,1,0:T(8,128)} custom-call(f32[5,3,1152]{2,1,0:T(4,128)S(1)} %bitcast.16, f32[5,64,384]{2,1,0:T(8,128)S(1)} %shard_map.77.token_ref.refs_0_), custom_call_target="tpu_custom_call" | custom-call | flops 1000000000 | bytes 1000 | tf_op jit(solution)/shard_map/pallas_call | solution.py:243
  3.8 15.9 %all-to-all-start = ((f32[16,24,128]{2,1,0:T(8,128)}), f32[16,24,128]{2,1,0:T(8,128)S(1)}, u32[]{:S(2)}, u32[]{:S(2)}) async-start(f32[16,24,128]{2,1,0:T(8,128)} %shard_map.78), calls=%async_computation | async-start | bytes 393216 | tf_op jit(solution)/shard_map/all_to_all | solution.py:244
  19.7 12.5 %collective-permute-start = (f32[5,3,1152]{2,1,0:T(4,128)S(1)}, f32[5,3,1152]{2,1,0:T(4,128)S(1)}, u32[]{:S(2)}, u32[]{:S(2)}) collective-permute-start(f32[5,3,1152]{2,1,0:T(4,128)S(1)} %bitcast.17), channel_id=1, source_target_pairs={{0,16},{16,0},{1,17},{17,1},{2,18},{18,2},{3,19},{19,3},{4,20},{20... | collective-permute-start | bytes 207368 | tf_op jit(solution)/shard_map/ppermute | solution.py:237
  32.2 4.6 %collective-permute-start.2 = (f32[5,64,384]{2,1,0:T(8,128)S(1)}, f32[5,64,384]{2,1,0:T(8,128)S(1)}, u32[]{:S(2)}, u32[]{:S(2)}) collective-permute-start(f32[5,64,384]{2,1,0:T(8,128)S(1)} %shard_map.77.token_ref.refs_0_), channel_id=1, source_target_pairs={{0,384},{128,0},{256,128},{384,256},{1,385},{129,1},{257,129},{385... | collective-permute-start | bytes 1474568 | tf_op jit(solution)/shard_map/ppermute | solution.py:240
  36.8 2.8 %collective-permute-start.4 = (f32[5,64,384]{2,1,0:T(8,128)S(1)}, f32[5,64,384]{2,1,0:T(8,128)S(1)}, u32[]{:S(2)}, u32[]{:S(2)}) collective-permute-start(f32[5,64,384]{2,1,0:T(8,128)S(1)} %shard_map.77.token_ref.refs_0_), channel_id=1, source_target_pairs={{0,256},{128,384},{256,0},{384,128},{1,257},{129,385},{257,1},{385... | collective-permute-start | bytes 1474568 | tf_op jit(solution)/shard_map/ppermute | solution.py:240
  39.6 2.8 %collective-permute-start.6 = (f32[5,64,384]{2,1,0:T(8,128)S(1)}, f32[5,64,384]{2,1,0:T(8,128)S(1)}, u32[]{:S(2)}, u32[]{:S(2)}) collective-permute-start(f32[5,64,384]{2,1,0:T(8,128)S(1)} %shard_map.77.token_ref.refs_0_), channel_id=1, source_target_pairs={{0,128},{128,256},{256,384},{384,0},{1,129},{129,257},{257,385},{3... | collective-permute-start | bytes 1474568 | tf_op jit(solution)/shard_map/ppermute | solution.py:240
  42.4 1.6 %collective-permute-done.other_ref = f32[5,3,1152]{2,1,0:T(4,128)S(1)} collective-permute-done((f32[5,3,1152]{2,1,0:T(4,128)S(1)}, f32[5,3,1152]{2,1,0:T(4,128)S(1)}, u32[]{:S(2)}, u32[]{:S(2)}) %collective-permute-start) | collective-permute-done | bytes 69152 | tf_op jit(solution)/shard_map/ppermute | solution.py:237
  44.0 1.3 %shard_map.79 = f32[4,672,128]{2,1,0:T(8,128)} custom-call(s32[1]{0:T(128)} %bitcast.5.zh_ref, f32[5,3,1152]{2,1,0:T(4,128)S(1)} %bitcast.18, f32[5,3,1152]{2,1,0:T(4,128)S(1)} %collective-permute-done.other_ref, f32[16,24,128]{2,1,0:T(8,128)S(1)} %all-to-all-done.two_ref), custom_call_target="tpu_custom_call" | custom-call | flops 1000000000 | bytes 1000 | tf_op jit(solution)/shard_map/pallas_call | solution.py:245
  45.2 4.5 %all-to-all-start.1 = ((f32[4,672,128]{2,1,0:T(8,128)}), f32[4,672,128]{2,1,0:T(8,128)}, u32[]{:S(2)}, u32[]{:S(2)}) async-start(f32[4,672,128]{2,1,0:T(8,128)} %shard_map.79), calls=%async_computation.1 | async-start | bytes 2752512 | tf_op jit(solution)/shard_map/all_to_all | solution.py:246
  49.7 1.9 %collective-permute-start.1 = (f32[5,64,384]{2,1,0:T(8,128)S(1)}, f32[5,64,384]{2,1,0:T(8,128)S(1)}, u32[]{:S(2)}, u32[]{:S(2)}) collective-permute-start(f32[5,64,384]{2,1,0:T(8,128)S(1)} %shard_map.77.token_ref.refs_0_), channel_id=1, source_target_pairs={{0,8},{8,0},{1,9},{9,1},{2,10},{10,2},{3,11},{11,3},{4,12},{12,4},... | collective-permute-start | bytes 1474568 | tf_op jit(solution)/shard_map/ppermute | solution.py:242
  51.6 6.3 %collective-permute-done.2.refs_2_ = f32[5,64,384]{2,1,0:T(8,128)S(1)} collective-permute-done((f32[5,64,384]{2,1,0:T(8,128)S(1)}, f32[5,64,384]{2,1,0:T(8,128)S(1)}, u32[]{:S(2)}, u32[]{:S(2)}) %collective-permute-start.2) | collective-permute-done | bytes 491552 | tf_op jit(solution)/shard_map/ppermute | solution.py:240
  57.9 1.9 %collective-permute-start.3 = (f32[5,64,384]{2,1,0:T(8,128)S(1)}, f32[5,64,384]{2,1,0:T(8,128)S(1)}, u32[]{:S(2)}, u32[]{:S(2)}) collective-permute-start(f32[5,64,384]{2,1,0:T(8,128)S(1)} %collective-permute-done.2.refs_2_), channel_id=1, source_target_pairs={{0,8},{8,0},{1,9},{9,1},{2,10},{10,2},{3,11},{11,3},{4,12},{12,4},... | collective-permute-start | bytes 1474568 | tf_op jit(solution)/shard_map/ppermute | solution.py:242
  59.8 2.4 %collective-permute-start.5 = (f32[5,64,384]{2,1,0:T(8,128)S(1)}, f32[5,64,384]{2,1,0:T(8,128)S(1)}, u32[]{:S(2)}, u32[]{:S(2)}) collective-permute-start(f32[5,64,384]{2,1,0:T(8,128)S(1)} %collective-permute-done.4.refs_4_), channel_id=1, source_target_pairs={{0,8},{8,0},{1,9},{9,1},{2,10},{10,2},{3,11},{11,3},{4,12},{12,4},... | collective-permute-start | bytes 1474568 | tf_op jit(solution)/shard_map/ppermute | solution.py:242
  62.2 1.2 %collective-permute-done.6.refs_6_ = f32[5,64,384]{2,1,0:T(8,128)S(1)} collective-permute-done((f32[5,64,384]{2,1,0:T(8,128)S(1)}, f32[5,64,384]{2,1,0:T(8,128)S(1)}, u32[]{:S(2)}, u32[]{:S(2)}) %collective-permute-start.6) | collective-permute-done | bytes 491552 | tf_op jit(solution)/shard_map/ppermute | solution.py:240
  63.5 2.0 %collective-permute-start.7 = (f32[5,64,384]{2,1,0:T(8,128)S(1)}, f32[5,64,384]{2,1,0:T(8,128)}, u32[]{:S(2)}, u32[]{:S(2)}) collective-permute-start(f32[5,64,384]{2,1,0:T(8,128)S(1)} %collective-permute-done.6.refs_6_), channel_id=1, source_target_pairs={{0,8},{8,0},{1,9},{9,1},{2,10},{10,2},{3,11},{11,3},{4,12},{12,4},... | collective-permute-start | bytes 1474568 | tf_op jit(solution)/shard_map/ppermute | solution.py:242
  65.5 1.8 %collective-permute-done.7.refs_7_ = f32[5,64,384]{2,1,0:T(8,128)} collective-permute-done((f32[5,64,384]{2,1,0:T(8,128)S(1)}, f32[5,64,384]{2,1,0:T(8,128)}, u32[]{:S(2)}, u32[]{:S(2)}) %collective-permute-start.7) | collective-permute-done | bytes 491552 | tf_op jit(solution)/shard_map/ppermute | solution.py:242
  68.1 6.2 %shard_map.81 = (f32[576,128]{1,0:T(8,128)S(1)}, f32[576,128]{1,0:T(8,128)S(1)}) custom-call(s32[1]{0:T(128)} %bitcast.4.par_ref, f32[4,672,128]{2,1,0:T(8,128)} %all-to-all-done.1.got_ref, f32[5,64,384]{2,1,0:T(8,128)S(1)} %shard_map.77.token_ref.refs_0_, f32[5,64,384]{2,1,0:T(8,128)S(1)} %collective-permute-done.1.refs_1_, f32[5,64,384]{2,1,0:T(8,128)} %copy-done, ...), custom_call_target="tpu_custom_call" | custom-call | flops 1000000000 | bytes 1000 | tf_op jit(solution)/shard_map/pallas_call | solution.py:249
  74.3 5.2 %collective-permute-start.8 = (f32[576,128]{1,0:T(8,128)S(1)}, f32[576,128]{1,0:T(8,128)S(1)}, u32[]{:S(2)}, u32[]{:S(2)}) collective-permute-start(f32[576,128]{1,0:T(8,128)S(1)} %get-tuple-element.7), channel_id=1, source_target_pairs={{0,1},{1,0},{2,3},{3,2},{4,5},{5,4},{6,7},{7,6},{8,9},{9,8},{10,11... | collective-permute-start | bytes 884744 | tf_op jit(solution)/shard_map/ppermute | solution.py:260
  79.5 5.6 %collective-permute-done.8 = f32[576,128]{1,0:T(8,128)S(1)} collective-permute-done((f32[576,128]{1,0:T(8,128)S(1)}, f32[576,128]{1,0:T(8,128)S(1)}, u32[]{:S(2)}, u32[]{:S(2)}) %collective-permute-start.8) | collective-permute-done | bytes 294944 | tf_op jit(solution)/shard_map/ppermute | solution.py:260
  85.8 9.5 %all-to-all-start.2 = ((f32[32,1,2304]{2,1,0:T(1,128)}), f32[32,1,2304]{2,1,0:T(1,128)S(1)}, u32[]{:S(2)}, u32[]{:S(2)}) async-start(f32[32,1,2304]{2,1,0:T(1,128)} %bitcast.8), calls=%async_computation.2 | async-start | bytes 589824 | tf_op jit(solution)/shard_map/all_to_all | solution.py:261
  96.1 20.4 %all-to-all-done.2 = f32[32,1,2304]{2,1,0:T(1,128)S(1)} async-done(((f32[32,1,2304]{2,1,0:T(1,128)}), f32[32,1,2304]{2,1,0:T(1,128)S(1)}, u32[]{:S(2)}, u32[]{:S(2)}) %all-to-all-start.2) | async-done | bytes 294944 | tf_op jit(solution)/shard_map/all_to_all | solution.py:261
  116.6 2.2 %shard_map.82 = (f32[5,3,1152]{2,1,0:T(4,128)}, f32[5,3,1152]{2,1,0:T(4,128)}) custom-call(s32[6]{0:T(128)S(1)} %stack.23.place_ref, f32[40]{0:T(128)S(1)} %copy-done.9, f32[192]{0:T(256)S(1)} %copy-done.8, f32[576,128]{1,0:T(8,128)S(1)} %bitcast.14, f32[1,192]{1,0:T(1,128)S(1)} %bitcast.20, f32[5,3,1152]{2,1,0:T(4,128)S(1)} %bitcast.19), custom_call_target="tpu_custom_call" | custom-call | flops 1000000000 | bytes 1000 | tf_op jit(solution)/shard_map/pallas_call | solution.py:264
  (28 shorter events, 1.8 us)
Async XLA Ops:
  0.6 1.1 copy-start.5
  1.7 0.9 copy-start.6
  3.8 40.1 %all-to-all-start = ((f32[16,24,128]{2,1,0:T(8,128)}), f32[16,24,128]{2,1,0:T(8,128)S(1)}, u32[]{:S(2)}, u32[]{:S(2)}) async-start(f32[16,24,128]{2,1,0:T(8,128)} %shard_map.78), calls=%async_computation | async-start | bytes 393216 | tf_op jit(solution)/shard_map/all_to_all | solution.py:244
  19.7 24.3 %collective-permute-start = (f32[5,3,1152]{2,1,0:T(4,128)S(1)}, f32[5,3,1152]{2,1,0:T(4,128)S(1)}, u32[]{:S(2)}, u32[]{:S(2)}) collective-permute-start(f32[5,3,1152]{2,1,0:T(4,128)S(1)} %bitcast.17), channel_id=1, source_target_pairs={{0,16},{16,0},{1,17},{17,1},{2,18},{18,2},{3,19},{19,3},{4,20},{20... | collective-permute-start | bytes 207368 | tf_op jit(solution)/shard_map/ppermute | solution.py:237
  32.2 25.7 %collective-permute-start.2 = (f32[5,64,384]{2,1,0:T(8,128)S(1)}, f32[5,64,384]{2,1,0:T(8,128)S(1)}, u32[]{:S(2)}, u32[]{:S(2)}) collective-permute-start(f32[5,64,384]{2,1,0:T(8,128)S(1)} %shard_map.77.token_ref.refs_0_), channel_id=1, source_target_pairs={{0,384},{128,0},{256,128},{384,256},{1,385},{129,1},{257,129},{385... | collective-permute-start | bytes 1474568 | tf_op jit(solution)/shard_map/ppermute | solution.py:240
  36.8 23.0 %collective-permute-start.4 = (f32[5,64,384]{2,1,0:T(8,128)S(1)}, f32[5,64,384]{2,1,0:T(8,128)S(1)}, u32[]{:S(2)}, u32[]{:S(2)}) collective-permute-start(f32[5,64,384]{2,1,0:T(8,128)S(1)} %shard_map.77.token_ref.refs_0_), channel_id=1, source_target_pairs={{0,256},{128,384},{256,0},{384,128},{1,257},{129,385},{257,1},{385... | collective-permute-start | bytes 1474568 | tf_op jit(solution)/shard_map/ppermute | solution.py:240
  39.6 23.9 %collective-permute-start.6 = (f32[5,64,384]{2,1,0:T(8,128)S(1)}, f32[5,64,384]{2,1,0:T(8,128)S(1)}, u32[]{:S(2)}, u32[]{:S(2)}) collective-permute-start(f32[5,64,384]{2,1,0:T(8,128)S(1)} %shard_map.77.token_ref.refs_0_), channel_id=1, source_target_pairs={{0,128},{128,256},{256,384},{384,0},{1,129},{129,257},{257,385},{3... | collective-permute-start | bytes 1474568 | tf_op jit(solution)/shard_map/ppermute | solution.py:240
  45.2 22.9 %all-to-all-start.1 = ((f32[4,672,128]{2,1,0:T(8,128)}), f32[4,672,128]{2,1,0:T(8,128)}, u32[]{:S(2)}, u32[]{:S(2)}) async-start(f32[4,672,128]{2,1,0:T(8,128)} %shard_map.79), calls=%async_computation.1 | async-start | bytes 2752512 | tf_op jit(solution)/shard_map/all_to_all | solution.py:246
  49.7 15.8 %collective-permute-start.1 = (f32[5,64,384]{2,1,0:T(8,128)S(1)}, f32[5,64,384]{2,1,0:T(8,128)S(1)}, u32[]{:S(2)}, u32[]{:S(2)}) collective-permute-start(f32[5,64,384]{2,1,0:T(8,128)S(1)} %shard_map.77.token_ref.refs_0_), channel_id=1, source_target_pairs={{0,8},{8,0},{1,9},{9,1},{2,10},{10,2},{3,11},{11,3},{4,12},{12,4},... | collective-permute-start | bytes 1474568 | tf_op jit(solution)/shard_map/ppermute | solution.py:242
  57.9 9.5 %copy-start = (f32[5,64,384]{2,1,0:T(8,128)}, f32[5,64,384]{2,1,0:T(8,128)S(1)}, u32[]{:S(2)}) copy-start(f32[5,64,384]{2,1,0:T(8,128)S(1)} %collective-permute-done.2.refs_2_) | copy-start | bytes 1474564
  57.9 7.6 %collective-permute-start.3 = (f32[5,64,384]{2,1,0:T(8,128)S(1)}, f32[5,64,384]{2,1,0:T(8,128)S(1)}, u32[]{:S(2)}, u32[]{:S(2)}) collective-permute-start(f32[5,64,384]{2,1,0:T(8,128)S(1)} %collective-permute-done.2.refs_2_), channel_id=1, source_target_pairs={{0,8},{8,0},{1,9},{9,1},{2,10},{10,2},{3,11},{11,3},{4,12},{12,4},... | collective-permute-start | bytes 1474568 | tf_op jit(solution)/shard_map/ppermute | solution.py:242
  59.8 7.5 %copy-start.1 = (f32[5,64,384]{2,1,0:T(8,128)}, f32[5,64,384]{2,1,0:T(8,128)S(1)}, u32[]{:S(2)}) copy-start(f32[5,64,384]{2,1,0:T(8,128)S(1)} %collective-permute-done.4.refs_4_) | copy-start | bytes 1474564
  59.8 5.7 %collective-permute-start.5 = (f32[5,64,384]{2,1,0:T(8,128)S(1)}, f32[5,64,384]{2,1,0:T(8,128)S(1)}, u32[]{:S(2)}, u32[]{:S(2)}) collective-permute-start(f32[5,64,384]{2,1,0:T(8,128)S(1)} %collective-permute-done.4.refs_4_), channel_id=1, source_target_pairs={{0,8},{8,0},{1,9},{9,1},{2,10},{10,2},{3,11},{11,3},{4,12},{12,4},... | collective-permute-start | bytes 1474568 | tf_op jit(solution)/shard_map/ppermute | solution.py:242
  63.5 3.9 %copy-start.2 = (f32[5,64,384]{2,1,0:T(8,128)}, f32[5,64,384]{2,1,0:T(8,128)S(1)}, u32[]{:S(2)}) copy-start(f32[5,64,384]{2,1,0:T(8,128)S(1)} %collective-permute-done.6.refs_6_) | copy-start | bytes 1474564
  63.5 3.9 %collective-permute-start.7 = (f32[5,64,384]{2,1,0:T(8,128)S(1)}, f32[5,64,384]{2,1,0:T(8,128)}, u32[]{:S(2)}, u32[]{:S(2)}) collective-permute-start(f32[5,64,384]{2,1,0:T(8,128)S(1)} %collective-permute-done.6.refs_6_), channel_id=1, source_target_pairs={{0,8},{8,0},{1,9},{9,1},{2,10},{10,2},{3,11},{11,3},{4,12},{12,4},... | collective-permute-start | bytes 1474568 | tf_op jit(solution)/shard_map/ppermute | solution.py:242
  65.5 1.8 %copy-start.3 = (f32[5,64,384]{2,1,0:T(8,128)}, f32[5,64,384]{2,1,0:T(8,128)S(1)}, u32[]{:S(2)}) copy-start(f32[5,64,384]{2,1,0:T(8,128)S(1)} %collective-permute-done.3.refs_3_) | copy-start | bytes 1474564
  65.5 1.8 %copy-start.4 = (f32[5,64,384]{2,1,0:T(8,128)}, f32[5,64,384]{2,1,0:T(8,128)S(1)}, u32[]{:S(2)}) copy-start(f32[5,64,384]{2,1,0:T(8,128)S(1)} %collective-permute-done.5.refs_5_) | copy-start | bytes 1474564
  74.3 42.3 %copy-start.7 = (f32[3,5,1152]{2,0,1:T(4,128)S(1)}, f32[3,5,1152]{2,0,1:T(4,128)}, u32[]{:S(2)}) copy-start(f32[3,5,1152]{2,0,1:T(4,128)} %param.8) | copy-start | bytes 207364
  74.3 42.3 %copy-start.8 = (f32[192]{0:T(256)S(1)}, f32[192]{0:T(256)}, u32[]{:S(2)}) copy-start(f32[192]{0:T(256)} %va_ref.1) | copy-start | bytes 2308
  74.3 42.3 %copy-start.9 = (f32[40]{0:T(128)S(1)}, f32[40]{0:T(128)}, u32[]{:S(2)}) copy-start(f32[40]{0:T(128)} %occ_ref.1) | copy-start | bytes 484
  74.3 10.8 %collective-permute-start.8 = (f32[576,128]{1,0:T(8,128)S(1)}, f32[576,128]{1,0:T(8,128)S(1)}, u32[]{:S(2)}, u32[]{:S(2)}) collective-permute-start(f32[576,128]{1,0:T(8,128)S(1)} %get-tuple-element.7), channel_id=1, source_target_pairs={{0,1},{1,0},{2,3},{3,2},{4,5},{5,4},{6,7},{7,6},{8,9},{9,8},{10,11... | collective-permute-start | bytes 884744 | tf_op jit(solution)/shard_map/ppermute | solution.py:260
  85.8 30.7 %all-to-all-start.2 = ((f32[32,1,2304]{2,1,0:T(1,128)}), f32[32,1,2304]{2,1,0:T(1,128)S(1)}, u32[]{:S(2)}, u32[]{:S(2)}) async-start(f32[32,1,2304]{2,1,0:T(1,128)} %bitcast.8), calls=%async_computation.2 | async-start | bytes 589824 | tf_op jit(solution)/shard_map/all_to_all | solution.py:261

commit v6 on v5

--- a/solution.py
+++ b/solution.py
@@ -83,7 +83,7 @@
     return (dot(low, hot) + dot(mid, hot)) + dot(high, hot)
 
 
-def weights_kernel(ints_ref, out_ref):
+def weights_kernel(ints_ref, token_ref, out_ref):
     out_ref[...] = jnp.zeros_like(out_ref)
     for k in range(5):
         for n in range(20):
@@ -91,7 +91,7 @@
             out_ref[k, at:at + 3, :] = ints_ref[k, :, n * 384:(n + 1) * 384]
 
 
-def swap_kernel(own_ref, token_ref, two_ref, rows):
+def swap_kernel(own_ref, two_ref, rows):
     rows[...] = jnp.zeros_like(rows)
     for k in range(5):
         for p in range(3):
@@ -110,7 +110,7 @@
             two_ref[n // 2 * 4 + zh * 2 + n % 2] = part
 
 
-def pack_kernel(zh_ref, own_ref, other_ref, two_ref, out_ref, rows):
+def merge_kernel(zh_ref, own_ref, other_ref, out_ref, rows):
     first = zh_ref[0] == 0
     rows[...] = jnp.zeros_like(rows)
     for k in range(5):
@@ -120,9 +120,13 @@
             at = k * 18 + p * 3
             rows[at:at + 3, :] = jnp.where(first, own, other)
             rows[at + 9:at + 12, :] = jnp.where(first, other, own)
+    for part in range(3):
+        out_ref[part * 96:(part + 1) * 96, :] = rows[:, part * 128:(part + 1) * 128]
+
+
+def pack_kernel(one_ref, two_ref, out_ref):
     for y in range(4):
-        for part in range(3):
-            out_ref[y, part * 96:(part + 1) * 96, :] = rows[:, part * 128:(part + 1) * 128]
+        out_ref[y, :288, :] = one_ref[...]
         out_ref[y, 288:, :] = two_ref[...].reshape(384, 128)
 
 
@@ -235,14 +239,15 @@
     ints = jnp.transpose(integrals, (1, 0, 2))
     res = jnp.transpose(residual, (1, 0, 2))
     other = lax.ppermute(amps, "zh", [(0, 1), (1, 0)])
-    weights = call(weights_kernel, 0, 1, [(5, 64, 384)], [])(ints)
+    two = call(swap_kernel, 0, 1, [(16, 24, 128)], [pltpu.VMEM((120, 256), F32)])(amps)
+    weights = call(weights_kernel, 0, 2, [(5, 64, 384)], [])(ints, two)
     along = [weights] + [
         lax.ppermute(weights, "x", [(s, (s - d) % 4) for s in range(4)]) for d in (1, 2, 3)
     ]
     across = [lax.ppermute(w, "core", [(0, 1), (1, 0)]) for w in along]
-    two = call(swap_kernel, 0, 2, [(16, 24, 128)], [pltpu.VMEM((120, 256), F32)])(amps, weights)
     two = lax.all_to_all(two, ("x", "zh", "core"), 0, 0, tiled=True)
-    both = call(pack_kernel, 1, 3, [(4, 672, 128)], [pltpu.VMEM((96, 384), F32)])(zh.reshape(1), amps, other, two)
+    one = call(merge_kernel, 1, 2, [(288, 128)], [pltpu.VMEM((96, 384), F32)], cost=8)(zh.reshape(1), amps, other)
+    both = call(pack_kernel, 0, 2, [(4, 672, 128)], [])(one, two)
     both = lax.all_to_all(both, "y", 0, 0, tiled=True)
     ordered = [w for pair in zip(along, across) for w in pair]
     mark = call(mark_kernel, 0, 8, [(8, 128)], [], 8, F32, 1, pl.ANY)(*ordered)

time: 119 us -> 118 us (level)
  starting transfers between devices: 65.9 us -> 56.7 us
  waiting for transfers between devices: 37.6 us -> 45.3 us
    all_to_all x1, starting transfers between devices: 15.9 us -> 4.4 us  [body(): two = lax.all_to_all(two, ('x', 'zh', 'core'), 0, 0, tiled=True)]
    all_to_all x1, waiting for transfers between devices: 0.01 us -> 6.73 us  [body(): two = lax.all_to_all(two, ('x', 'zh', 'core'), 0, 0, tiled=True)]
    all_to_all x1, waiting for transfers between devices: 0.73 us -> 4.85 us  [body(): both = lax.all_to_all(both, 'y', 0, 0, tiled=True)]
    ppermute x3, waiting for transfers between devices: 7.52 us -> 3.7 us  [body(): lax.ppermute(weights, 'x', [(s, (s - d) % 4) for s in range(4)])]
    all_to_all x1, starting transfers between devices: 9.5 us -> 12.9 us  [body(): lax.all_to_all(half.reshape(32, 1, 2304), ('y', 'zh', 'pair'), 0, 0, tile...]
    ppermute x1, starting transfers between devices: 5.22 us -> 2.05 us  [body(): half = keep + lax.ppermute(send, 'par', [(0, 1), (1, 0)])]
    ppermute x1, waiting for transfers between devices: 5.56 us -> 7.54 us  [body(): half = keep + lax.ppermute(send, 'par', [(0, 1), (1, 0)])]
    ppermute x1, waiting for transfers between devices: 1.59 us -> 0.01 us  [body(): other = lax.ppermute(amps, 'zh', [(0, 1), (1, 0)])]
  transfers between devices with their start and end apart: 12 -> 12, of which waited for: 7 -> 7; matrix products, arithmetic and copies ran while one was open for 0% -> 0% of each run, Pallas kernels for 1% -> 3%
where the time goes in v6:
time: 118 us; the launch traced here: 117 us
  starting transfers between devices  56.7 us (48%)
  waiting for transfers between devices  45.3 us (38%)
  Pallas kernels  11.9 us (10%)
  between operations  1.57 us (1%)
    all_to_all x1, waiting for transfers between devices, body(): lax.all_to_all(half.reshape(32, 1, 2304), ('y', 'zh', 'pair'), 0, 0, tile...  20.7 us
    ppermute x1, starting transfers between devices, body(): other = lax.ppermute(amps, 'zh', [(0, 1), (1, 0)])  14.1 us
    all_to_all x1, starting transfers between devices, body(): lax.all_to_all(half.reshape(32, 1, 2304), ('y', 'zh', 'pair'), 0, 0, tile...  12.9 us
    ppermute x3, starting transfers between devices, body(): lax.ppermute(weights, 'x', [(s, (s - d) % 4) for s in range(4)])  10.6 us
    ppermute x4, starting transfers between devices, body(): across = [lax.ppermute(w, 'core', [(0, 1), (1, 0)]) for w in along]  8.24 us
    ppermute x1, waiting for transfers between devices, body(): half = keep + lax.ppermute(send, 'par', [(0, 1), (1, 0)])  7.54 us
    all_to_all x1, waiting for transfers between devices, body(): two = lax.all_to_all(two, ('x', 'zh', 'core'), 0, 0, tiled=True)  6.73 us
    pallas_call x1, Pallas kernels, body(): pl.pallas_call(product_kernel, out_shape=[jax.ShapeDtypeStruct((576, 128)...  6.16 us
  transfers between devices with their start and end apart: 12, of which 7 were waited for; matrix products, arithmetic and copies ran while one was open for 0% of the time, Pallas kernels for 3%

profile of v6, /device:TPU:64, one launch (start us, length us, event | category | flops | bytes accessed | tf_op | source)
XLA Modules:
  0.0 117.2 jit_solution(10578145767388776565)
XLA Ops:
  0.6 14.1 %collective-permute-start = (f32[5,3,1152]{2,1,0:T(4,128)}, f32[5,3,1152]{2,1,0:T(4,128)S(1)}, u32[]{:S(2)}, u32[]{:S(2)}) collective-permute-start(f32[5,3,1152]{2,1,0:T(4,128)} %bitcast.16), channel_id=1, source_target_pairs={{0,16},{16,0},{1,17},{17,1},{2,18},{18,2},{3,19},{19,3},{4,20},{20... | collective-permute-start | bytes 207368 | tf_op jit(solution)/shard_map/ppermute | solution.py:241
  15.6 1.2 %shard_map.78.token_ref = f32[16,24,128]{2,1,0:T(8,128)} custom-call(f32[5,3,1152]{2,1,0:T(4,128)S(1)} %bitcast.17), custom_call_target="tpu_custom_call" | custom-call | flops 1000000000 | bytes 1000 | tf_op jit(solution)/shard_map/pallas_call | solution.py:242
  16.8 4.4 %all-to-all-start = ((f32[16,24,128]{2,1,0:T(8,128)}), f32[16,24,128]{2,1,0:T(8,128)S(1)}, u32[]{:S(2)}, u32[]{:S(2)}) async-start(f32[16,24,128]{2,1,0:T(8,128)} %shard_map.78.token_ref), calls=%async_computation | async-start | bytes 393216 | tf_op jit(solution)/shard_map/all_to_all | solution.py:248
  21.3 1.1 shard_map.80.refs_0_
  22.4 5.1 %collective-permute-start.2 = (f32[5,64,384]{2,1,0:T(8,128)S(1)}, f32[5,64,384]{2,1,0:T(8,128)S(1)}, u32[]{:S(2)}, u32[]{:S(2)}) collective-permute-start(f32[5,64,384]{2,1,0:T(8,128)S(1)} %shard_map.80.refs_0_), channel_id=1, source_target_pairs={{0,384},{128,0},{256,128},{384,256},{1,385},{129,1},{257,129},{385... | collective-permute-start | bytes 1474568 | tf_op jit(solution)/shard_map/ppermute | solution.py:245
  27.4 2.8 %collective-permute-start.4 = (f32[5,64,384]{2,1,0:T(8,128)S(1)}, f32[5,64,384]{2,1,0:T(8,128)S(1)}, u32[]{:S(2)}, u32[]{:S(2)}) collective-permute-start(f32[5,64,384]{2,1,0:T(8,128)S(1)} %shard_map.80.refs_0_), channel_id=1, source_target_pairs={{0,256},{128,384},{256,0},{384,128},{1,257},{129,385},{257,1},{385... | collective-permute-start | bytes 1474568 | tf_op jit(solution)/shard_map/ppermute | solution.py:245
  30.2 2.8 %collective-permute-start.6 = (f32[5,64,384]{2,1,0:T(8,128)S(1)}, f32[5,64,384]{2,1,0:T(8,128)S(1)}, u32[]{:S(2)}, u32[]{:S(2)}) collective-permute-start(f32[5,64,384]{2,1,0:T(8,128)S(1)} %shard_map.80.refs_0_), channel_id=1, source_target_pairs={{0,128},{128,256},{256,384},{384,0},{1,129},{129,257},{257,385},{3... | collective-permute-start | bytes 1474568 | tf_op jit(solution)/shard_map/ppermute | solution.py:245
  33.1 6.7 %all-to-all-done.two_ref = f32[16,24,128]{2,1,0:T(8,128)S(1)} async-done(((f32[16,24,128]{2,1,0:T(8,128)}), f32[16,24,128]{2,1,0:T(8,128)S(1)}, u32[]{:S(2)}, u32[]{:S(2)}) %all-to-all-start) | async-done | bytes 196640 | tf_op jit(solution)/shard_map/all_to_all | solution.py:248
  39.8 1.2 %shard_map.79 = f32[4,672,128]{2,1,0:T(8,128)} custom-call(f32[288,128]{1,0:T(8,128)S(1)} %shard_map.77.one_ref, f32[16,24,128]{2,1,0:T(8,128)S(1)} %all-to-all-done.two_ref), custom_call_target="tpu_custom_call" | custom-call | flops 1000000000 | bytes 1000 | tf_op jit(solution)/shard_map/pallas_call | solution.py:250
  41.0 4.5 %all-to-all-start.1 = ((f32[4,672,128]{2,1,0:T(8,128)}), f32[4,672,128]{2,1,0:T(8,128)}, u32[]{:S(2)}, u32[]{:S(2)}) async-start(f32[4,672,128]{2,1,0:T(8,128)} %shard_map.79), calls=%async_computation.1 | async-start | bytes 2752512 | tf_op jit(solution)/shard_map/all_to_all | solution.py:251
  45.4 1.9 %collective-permute-start.1 = (f32[5,64,384]{2,1,0:T(8,128)S(1)}, f32[5,64,384]{2,1,0:T(8,128)S(1)}, u32[]{:S(2)}, u32[]{:S(2)}) collective-permute-start(f32[5,64,384]{2,1,0:T(8,128)S(1)} %shard_map.80.refs_0_), channel_id=1, source_target_pairs={{0,8},{8,0},{1,9},{9,1},{2,10},{10,2},{3,11},{11,3},{4,12},{12,4},... | collective-permute-start | bytes 1474568 | tf_op jit(solution)/shard_map/ppermute | solution.py:247
  47.4 2.4 %collective-permute-done.2.refs_2_ = f32[5,64,384]{2,1,0:T(8,128)S(1)} collective-permute-done((f32[5,64,384]{2,1,0:T(8,128)S(1)}, f32[5,64,384]{2,1,0:T(8,128)S(1)}, u32[]{:S(2)}, u32[]{:S(2)}) %collective-permute-start.2) | collective-permute-done | bytes 491552 | tf_op jit(solution)/shard_map/ppermute | solution.py:245
  49.8 1.9 %collective-permute-start.3 = (f32[5,64,384]{2,1,0:T(8,128)S(1)}, f32[5,64,384]{2,1,0:T(8,128)S(1)}, u32[]{:S(2)}, u32[]{:S(2)}) collective-permute-start(f32[5,64,384]{2,1,0:T(8,128)S(1)} %collective-permute-done.2.refs_2_), channel_id=1, source_target_pairs={{0,8},{8,0},{1,9},{9,1},{2,10},{10,2},{3,11},{11,3},{4,12},{12,4},... | collective-permute-start | bytes 1474568 | tf_op jit(solution)/shard_map/ppermute | solution.py:247
  51.7 2.4 %collective-permute-start.5 = (f32[5,64,384]{2,1,0:T(8,128)S(1)}, f32[5,64,384]{2,1,0:T(8,128)S(1)}, u32[]{:S(2)}, u32[]{:S(2)}) collective-permute-start(f32[5,64,384]{2,1,0:T(8,128)S(1)} %collective-permute-done.4.refs_4_), channel_id=1, source_target_pairs={{0,8},{8,0},{1,9},{9,1},{2,10},{10,2},{3,11},{11,3},{4,12},{12,4},... | collective-permute-start | bytes 1474568 | tf_op jit(solution)/shard_map/ppermute | solution.py:247
  54.1 1.3 %collective-permute-done.6.refs_6_ = f32[5,64,384]{2,1,0:T(8,128)S(1)} collective-permute-done((f32[5,64,384]{2,1,0:T(8,128)S(1)}, f32[5,64,384]{2,1,0:T(8,128)S(1)}, u32[]{:S(2)}, u32[]{:S(2)}) %collective-permute-start.6) | collective-permute-done | bytes 491552 | tf_op jit(solution)/shard_map/ppermute | solution.py:245
  55.4 2.0 %collective-permute-start.7 = (f32[5,64,384]{2,1,0:T(8,128)S(1)}, f32[5,64,384]{2,1,0:T(8,128)}, u32[]{:S(2)}, u32[]{:S(2)}) collective-permute-start(f32[5,64,384]{2,1,0:T(8,128)S(1)} %collective-permute-done.6.refs_6_), channel_id=1, source_target_pairs={{0,8},{8,0},{1,9},{9,1},{2,10},{10,2},{3,11},{11,3},{4,12},{12,4},... | collective-permute-start | bytes 1474568 | tf_op jit(solution)/shard_map/ppermute | solution.py:247
  57.5 1.8 %collective-permute-done.7.refs_7_ = f32[5,64,384]{2,1,0:T(8,128)} collective-permute-done((f32[5,64,384]{2,1,0:T(8,128)S(1)}, f32[5,64,384]{2,1,0:T(8,128)}, u32[]{:S(2)}, u32[]{:S(2)}) %collective-permute-start.7) | collective-permute-done | bytes 491552 | tf_op jit(solution)/shard_map/ppermute | solution.py:247
  59.3 4.8 %all-to-all-done.1.got_ref = f32[4,672,128]{2,1,0:T(8,128)} async-done(((f32[4,672,128]{2,1,0:T(8,128)}), f32[4,672,128]{2,1,0:T(8,128)}, u32[]{:S(2)}, u32[]{:S(2)}) %all-to-all-start.1) | async-done | bytes 1376288 | tf_op jit(solution)/shard_map/all_to_all | solution.py:251
  64.2 6.2 %shard_map.82 = (f32[576,128]{1,0:T(8,128)S(1)}, f32[576,128]{1,0:T(8,128)S(1)}) custom-call(s32[1]{0:T(128)} %bitcast.4.par_ref, f32[4,672,128]{2,1,0:T(8,128)} %all-to-all-done.1.got_ref, f32[5,64,384]{2,1,0:T(8,128)S(1)} %shard_map.80.refs_0_, f32[5,64,384]{2,1,0:T(8,128)S(1)} %collective-permute-done.1.refs_1_, f32[5,64,384]{2,1,0:T(8,128)} %copy-done, ...), custom_call_target="tpu_custom_call" | custom-call | flops 1000000000 | bytes 1000 | tf_op jit(solution)/shard_map/pallas_call | solution.py:254
  70.4 2.1 %collective-permute-start.8 = (f32[576,128]{1,0:T(8,128)S(1)}, f32[576,128]{1,0:T(8,128)S(1)}, u32[]{:S(2)}, u32[]{:S(2)}) collective-permute-start(f32[576,128]{1,0:T(8,128)S(1)} %get-tuple-element.7), channel_id=1, source_target_pairs={{0,1},{1,0},{2,3},{3,2},{4,5},{5,4},{6,7},{7,6},{8,9},{9,8},{10,11... | collective-permute-start | bytes 884744 | tf_op jit(solution)/shard_map/ppermute | solution.py:265
  72.4 7.5 %collective-permute-done.8 = f32[576,128]{1,0:T(8,128)S(1)} collective-permute-done((f32[576,128]{1,0:T(8,128)S(1)}, f32[576,128]{1,0:T(8,128)S(1)}, u32[]{:S(2)}, u32[]{:S(2)}) %collective-permute-start.8) | collective-permute-done | bytes 294944 | tf_op jit(solution)/shard_map/ppermute | solution.py:265
  80.7 12.9 %all-to-all-start.2 = ((f32[32,1,2304]{2,1,0:T(1,128)}), f32[32,1,2304]{2,1,0:T(1,128)S(1)}, u32[]{:S(2)}, u32[]{:S(2)}) async-start(f32[32,1,2304]{2,1,0:T(1,128)} %bitcast.8), calls=%async_computation.2 | async-start | bytes 589824 | tf_op jit(solution)/shard_map/all_to_all | solution.py:266
  94.4 20.7 %all-to-all-done.2 = f32[32,1,2304]{2,1,0:T(1,128)S(1)} async-done(((f32[32,1,2304]{2,1,0:T(1,128)}), f32[32,1,2304]{2,1,0:T(1,128)S(1)}, u32[]{:S(2)}, u32[]{:S(2)}) %all-to-all-start.2) | async-done | bytes 294944 | tf_op jit(solution)/shard_map/all_to_all | solution.py:266
  115.1 2.2 %shard_map.83 = (f32[5,3,1152]{2,1,0:T(4,128)}, f32[5,3,1152]{2,1,0:T(4,128)}) custom-call(s32[6]{0:T(128)S(1)} %stack.23.place_ref, f32[40]{0:T(128)S(1)} %copy-done.10, f32[192]{0:T(256)S(1)} %copy-done.9, f32[576,128]{1,0:T(8,128)S(1)} %bitcast.14, f32[1,192]{1,0:T(1,128)S(1)} %bitcast.20, f32[5,3,1152]{2,1,0:T(4,128)S(1)} %bitcast.19), custom_call_target="tpu_custom_call" | custom-call | flops 1000000000 | bytes 1000 | tf_op jit(solution)/shard_map/pallas_call | solution.py:269
  (31 shorter events, 1.8 us)
Async XLA Ops:
  0.6 20.6 %copy-start.5 = (f32[3,5,7680]{2,0,1:T(4,128)S(1)}, f32[3,5,7680]{2,0,1:T(4,128)}, u32[]{:S(2)}) copy-start(f32[3,5,7680]{2,0,1:T(4,128)} %param.7) | copy-start | bytes 1382404
  0.6 32.3 %collective-permute-start = (f32[5,3,1152]{2,1,0:T(4,128)}, f32[5,3,1152]{2,1,0:T(4,128)S(1)}, u32[]{:S(2)}, u32[]{:S(2)}) collective-permute-start(f32[5,3,1152]{2,1,0:T(4,128)} %bitcast.16), channel_id=1, source_target_pairs={{0,16},{16,0},{1,17},{17,1},{2,18},{18,2},{3,19},{19,3},{4,20},{20... | collective-permute-start | bytes 207368 | tf_op jit(solution)/shard_map/ppermute | solution.py:241
  14.7 0.9 copy-start.6
  16.8 23.0 %all-to-all-start = ((f32[16,24,128]{2,1,0:T(8,128)}), f32[16,24,128]{2,1,0:T(8,128)S(1)}, u32[]{:S(2)}, u32[]{:S(2)}) async-start(f32[16,24,128]{2,1,0:T(8,128)} %shard_map.78.token_ref), calls=%async_computation | async-start | bytes 393216 | tf_op jit(solution)/shard_map/all_to_all | solution.py:248
  21.2 11.8 %copy-start.7 = (f32[3,5,1152]{2,0,1:T(4,128)S(1)}, f32[3,5,1152]{2,0,1:T(4,128)}, u32[]{:S(2)}) copy-start(f32[3,5,1152]{2,0,1:T(4,128)} %param.6) | copy-start | bytes 207364
  22.4 27.4 %collective-permute-start.2 = (f32[5,64,384]{2,1,0:T(8,128)S(1)}, f32[5,64,384]{2,1,0:T(8,128)S(1)}, u32[]{:S(2)}, u32[]{:S(2)}) collective-permute-start(f32[5,64,384]{2,1,0:T(8,128)S(1)} %shard_map.80.refs_0_), channel_id=1, source_target_pairs={{0,384},{128,0},{256,128},{384,256},{1,385},{129,1},{257,129},{385... | collective-permute-start | bytes 1474568 | tf_op jit(solution)/shard_map/ppermute | solution.py:245
  27.4 24.3 %collective-permute-start.4 = (f32[5,64,384]{2,1,0:T(8,128)S(1)}, f32[5,64,384]{2,1,0:T(8,128)S(1)}, u32[]{:S(2)}, u32[]{:S(2)}) collective-permute-start(f32[5,64,384]{2,1,0:T(8,128)S(1)} %shard_map.80.refs_0_), channel_id=1, source_target_pairs={{0,256},{128,384},{256,0},{384,128},{1,257},{129,385},{257,1},{385... | collective-permute-start | bytes 1474568 | tf_op jit(solution)/shard_map/ppermute | solution.py:245
  30.2 25.2 %collective-permute-start.6 = (f32[5,64,384]{2,1,0:T(8,128)S(1)}, f32[5,64,384]{2,1,0:T(8,128)S(1)}, u32[]{:S(2)}, u32[]{:S(2)}) collective-permute-start(f32[5,64,384]{2,1,0:T(8,128)S(1)} %shard_map.80.refs_0_), channel_id=1, source_target_pairs={{0,128},{128,256},{256,384},{384,0},{1,129},{129,257},{257,385},{3... | collective-permute-start | bytes 1474568 | tf_op jit(solution)/shard_map/ppermute | solution.py:245
  41.0 23.2 %all-to-all-start.1 = ((f32[4,672,128]{2,1,0:T(8,128)}), f32[4,672,128]{2,1,0:T(8,128)}, u32[]{:S(2)}, u32[]{:S(2)}) async-start(f32[4,672,128]{2,1,0:T(8,128)} %shard_map.79), calls=%async_computation.1 | async-start | bytes 2752512 | tf_op jit(solution)/shard_map/all_to_all | solution.py:251
  45.4 12.0 %collective-permute-start.1 = (f32[5,64,384]{2,1,0:T(8,128)S(1)}, f32[5,64,384]{2,1,0:T(8,128)S(1)}, u32[]{:S(2)}, u32[]{:S(2)}) collective-permute-start(f32[5,64,384]{2,1,0:T(8,128)S(1)} %shard_map.80.refs_0_), channel_id=1, source_target_pairs={{0,8},{8,0},{1,9},{9,1},{2,10},{10,2},{3,11},{11,3},{4,12},{12,4},... | collective-permute-start | bytes 1474568 | tf_op jit(solution)/shard_map/ppermute | solution.py:247
  49.8 9.5 %copy-start = (f32[5,64,384]{2,1,0:T(8,128)}, f32[5,64,384]{2,1,0:T(8,128)S(1)}, u32[]{:S(2)}) copy-start(f32[5,64,384]{2,1,0:T(8,128)S(1)} %collective-permute-done.2.refs_2_) | copy-start | bytes 1474564
  49.8 7.7 %collective-permute-start.3 = (f32[5,64,384]{2,1,0:T(8,128)S(1)}, f32[5,64,384]{2,1,0:T(8,128)S(1)}, u32[]{:S(2)}, u32[]{:S(2)}) collective-permute-start(f32[5,64,384]{2,1,0:T(8,128)S(1)} %collective-permute-done.2.refs_2_), channel_id=1, source_target_pairs={{0,8},{8,0},{1,9},{9,1},{2,10},{10,2},{3,11},{11,3},{4,12},{12,4},... | collective-permute-start | bytes 1474568 | tf_op jit(solution)/shard_map/ppermute | solution.py:247
  51.7 7.6 %copy-start.1 = (f32[5,64,384]{2,1,0:T(8,128)}, f32[5,64,384]{2,1,0:T(8,128)S(1)}, u32[]{:S(2)}) copy-start(f32[5,64,384]{2,1,0:T(8,128)S(1)} %collective-permute-done.4.refs_4_) | copy-start | bytes 1474564
  51.7 5.8 %collective-permute-start.5 = (f32[5,64,384]{2,1,0:T(8,128)S(1)}, f32[5,64,384]{2,1,0:T(8,128)S(1)}, u32[]{:S(2)}, u32[]{:S(2)}) collective-permute-start(f32[5,64,384]{2,1,0:T(8,128)S(1)} %collective-permute-done.4.refs_4_), channel_id=1, source_target_pairs={{0,8},{8,0},{1,9},{9,1},{2,10},{10,2},{3,11},{11,3},{4,12},{12,4},... | collective-permute-start | bytes 1474568 | tf_op jit(solution)/shard_map/ppermute | solution.py:247
  55.4 3.9 %copy-start.2 = (f32[5,64,384]{2,1,0:T(8,128)}, f32[5,64,384]{2,1,0:T(8,128)S(1)}, u32[]{:S(2)}) copy-start(f32[5,64,384]{2,1,0:T(8,128)S(1)} %collective-permute-done.6.refs_6_) | copy-start | bytes 1474564
  55.4 3.9 %collective-permute-start.7 = (f32[5,64,384]{2,1,0:T(8,128)S(1)}, f32[5,64,384]{2,1,0:T(8,128)}, u32[]{:S(2)}, u32[]{:S(2)}) collective-permute-start(f32[5,64,384]{2,1,0:T(8,128)S(1)} %collective-permute-done.6.refs_6_), channel_id=1, source_target_pairs={{0,8},{8,0},{1,9},{9,1},{2,10},{10,2},{3,11},{11,3},{4,12},{12,4},... | collective-permute-start | bytes 1474568 | tf_op jit(solution)/shard_map/ppermute | solution.py:247
  57.5 1.8 %copy-start.3 = (f32[5,64,384]{2,1,0:T(8,128)}, f32[5,64,384]{2,1,0:T(8,128)S(1)}, u32[]{:S(2)}) copy-start(f32[5,64,384]{2,1,0:T(8,128)S(1)} %collective-permute-done.3.refs_3_) | copy-start | bytes 1474564
  57.5 1.8 %copy-start.4 = (f32[5,64,384]{2,1,0:T(8,128)}, f32[5,64,384]{2,1,0:T(8,128)S(1)}, u32[]{:S(2)}) copy-start(f32[5,64,384]{2,1,0:T(8,128)S(1)} %collective-permute-done.5.refs_5_) | copy-start | bytes 1474564
  70.3 44.7 %copy-start.8 = (f32[3,5,1152]{2,0,1:T(4,128)S(1)}, f32[3,5,1152]{2,0,1:T(4,128)}, u32[]{:S(2)}) copy-start(f32[3,5,1152]{2,0,1:T(4,128)} %param.8) | copy-start | bytes 207364
  70.4 44.7 %copy-start.9 = (f32[192]{0:T(256)S(1)}, f32[192]{0:T(256)}, u32[]{:S(2)}) copy-start(f32[192]{0:T(256)} %va_ref.1) | copy-start | bytes 2308
  70.4 44.7 %copy-start.10 = (f32[40]{0:T(128)S(1)}, f32[40]{0:T(128)}, u32[]{:S(2)}) copy-start(f32[40]{0:T(128)} %occ_ref.1) | copy-start | bytes 484
  70.4 9.6 %collective-permute-start.8 = (f32[576,128]{1,0:T(8,128)S(1)}, f32[576,128]{1,0:T(8,128)S(1)}, u32[]{:S(2)}, u32[]{:S(2)}) collective-permute-start(f32[576,128]{1,0:T(8,128)S(1)} %get-tuple-element.7), channel_id=1, source_target_pairs={{0,1},{1,0},{2,3},{3,2},{4,5},{5,4},{6,7},{7,6},{8,9},{9,8},{10,11... | collective-permute-start | bytes 884744 | tf_op jit(solution)/shard_map/ppermute | solution.py:265
  80.7 34.3 %all-to-all-start.2 = ((f32[32,1,2304]{2,1,0:T(1,128)}), f32[32,1,2304]{2,1,0:T(1,128)S(1)}, u32[]{:S(2)}, u32[]{:S(2)}) async-start(f32[32,1,2304]{2,1,0:T(1,128)} %bitcast.8), calls=%async_computation.2 | async-start | bytes 589824 | tf_op jit(solution)/shard_map/all_to_all | solution.py:266

commit v7 on v6

--- a/solution.py
+++ b/solution.py
@@ -27,10 +27,12 @@
 
 
 def order_matrix(e):
-    n = index((1, 512), 1)
-    v = ((n >> 5) & 3) * 48 + (n >> 7) * 12 + ((n >> 4) & 1) * 6 + ((n >> 3) & 1) * 3 + (n & 3)
-    v = jnp.where(((n & 3) < 3) & (((n >> 2) & 1) == e), v, -1)
-    return hot(index((256, 512), 0) == v)
+    n = index((1, 384), 1)
+    source = (n * 10923) >> 16
+    m = n - source * 6 - e * 3
+    v = ((source >> 2) & 3) * 48 + (source >> 4) * 12 + ((source >> 1) & 1) * 6 + (source & 1) * 3 + m
+    v = jnp.where((m >= 0) & (m < 3), v, -1)
+    return hot(index((256, 384), 0) == v)
 
 
 def choose_matrix():
@@ -96,9 +98,9 @@
     for k in range(5):
         for p in range(3):
             v = own_ref[k, :, p * 384:(p + 1) * 384]
-            at = k * 24 + p * 8
+            at = k * 24 + p * 6
             rows[at:at + 3, :] = v[:, :256]
-            rows[at + 4:at + 7, :] = pltpu.roll(v[:, 128:], 192, 1)
+            rows[at + 3:at + 6, :] = pltpu.roll(v[:, 128:], 192, 1)
     chosen = moved(rows[...], choose_matrix())
     lane = index((24, 128), 1)
     for n in range(8):
@@ -127,7 +129,8 @@
 def pack_kernel(one_ref, two_ref, out_ref):
     for y in range(4):
         out_ref[y, :288, :] = one_ref[...]
-        out_ref[y, 288:, :] = two_ref[...].reshape(384, 128)
+        for n in range(16):
+            out_ref[y, 288 + n * 18:306 + n * 18, :] = two_ref[n, :18, :]
 
 
 def mark_kernel(*refs):
@@ -136,14 +139,16 @@
 
 def product_kernel(par_ref, got_ref, *refs):
     away, (keep_ref, send_ref) = refs[:8], refs[9:11]
-    two_high, two_low, swapped, whole, mixed, weights, arrived = refs[11:]
+    two_high, two_low, stage, swapped, whole, mixed, weights, arrived = refs[11:]
     copies = [pltpu.make_async_copy(away[n], weights.at[n], arrived.at[n]) for n in range(8)]
     for copy in copies:
         copy.start()
     for p in range(3):
-        starts = [288 + s * 24 + p * 8 for s in range(16)]
-        part = jnp.concatenate([got_ref[y, at:at + 8, :] for y in range(4) for at in starts], 0)
-        high, low = split2(part)
+        for y in range(4):
+            for n in range(16):
+                at = 288 + n * 18 + p * 6
+                stage[y * 96 + n * 6:y * 96 + n * 6 + 6, :] = got_ref[y, at:at + 6, :]
+        high, low = split2(stage[...])
         two_high[:, p * 128:(p + 1) * 128] = high
         two_low[:, p * 128:(p + 1) * 128] = low
     turn = turn_matrix()
@@ -220,7 +225,7 @@
         inc_ref[j] = new / (den[...] - occ_ref[place_ref[3] + j])
 
 
-def call(kernel, n_smem, n_vmem, outs, scratch, mib=8, dtype=F32, cost=1, space=pltpu.VMEM):
+def call(kernel, n_smem, n_vmem, outs, scratch, mib=8, dtype=F32, cost=1000, space=pltpu.VMEM):
     shapes = [jax.ShapeDtypeStruct(s, dtype) for s in outs]
     return pl.pallas_call(
         kernel,
@@ -228,7 +233,7 @@
         in_specs=[SMEM] * n_smem + [pl.BlockSpec(memory_space=space)] * n_vmem,
         out_specs=[VMEM] * len(shapes) if len(shapes) > 1 else VMEM,
         scratch_shapes=scratch,
-        cost_estimate=pl.CostEstimate(flops=cost * 10**9, bytes_accessed=1000, transcendentals=0),
+        cost_estimate=pl.CostEstimate(flops=cost * 10**6, bytes_accessed=1000, transcendentals=0),
         compiler_params=pltpu.CompilerParams(vmem_limit_bytes=mib * 1024 * 1024),
     )
 
@@ -242,21 +247,22 @@
     two = call(swap_kernel, 0, 1, [(16, 24, 128)], [pltpu.VMEM((120, 256), F32)])(amps)
     weights = call(weights_kernel, 0, 2, [(5, 64, 384)], [])(ints, two)
     along = [weights] + [
-        lax.ppermute(weights, "x", [(s, (s - d) % 4) for s in range(4)]) for d in (1, 2, 3)
+        lax.ppermute(weights, "x", [(s, (s - d) % 4) for s in range(4)]) for d in (1, 3, 2)
     ]
     across = [lax.ppermute(w, "core", [(0, 1), (1, 0)]) for w in along]
     two = lax.all_to_all(two, ("x", "zh", "core"), 0, 0, tiled=True)
-    one = call(merge_kernel, 1, 2, [(288, 128)], [pltpu.VMEM((96, 384), F32)], cost=8)(zh.reshape(1), amps, other)
-    both = call(pack_kernel, 0, 2, [(4, 672, 128)], [])(one, two)
+    one = call(merge_kernel, 1, 2, [(288, 128)], [pltpu.VMEM((96, 384), F32)], cost=8000)(zh.reshape(1), amps, other)
+    both = call(pack_kernel, 0, 2, [(4, 576, 128)], [])(one, two)
     both = lax.all_to_all(both, "y", 0, 0, tiled=True)
     ordered = [w for pair in zip(along, across) for w in pair]
-    mark = call(mark_kernel, 0, 8, [(8, 128)], [], 8, F32, 1, pl.ANY)(*ordered)
+    ordered = ordered[:4] + ordered[6:] + ordered[4:6]
+    mark = call(mark_kernel, 0, 8, [(8, 128)], [], 8, F32, 1000, pl.ANY)(*ordered)
     keep, send = pl.pallas_call(
         product_kernel,
         out_shape=[jax.ShapeDtypeStruct((576, 128), F32)] * 2,
         in_specs=[SMEM, VMEM] + [pl.BlockSpec(memory_space=pl.ANY)] * 9,
         out_specs=[VMEM] * 2,
-        scratch_shapes=[pltpu.VMEM((512, 384), BF16)] * 2
+        scratch_shapes=[pltpu.VMEM((384, 384), BF16)] * 2 + [pltpu.VMEM((384, 128), F32)]
         + [pltpu.VMEM((2, 480, 256), F32), pltpu.VMEM((192, 256), F32), pltpu.VMEM((5, 384, 256), BF16)]
         + [pltpu.VMEM((8, 5, 64, 384), F32), pltpu.SemaphoreType.DMA((8,))],
         cost_estimate=pl.CostEstimate(flops=10**9, bytes_accessed=1000, transcendentals=0),

time: 118 us -> 118 us (level)
    all_to_all x1, waiting for transfers between devices: 4.85 us -> 2.62 us  [body(): both = lax.all_to_all(both, 'y', 0, 0, tiled=True)]
    all_to_all x1, waiting for transfers between devices: 20.7 us -> 22.2 us  [body(): lax.all_to_all(half.reshape(32, 1, 2304), ('y', 'zh', 'pair'), 0, 0, tile...]
where the time goes in v7:
time: 118 us; the launch traced here: 117 us
  starting transfers between devices  57.4 us (49%)
  waiting for transfers between devices  44.6 us (38%)
  Pallas kernels  11.7 us (10%)
  between operations  1.57 us (1%)
    all_to_all x1, waiting for transfers between devices, body(): lax.all_to_all(half.reshape(32, 1, 2304), ('y', 'zh', 'pair'), 0, 0, tile...  22.2 us
    ppermute x1, starting transfers between devices, body(): other = lax.ppermute(amps, 'zh', [(0, 1), (1, 0)])  14.1 us
    all_to_all x1, starting transfers between devices, body(): lax.all_to_all(half.reshape(32, 1, 2304), ('y', 'zh', 'pair'), 0, 0, tile...  13.6 us
    ppermute x3, starting transfers between devices, body(): lax.ppermute(weights, 'x', [(s, (s - d) % 4) for s in range(4)])  10.6 us
    ppermute x4, starting transfers between devices, body(): across = [lax.ppermute(w, 'core', [(0, 1), (1, 0)]) for w in along]  8.24 us
    ppermute x1, waiting for transfers between devices, body(): half = keep + lax.ppermute(send, 'par', [(0, 1), (1, 0)])  7.49 us
    all_to_all x1, waiting for transfers between devices, body(): two = lax.all_to_all(two, ('x', 'zh', 'core'), 0, 0, tiled=True)  6.73 us
    pallas_call x1, Pallas kernels, body(): pl.pallas_call(product_kernel, out_shape=[jax.ShapeDtypeStruct((576, 128)...  6.05 us
  transfers between devices with their start and end apart: 12, of which 7 were waited for; matrix products, arithmetic and copies ran while one was open for 0% of the time, Pallas kernels for 3%

profile of v7, /device:TPU:64, one launch (start us, length us, event | category | flops | bytes accessed | tf_op | source)
XLA Modules:
  0.0 117.0 jit_solution(11835422852648105839)
XLA Ops:
  0.6 14.1 %collective-permute-start = (f32[5,3,1152]{2,1,0:T(4,128)}, f32[5,3,1152]{2,1,0:T(4,128)S(1)}, u32[]{:S(2)}, u32[]{:S(2)}) collective-permute-start(f32[5,3,1152]{2,1,0:T(4,128)} %bitcast.16), channel_id=1, source_target_pairs={{0,16},{16,0},{1,17},{17,1},{2,18},{18,2},{3,19},{19,3},{4,20},{20... | collective-permute-start | bytes 207368 | tf_op jit(solution)/shard_map/ppermute | solution.py:246
  15.6 1.2 %shard_map.78.token_ref = f32[16,24,128]{2,1,0:T(8,128)} custom-call(f32[5,3,1152]{2,1,0:T(4,128)S(1)} %bitcast.17), custom_call_target="tpu_custom_call" | custom-call | flops 1000000000 | bytes 1000 | tf_op jit(solution)/shard_map/pallas_call | solution.py:247
  16.8 4.4 %all-to-all-start = ((f32[16,24,128]{2,1,0:T(8,128)}), f32[16,24,128]{2,1,0:T(8,128)S(1)}, u32[]{:S(2)}, u32[]{:S(2)}) async-start(f32[16,24,128]{2,1,0:T(8,128)} %shard_map.78.token_ref), calls=%async_computation | async-start | bytes 393216 | tf_op jit(solution)/shard_map/all_to_all | solution.py:253
  21.3 1.1 shard_map.80.refs_0_
  22.4 5.1 %collective-permute-start.2 = (f32[5,64,384]{2,1,0:T(8,128)S(1)}, f32[5,64,384]{2,1,0:T(8,128)S(1)}, u32[]{:S(2)}, u32[]{:S(2)}) collective-permute-start(f32[5,64,384]{2,1,0:T(8,128)S(1)} %shard_map.80.refs_0_), channel_id=1, source_target_pairs={{0,384},{128,0},{256,128},{384,256},{1,385},{129,1},{257,129},{385... | collective-permute-start | bytes 1474568 | tf_op jit(solution)/shard_map/ppermute | solution.py:250
  27.4 2.8 %collective-permute-start.4 = (f32[5,64,384]{2,1,0:T(8,128)S(1)}, f32[5,64,384]{2,1,0:T(8,128)S(1)}, u32[]{:S(2)}, u32[]{:S(2)}) collective-permute-start(f32[5,64,384]{2,1,0:T(8,128)S(1)} %shard_map.80.refs_0_), channel_id=1, source_target_pairs={{0,256},{128,384},{256,0},{384,128},{1,257},{129,385},{257,1},{385... | collective-permute-start | bytes 1474568 | tf_op jit(solution)/shard_map/ppermute | solution.py:250
  30.2 2.8 %collective-permute-start.6 = (f32[5,64,384]{2,1,0:T(8,128)S(1)}, f32[5,64,384]{2,1,0:T(8,128)S(1)}, u32[]{:S(2)}, u32[]{:S(2)}) collective-permute-start(f32[5,64,384]{2,1,0:T(8,128)S(1)} %shard_map.80.refs_0_), channel_id=1, source_target_pairs={{0,128},{128,256},{256,384},{384,0},{1,129},{129,257},{257,385},{3... | collective-permute-start | bytes 1474568 | tf_op jit(solution)/shard_map/ppermute | solution.py:250
  33.1 6.7 %all-to-all-done.two_ref = f32[16,24,128]{2,1,0:T(8,128)S(1)} async-done(((f32[16,24,128]{2,1,0:T(8,128)}), f32[16,24,128]{2,1,0:T(8,128)S(1)}, u32[]{:S(2)}, u32[]{:S(2)}) %all-to-all-start) | async-done | bytes 196640 | tf_op jit(solution)/shard_map/all_to_all | solution.py:253
  39.8 1.1 shard_map.79
  40.9 4.5 %all-to-all-start.1 = ((f32[4,576,128]{2,1,0:T(8,128)}), f32[4,576,128]{2,1,0:T(8,128)}, u32[]{:S(2)}, u32[]{:S(2)}) async-start(f32[4,576,128]{2,1,0:T(8,128)} %shard_map.79), calls=%async_computation.1 | async-start | bytes 2359296 | tf_op jit(solution)/shard_map/all_to_all | solution.py:256
  45.4 1.9 %collective-permute-start.1 = (f32[5,64,384]{2,1,0:T(8,128)S(1)}, f32[5,64,384]{2,1,0:T(8,128)S(1)}, u32[]{:S(2)}, u32[]{:S(2)}) collective-permute-start(f32[5,64,384]{2,1,0:T(8,128)S(1)} %shard_map.80.refs_0_), channel_id=1, source_target_pairs={{0,8},{8,0},{1,9},{9,1},{2,10},{10,2},{3,11},{11,3},{4,12},{12,4},... | collective-permute-start | bytes 1474568 | tf_op jit(solution)/shard_map/ppermute | solution.py:252
  47.3 2.5 %collective-permute-done.2.refs_2_ = f32[5,64,384]{2,1,0:T(8,128)S(1)} collective-permute-done((f32[5,64,384]{2,1,0:T(8,128)S(1)}, f32[5,64,384]{2,1,0:T(8,128)S(1)}, u32[]{:S(2)}, u32[]{:S(2)}) %collective-permute-start.2) | collective-permute-done | bytes 491552 | tf_op jit(solution)/shard_map/ppermute | solution.py:250
  49.8 1.9 %collective-permute-start.3 = (f32[5,64,384]{2,1,0:T(8,128)S(1)}, f32[5,64,384]{2,1,0:T(8,128)S(1)}, u32[]{:S(2)}, u32[]{:S(2)}) collective-permute-start(f32[5,64,384]{2,1,0:T(8,128)S(1)} %collective-permute-done.2.refs_2_), channel_id=1, source_target_pairs={{0,8},{8,0},{1,9},{9,1},{2,10},{10,2},{3,11},{11,3},{4,12},{12,4},... | collective-permute-start | bytes 1474568 | tf_op jit(solution)/shard_map/ppermute | solution.py:252
  51.7 2.4 %collective-permute-start.5 = (f32[5,64,384]{2,1,0:T(8,128)S(1)}, f32[5,64,384]{2,1,0:T(8,128)S(1)}, u32[]{:S(2)}, u32[]{:S(2)}) collective-permute-start(f32[5,64,384]{2,1,0:T(8,128)S(1)} %collective-permute-done.4.refs_4_), channel_id=1, source_target_pairs={{0,8},{8,0},{1,9},{9,1},{2,10},{10,2},{3,11},{11,3},{4,12},{12,4},... | collective-permute-start | bytes 1474568 | tf_op jit(solution)/shard_map/ppermute | solution.py:252
  54.2 1.3 %collective-permute-done.6.refs_6_ = f32[5,64,384]{2,1,0:T(8,128)S(1)} collective-permute-done((f32[5,64,384]{2,1,0:T(8,128)S(1)}, f32[5,64,384]{2,1,0:T(8,128)S(1)}, u32[]{:S(2)}, u32[]{:S(2)}) %collective-permute-start.6) | collective-permute-done | bytes 491552 | tf_op jit(solution)/shard_map/ppermute | solution.py:250
  55.4 2.0 %collective-permute-start.7 = (f32[5,64,384]{2,1,0:T(8,128)S(1)}, f32[5,64,384]{2,1,0:T(8,128)}, u32[]{:S(2)}, u32[]{:S(2)}) collective-permute-start(f32[5,64,384]{2,1,0:T(8,128)S(1)} %collective-permute-done.6.refs_6_), channel_id=1, source_target_pairs={{0,8},{8,0},{1,9},{9,1},{2,10},{10,2},{3,11},{11,3},{4,12},{12,4},... | collective-permute-start | bytes 1474568 | tf_op jit(solution)/shard_map/ppermute | solution.py:252
  57.5 1.8 %collective-permute-done.7.refs_7_ = f32[5,64,384]{2,1,0:T(8,128)} collective-permute-done((f32[5,64,384]{2,1,0:T(8,128)S(1)}, f32[5,64,384]{2,1,0:T(8,128)}, u32[]{:S(2)}, u32[]{:S(2)}) %collective-permute-start.7) | collective-permute-done | bytes 491552 | tf_op jit(solution)/shard_map/ppermute | solution.py:252
  59.3 2.6 %all-to-all-done.1.got_ref = f32[4,576,128]{2,1,0:T(8,128)} async-done(((f32[4,576,128]{2,1,0:T(8,128)}), f32[4,576,128]{2,1,0:T(8,128)}, u32[]{:S(2)}, u32[]{:S(2)}) %all-to-all-start.1) | async-done | bytes 1179680 | tf_op jit(solution)/shard_map/all_to_all | solution.py:256
  62.0 6.0 %shard_map.82 = (f32[576,128]{1,0:T(8,128)S(1)}, f32[576,128]{1,0:T(8,128)S(1)}) custom-call(s32[1]{0:T(128)} %bitcast.4.par_ref, f32[4,576,128]{2,1,0:T(8,128)} %all-to-all-done.1.got_ref, f32[5,64,384]{2,1,0:T(8,128)S(1)} %shard_map.80.refs_0_, f32[5,64,384]{2,1,0:T(8,128)S(1)} %collective-permute-done.1.refs_1_, f32[5,64,384]{2,1,0:T(8,128)} %copy-done, ...), custom_call_target="tpu_custom_call" | custom-call | flops 1000000000 | bytes 1000 | tf_op jit(solution)/shard_map/pallas_call | solution.py:260
  68.0 2.1 %collective-permute-start.8 = (f32[576,128]{1,0:T(8,128)S(1)}, f32[576,128]{1,0:T(8,128)S(1)}, u32[]{:S(2)}, u32[]{:S(2)}) collective-permute-start(f32[576,128]{1,0:T(8,128)S(1)} %get-tuple-element.7), channel_id=1, source_target_pairs={{0,1},{1,0},{2,3},{3,2},{4,5},{5,4},{6,7},{7,6},{8,9},{9,8},{10,11... | collective-permute-start | bytes 884744 | tf_op jit(solution)/shard_map/ppermute | solution.py:271
  70.1 7.5 %collective-permute-done.8 = f32[576,128]{1,0:T(8,128)S(1)} collective-permute-done((f32[576,128]{1,0:T(8,128)S(1)}, f32[576,128]{1,0:T(8,128)S(1)}, u32[]{:S(2)}, u32[]{:S(2)}) %collective-permute-start.8) | collective-permute-done | bytes 294944 | tf_op jit(solution)/shard_map/ppermute | solution.py:271
  78.3 13.6 %all-to-all-start.2 = ((f32[32,1,2304]{2,1,0:T(1,128)}), f32[32,1,2304]{2,1,0:T(1,128)S(1)}, u32[]{:S(2)}, u32[]{:S(2)}) async-start(f32[32,1,2304]{2,1,0:T(1,128)} %bitcast.8), calls=%async_computation.2 | async-start | bytes 589824 | tf_op jit(solution)/shard_map/all_to_all | solution.py:272
  92.7 22.2 %all-to-all-done.2 = f32[32,1,2304]{2,1,0:T(1,128)S(1)} async-done(((f32[32,1,2304]{2,1,0:T(1,128)}), f32[32,1,2304]{2,1,0:T(1,128)S(1)}, u32[]{:S(2)}, u32[]{:S(2)}) %all-to-all-start.2) | async-done | bytes 294944 | tf_op jit(solution)/shard_map/all_to_all | solution.py:272
  114.9 2.2 %shard_map.83 = (f32[5,3,1152]{2,1,0:T(4,128)}, f32[5,3,1152]{2,1,0:T(4,128)}) custom-call(s32[6]{0:T(128)S(1)} %stack.23.place_ref, f32[40]{0:T(128)S(1)} %copy-done.10, f32[192]{0:T(256)S(1)} %copy-done.9, f32[576,128]{1,0:T(8,128)S(1)} %bitcast.14, f32[1,192]{1,0:T(1,128)S(1)} %bitcast.20, f32[5,3,1152]{2,1,0:T(4,128)S(1)} %bitcast.19), custom_call_target="tpu_custom_call" | custom-call | flops 1000000000 | bytes 1000 | tf_op jit(solution)/shard_map/pallas_call | solution.py:275
  (31 shorter events, 1.8 us)
Async XLA Ops:
  0.6 20.6 %copy-start.5 = (f32[3,5,7680]{2,0,1:T(4,128)S(1)}, f32[3,5,7680]{2,0,1:T(4,128)}, u32[]{:S(2)}) copy-start(f32[3,5,7680]{2,0,1:T(4,128)} %param.7) | copy-start | bytes 1382404
  0.6 32.4 %collective-permute-start = (f32[5,3,1152]{2,1,0:T(4,128)}, f32[5,3,1152]{2,1,0:T(4,128)S(1)}, u32[]{:S(2)}, u32[]{:S(2)}) collective-permute-start(f32[5,3,1152]{2,1,0:T(4,128)} %bitcast.16), channel_id=1, source_target_pairs={{0,16},{16,0},{1,17},{17,1},{2,18},{18,2},{3,19},{19,3},{4,20},{20... | collective-permute-start | bytes 207368 | tf_op jit(solution)/shard_map/ppermute | solution.py:246
  14.7 0.9 copy-start.6
  16.8 23.0 %all-to-all-start = ((f32[16,24,128]{2,1,0:T(8,128)}), f32[16,24,128]{2,1,0:T(8,128)S(1)}, u32[]{:S(2)}, u32[]{:S(2)}) async-start(f32[16,24,128]{2,1,0:T(8,128)} %shard_map.78.token_ref), calls=%async_computation | async-start | bytes 393216 | tf_op jit(solution)/shard_map/all_to_all | solution.py:253
  21.3 11.8 %copy-start.7 = (f32[3,5,1152]{2,0,1:T(4,128)S(1)}, f32[3,5,1152]{2,0,1:T(4,128)}, u32[]{:S(2)}) copy-start(f32[3,5,1152]{2,0,1:T(4,128)} %param.6) | copy-start | bytes 207364
  22.4 27.4 %collective-permute-start.2 = (f32[5,64,384]{2,1,0:T(8,128)S(1)}, f32[5,64,384]{2,1,0:T(8,128)S(1)}, u32[]{:S(2)}, u32[]{:S(2)}) collective-permute-start(f32[5,64,384]{2,1,0:T(8,128)S(1)} %shard_map.80.refs_0_), channel_id=1, source_target_pairs={{0,384},{128,0},{256,128},{384,256},{1,385},{129,1},{257,129},{385... | collective-permute-start | bytes 1474568 | tf_op jit(solution)/shard_map/ppermute | solution.py:250
  27.4 24.3 %collective-permute-start.4 = (f32[5,64,384]{2,1,0:T(8,128)S(1)}, f32[5,64,384]{2,1,0:T(8,128)S(1)}, u32[]{:S(2)}, u32[]{:S(2)}) collective-permute-start(f32[5,64,384]{2,1,0:T(8,128)S(1)} %shard_map.80.refs_0_), channel_id=1, source_target_pairs={{0,256},{128,384},{256,0},{384,128},{1,257},{129,385},{257,1},{385... | collective-permute-start | bytes 1474568 | tf_op jit(solution)/shard_map/ppermute | solution.py:250
  30.2 25.2 %collective-permute-start.6 = (f32[5,64,384]{2,1,0:T(8,128)S(1)}, f32[5,64,384]{2,1,0:T(8,128)S(1)}, u32[]{:S(2)}, u32[]{:S(2)}) collective-permute-start(f32[5,64,384]{2,1,0:T(8,128)S(1)} %shard_map.80.refs_0_), channel_id=1, source_target_pairs={{0,128},{128,256},{256,384},{384,0},{1,129},{129,257},{257,385},{3... | collective-permute-start | bytes 1474568 | tf_op jit(solution)/shard_map/ppermute | solution.py:250
  40.9 21.0 %all-to-all-start.1 = ((f32[4,576,128]{2,1,0:T(8,128)}), f32[4,576,128]{2,1,0:T(8,128)}, u32[]{:S(2)}, u32[]{:S(2)}) async-start(f32[4,576,128]{2,1,0:T(8,128)} %shard_map.79), calls=%async_computation.1 | async-start | bytes 2359296 | tf_op jit(solution)/shard_map/all_to_all | solution.py:256
  45.4 12.1 %collective-permute-start.1 = (f32[5,64,384]{2,1,0:T(8,128)S(1)}, f32[5,64,384]{2,1,0:T(8,128)S(1)}, u32[]{:S(2)}, u32[]{:S(2)}) collective-permute-start(f32[5,64,384]{2,1,0:T(8,128)S(1)} %shard_map.80.refs_0_), channel_id=1, source_target_pairs={{0,8},{8,0},{1,9},{9,1},{2,10},{10,2},{3,11},{11,3},{4,12},{12,4},... | collective-permute-start | bytes 1474568 | tf_op jit(solution)/shard_map/ppermute | solution.py:252
  49.8 9.5 %copy-start = (f32[5,64,384]{2,1,0:T(8,128)}, f32[5,64,384]{2,1,0:T(8,128)S(1)}, u32[]{:S(2)}) copy-start(f32[5,64,384]{2,1,0:T(8,128)S(1)} %collective-permute-done.2.refs_2_) | copy-start | bytes 1474564
  49.8 7.7 %collective-permute-start.3 = (f32[5,64,384]{2,1,0:T(8,128)S(1)}, f32[5,64,384]{2,1,0:T(8,128)S(1)}, u32[]{:S(2)}, u32[]{:S(2)}) collective-permute-start(f32[5,64,384]{2,1,0:T(8,128)S(1)} %collective-permute-done.2.refs_2_), channel_id=1, source_target_pairs={{0,8},{8,0},{1,9},{9,1},{2,10},{10,2},{3,11},{11,3},{4,12},{12,4},... | collective-permute-start | bytes 1474568 | tf_op jit(solution)/shard_map/ppermute | solution.py:252
  51.7 7.6 %copy-start.1 = (f32[5,64,384]{2,1,0:T(8,128)}, f32[5,64,384]{2,1,0:T(8,128)S(1)}, u32[]{:S(2)}) copy-start(f32[5,64,384]{2,1,0:T(8,128)S(1)} %collective-permute-done.4.refs_4_) | copy-start | bytes 1474564
  51.7 5.8 %collective-permute-start.5 = (f32[5,64,384]{2,1,0:T(8,128)S(1)}, f32[5,64,384]{2,1,0:T(8,128)S(1)}, u32[]{:S(2)}, u32[]{:S(2)}) collective-permute-start(f32[5,64,384]{2,1,0:T(8,128)S(1)} %collective-permute-done.4.refs_4_), channel_id=1, source_target_pairs={{0,8},{8,0},{1,9},{9,1},{2,10},{10,2},{3,11},{11,3},{4,12},{12,4},... | collective-permute-start | bytes 1474568 | tf_op jit(solution)/shard_map/ppermute | solution.py:252
  55.4 3.9 %copy-start.2 = (f32[5,64,384]{2,1,0:T(8,128)}, f32[5,64,384]{2,1,0:T(8,128)S(1)}, u32[]{:S(2)}) copy-start(f32[5,64,384]{2,1,0:T(8,128)S(1)} %collective-permute-done.6.refs_6_) | copy-start | bytes 1474564
  55.4 3.9 %collective-permute-start.7 = (f32[5,64,384]{2,1,0:T(8,128)S(1)}, f32[5,64,384]{2,1,0:T(8,128)}, u32[]{:S(2)}, u32[]{:S(2)}) collective-permute-start(f32[5,64,384]{2,1,0:T(8,128)S(1)} %collective-permute-done.6.refs_6_), channel_id=1, source_target_pairs={{0,8},{8,0},{1,9},{9,1},{2,10},{10,2},{3,11},{11,3},{4,12},{12,4},... | collective-permute-start | bytes 1474568 | tf_op jit(solution)/shard_map/ppermute | solution.py:252
  57.5 1.8 %copy-start.3 = (f32[5,64,384]{2,1,0:T(8,128)}, f32[5,64,384]{2,1,0:T(8,128)S(1)}, u32[]{:S(2)}) copy-start(f32[5,64,384]{2,1,0:T(8,128)S(1)} %collective-permute-done.3.refs_3_) | copy-start | bytes 1474564
  57.5 1.8 %copy-start.4 = (f32[5,64,384]{2,1,0:T(8,128)}, f32[5,64,384]{2,1,0:T(8,128)S(1)}, u32[]{:S(2)}) copy-start(f32[5,64,384]{2,1,0:T(8,128)S(1)} %collective-permute-done.5.refs_5_) | copy-start | bytes 1474564
  68.0 46.8 %copy-start.8 = (f32[3,5,1152]{2,0,1:T(4,128)S(1)}, f32[3,5,1152]{2,0,1:T(4,128)}, u32[]{:S(2)}) copy-start(f32[3,5,1152]{2,0,1:T(4,128)} %param.8) | copy-start | bytes 207364
  68.0 46.8 %copy-start.9 = (f32[192]{0:T(256)S(1)}, f32[192]{0:T(256)}, u32[]{:S(2)}) copy-start(f32[192]{0:T(256)} %va_ref.1) | copy-start | bytes 2308
  68.0 46.8 %copy-start.10 = (f32[40]{0:T(128)S(1)}, f32[40]{0:T(128)}, u32[]{:S(2)}) copy-start(f32[40]{0:T(128)} %occ_ref.1) | copy-start | bytes 484
  68.0 9.6 %collective-permute-start.8 = (f32[576,128]{1,0:T(8,128)S(1)}, f32[576,128]{1,0:T(8,128)S(1)}, u32[]{:S(2)}, u32[]{:S(2)}) collective-permute-start(f32[576,128]{1,0:T(8,128)S(1)} %get-tuple-element.7), channel_id=1, source_target_pairs={{0,1},{1,0},{2,3},{3,2},{4,5},{5,4},{6,7},{7,6},{8,9},{9,8},{10,11... | collective-permute-start | bytes 884744 | tf_op jit(solution)/shard_map/ppermute | solution.py:271
  78.3 36.5 %all-to-all-start.2 = ((f32[32,1,2304]{2,1,0:T(1,128)}), f32[32,1,2304]{2,1,0:T(1,128)S(1)}, u32[]{:S(2)}, u32[]{:S(2)}) async-start(f32[32,1,2304]{2,1,0:T(1,128)} %bitcast.8), calls=%async_computation.2 | async-start | bytes 589824 | tf_op jit(solution)/shard_map/all_to_all | solution.py:272

commit v8 on v7

--- a/solution.py
+++ b/solution.py
@@ -138,11 +138,8 @@
 
 
 def product_kernel(par_ref, got_ref, *refs):
-    away, (keep_ref, send_ref) = refs[:8], refs[9:11]
-    two_high, two_low, stage, swapped, whole, mixed, weights, arrived = refs[11:]
-    copies = [pltpu.make_async_copy(away[n], weights.at[n], arrived.at[n]) for n in range(8)]
-    for copy in copies:
-        copy.start()
+    weights, (keep_ref, send_ref) = refs[:8], refs[10:12]
+    two_high, two_low, stage, swapped, whole, mixed = refs[12:]
     for p in range(3):
         for y in range(4):
             for n in range(16):
@@ -170,14 +167,12 @@
         high, low = split2(whole[...])
         mixed[k, :192] = high
         mixed[k, 192:] = low
-    for copy in copies:
-        copy.wait()
     even = par_ref[0] == 0
     slot = index((192, 128), 1) & 15
     for q in range(4):
         total = jnp.zeros((192, 256), F32)
         for k in range(5):
-            rows = [weights[n, k, q * 16:(q + 1) * 16, :] for n in range(8)]
+            rows = [ref[k, q * 16:(q + 1) * 16, :] for ref in weights]
             near = [v[:, :256] for v in rows]
             far = [pltpu.roll(v[:, 128:], 192, 1) for v in rows]
             high, low = split2(jnp.concatenate(near + far, 0))
@@ -256,18 +251,18 @@
     both = lax.all_to_all(both, "y", 0, 0, tiled=True)
     ordered = [w for pair in zip(along, across) for w in pair]
     ordered = ordered[:4] + ordered[6:] + ordered[4:6]
-    mark = call(mark_kernel, 0, 8, [(8, 128)], [], 8, F32, 1000, pl.ANY)(*ordered)
+    mark = call(mark_kernel, 0, 4, [(8, 128)], [], 8, F32, 5000, pl.ANY)(*along)
+    wait = call(mark_kernel, 0, 1, [(8, 128)], [], 8, F32, 1000, pl.ANY)(both)
     keep, send = pl.pallas_call(
         product_kernel,
         out_shape=[jax.ShapeDtypeStruct((576, 128), F32)] * 2,
-        in_specs=[SMEM, VMEM] + [pl.BlockSpec(memory_space=pl.ANY)] * 9,
+        in_specs=[SMEM] + [VMEM] * 9 + [pl.BlockSpec(memory_space=pl.ANY)] * 2,
         out_specs=[VMEM] * 2,
         scratch_shapes=[pltpu.VMEM((384, 384), BF16)] * 2 + [pltpu.VMEM((384, 128), F32)]
-        + [pltpu.VMEM((2, 480, 256), F32), pltpu.VMEM((192, 256), F32), pltpu.VMEM((5, 384, 256), BF16)]
-        + [pltpu.VMEM((8, 5, 64, 384), F32), pltpu.SemaphoreType.DMA((8,))],
+        + [pltpu.VMEM((2, 480, 256), F32), pltpu.VMEM((192, 256), F32), pltpu.VMEM((5, 384, 256), BF16)],
         cost_estimate=pl.CostEstimate(flops=10**9, bytes_accessed=1000, transcendentals=0),
-        compiler_params=pltpu.CompilerParams(vmem_limit_bytes=52 * 1024 * 1024),
-    )(par.reshape(1), both, *ordered, mark)
+        compiler_params=pltpu.CompilerParams(vmem_limit_bytes=24 * 1024 * 1024),
+    )(par.reshape(1), both, *ordered, mark, wait)
     half = keep + lax.ppermute(send, "par", [(0, 1), (1, 0)])
     got = lax.all_to_all(half.reshape(32, 1, 2304), ("y", "zh", "pair"), 0, 0, tiled=True).reshape(576, 128)
     r = ((x * 4 + y) * 2 + zh) * 2 + core

time: 118 us -> 116 us (0.983)
  Pallas kernels: 11.7 us -> 10.4 us
    all_to_all x1, waiting for transfers between devices: 2.62 us -> 4.46 us  [body(): both = lax.all_to_all(both, 'y', 0, 0, tiled=True)]
    ppermute x4, waiting for transfers between devices: 1.8 us -> 0.01 us  [body(): across = [lax.ppermute(w, 'core', [(0, 1), (1, 0)]) for w in along]]
    pallas_call x1, Pallas kernels: 6.05 us -> 4.73 us  [body(): pl.pallas_call(product_kernel, out_shape=[jax.ShapeDtypeStruct((576, 128)...]
  transfers between devices with their start and end apart: 12 -> 12, of which waited for: 7 -> 6; matrix products, arithmetic and copies ran while one was open for 0% -> 0% of each run, Pallas kernels for 3% -> 3%
where the time goes in v8:
time: 116 us
  starting transfers between devices  57.4 us (49%)
  waiting for transfers between devices  44.7 us (39%)
  Pallas kernels  10.4 us (9%)
  between operations  1.52 us (1%)
    all_to_all x1, waiting for transfers between devices, body(): lax.all_to_all(half.reshape(32, 1, 2304), ('y', 'zh', 'pair'), 0, 0, tile...  22.2 us
    ppermute x1, starting transfers between devices, body(): other = lax.ppermute(amps, 'zh', [(0, 1), (1, 0)])  14.1 us
    all_to_all x1, starting transfers between devices, body(): lax.all_to_all(half.reshape(32, 1, 2304), ('y', 'zh', 'pair'), 0, 0, tile...  13.7 us
    ppermute x3, starting transfers between devices, body(): lax.ppermute(weights, 'x', [(s, (s - d) % 4) for s in range(4)])  10.6 us
    ppermute x4, starting transfers between devices, body(): across = [lax.ppermute(w, 'core', [(0, 1), (1, 0)]) for w in along]  8.14 us
    ppermute x1, waiting for transfers between devices, body(): half = keep + lax.ppermute(send, 'par', [(0, 1), (1, 0)])  7.44 us
    all_to_all x1, waiting for transfers between devices, body(): two = lax.all_to_all(two, ('x', 'zh', 'core'), 0, 0, tiled=True)  6.73 us
    pallas_call x1, Pallas kernels, body(): pl.pallas_call(product_kernel, out_shape=[jax.ShapeDtypeStruct((576, 128)...  4.73 us
  transfers between devices with their start and end apart: 12, of which 6 were waited for; matrix products, arithmetic and copies ran while one was open for 0% of the time, Pallas kernels for 3%

profile of v8, /device:TPU:64, one launch (start us, length us, event | category | flops | bytes accessed | tf_op | source)
XLA Modules:
  0.0 115.7 jit_solution(10071801257182830375)
XLA Ops:
  0.6 14.1 %collective-permute-start = (f32[5,3,1152]{2,1,0:T(4,128)}, f32[5,3,1152]{2,1,0:T(4,128)S(1)}, u32[]{:S(2)}, u32[]{:S(2)}) collective-permute-start(f32[5,3,1152]{2,1,0:T(4,128)} %bitcast.16), channel_id=1, source_target_pairs={{0,16},{16,0},{1,17},{17,1},{2,18},{18,2},{3,19},{19,3},{4,20},{20... | collective-permute-start | bytes 207368 | tf_op jit(solution)/shard_map/ppermute | solution.py:241
  14.7 0.9 copy-done.1
  15.6 1.2 %shard_map.78.token_ref = f32[16,24,128]{2,1,0:T(8,128)} custom-call(f32[5,3,1152]{2,1,0:T(4,128)S(1)} %bitcast.17), custom_call_target="tpu_custom_call" | custom-call | flops 1000000000 | bytes 1000 | tf_op jit(solution)/shard_map/pallas_call | solution.py:242
  16.8 4.4 %all-to-all-start = ((f32[16,24,128]{2,1,0:T(8,128)}), f32[16,24,128]{2,1,0:T(8,128)S(1)}, u32[]{:S(2)}, u32[]{:S(2)}) async-start(f32[16,24,128]{2,1,0:T(8,128)} %shard_map.78.token_ref), calls=%async_computation | async-start | bytes 393216 | tf_op jit(solution)/shard_map/all_to_all | solution.py:248
  21.3 1.1 shard_map.80.refs_0_
  22.4 5.1 %collective-permute-start.2 = (f32[5,64,384]{2,1,0:T(8,128)S(1)}, f32[5,64,384]{2,1,0:T(8,128)S(1)}, u32[]{:S(2)}, u32[]{:S(2)}) collective-permute-start(f32[5,64,384]{2,1,0:T(8,128)S(1)} %shard_map.80.refs_0_), channel_id=1, source_target_pairs={{0,384},{128,0},{256,128},{384,256},{1,385},{129,1},{257,129},{385... | collective-permute-start | bytes 1474568 | tf_op jit(solution)/shard_map/ppermute | solution.py:245
  27.4 2.8 %collective-permute-start.4 = (f32[5,64,384]{2,1,0:T(8,128)S(1)}, f32[5,64,384]{2,1,0:T(8,128)S(1)}, u32[]{:S(2)}, u32[]{:S(2)}) collective-permute-start(f32[5,64,384]{2,1,0:T(8,128)S(1)} %shard_map.80.refs_0_), channel_id=1, source_target_pairs={{0,256},{128,384},{256,0},{384,128},{1,257},{129,385},{257,1},{385... | collective-permute-start | bytes 1474568 | tf_op jit(solution)/shard_map/ppermute | solution.py:245
  30.2 2.8 %collective-permute-start.6 = (f32[5,64,384]{2,1,0:T(8,128)S(1)}, f32[5,64,384]{2,1,0:T(8,128)S(1)}, u32[]{:S(2)}, u32[]{:S(2)}) collective-permute-start(f32[5,64,384]{2,1,0:T(8,128)S(1)} %shard_map.80.refs_0_), channel_id=1, source_target_pairs={{0,128},{128,256},{256,384},{384,0},{1,129},{129,257},{257,385},{3... | collective-permute-start | bytes 1474568 | tf_op jit(solution)/shard_map/ppermute | solution.py:245
  33.1 6.7 %all-to-all-done.two_ref = f32[16,24,128]{2,1,0:T(8,128)S(1)} async-done(((f32[16,24,128]{2,1,0:T(8,128)}), f32[16,24,128]{2,1,0:T(8,128)S(1)}, u32[]{:S(2)}, u32[]{:S(2)}) %all-to-all-start) | async-done | bytes 196640 | tf_op jit(solution)/shard_map/all_to_all | solution.py:248
  39.8 1.1 shard_map.79
  40.9 4.5 %all-to-all-start.1 = ((f32[4,576,128]{2,1,0:T(8,128)}), f32[4,576,128]{2,1,0:T(8,128)S(1)}, u32[]{:S(2)}, u32[]{:S(2)}) async-start(f32[4,576,128]{2,1,0:T(8,128)} %shard_map.79), calls=%async_computation.1 | async-start | bytes 2359296 | tf_op jit(solution)/shard_map/all_to_all | solution.py:251
  45.4 1.9 %collective-permute-start.1 = (f32[5,64,384]{2,1,0:T(8,128)S(1)}, f32[5,64,384]{2,1,0:T(8,128)}, u32[]{:S(2)}, u32[]{:S(2)}) collective-permute-start(f32[5,64,384]{2,1,0:T(8,128)S(1)} %shard_map.80.refs_0_), channel_id=1, source_target_pairs={{0,8},{8,0},{1,9},{9,1},{2,10},{10,2},{3,11},{11,3},{4,12},{12,4},... | collective-permute-start | bytes 1474568 | tf_op jit(solution)/shard_map/ppermute | solution.py:247
  47.3 2.5 %collective-permute-done.2.refs_1_.refs_2_ = f32[5,64,384]{2,1,0:T(8,128)S(1)} collective-permute-done((f32[5,64,384]{2,1,0:T(8,128)S(1)}, f32[5,64,384]{2,1,0:T(8,128)S(1)}, u32[]{:S(2)}, u32[]{:S(2)}) %collective-permute-start.2) | collective-permute-done | bytes 491552 | tf_op jit(solution)/shard_map/ppermute | solution.py:245
  49.8 1.9 %collective-permute-start.3 = (f32[5,64,384]{2,1,0:T(8,128)S(1)}, f32[5,64,384]{2,1,0:T(8,128)}, u32[]{:S(2)}, u32[]{:S(2)}) collective-permute-start(f32[5,64,384]{2,1,0:T(8,128)S(1)} %collective-permute-done.2.refs_1_.refs_2_), channel_id=1, source_target_pairs={{0,8},{8,0},{1,9},{9,1},{2,10},{10,2},{3,11},{11,3},{4,12},{12,4},... | collective-permute-start | bytes 1474568 | tf_op jit(solution)/shard_map/ppermute | solution.py:247
  51.7 2.4 %collective-permute-start.5 = (f32[5,64,384]{2,1,0:T(8,128)S(1)}, f32[5,64,384]{2,1,0:T(8,128)}, u32[]{:S(2)}, u32[]{:S(2)}) collective-permute-start(f32[5,64,384]{2,1,0:T(8,128)S(1)} %collective-permute-done.4.refs_3_.refs_4_), channel_id=1, source_target_pairs={{0,8},{8,0},{1,9},{9,1},{2,10},{10,2},{3,11},{11,3},{4,12},{12,4},... | collective-permute-start | bytes 1474568 | tf_op jit(solution)/shard_map/ppermute | solution.py:247
  54.1 1.3 %collective-permute-done.6.refs_2_.refs_6_ = f32[5,64,384]{2,1,0:T(8,128)S(1)} collective-permute-done((f32[5,64,384]{2,1,0:T(8,128)S(1)}, f32[5,64,384]{2,1,0:T(8,128)S(1)}, u32[]{:S(2)}, u32[]{:S(2)}) %collective-permute-start.6) | collective-permute-done | bytes 491552 | tf_op jit(solution)/shard_map/ppermute | solution.py:245
  55.4 1.9 %collective-permute-start.7 = (f32[5,64,384]{2,1,0:T(8,128)S(1)}, f32[5,64,384]{2,1,0:T(8,128)}, u32[]{:S(2)}, u32[]{:S(2)}) collective-permute-start(f32[5,64,384]{2,1,0:T(8,128)S(1)} %collective-permute-done.6.refs_2_.refs_6_), channel_id=1, source_target_pairs={{0,8},{8,0},{1,9},{9,1},{2,10},{10,2},{3,11},{11,3},{4,12},{12,4},... | collective-permute-start | bytes 1474568 | tf_op jit(solution)/shard_map/ppermute | solution.py:247
  57.4 4.5 %all-to-all-done.1.refs_0_.got_ref = f32[4,576,128]{2,1,0:T(8,128)S(1)} async-done(((f32[4,576,128]{2,1,0:T(8,128)}), f32[4,576,128]{2,1,0:T(8,128)S(1)}, u32[]{:S(2)}, u32[]{:S(2)}) %all-to-all-start.1) | async-done | bytes 1179680 | tf_op jit(solution)/shard_map/all_to_all | solution.py:251
  61.9 4.7 %shard_map.83 = (f32[576,128]{1,0:T(8,128)S(1)}, f32[576,128]{1,0:T(8,128)S(1)}) custom-call(s32[1]{0:T(128)} %bitcast.4.par_ref, f32[4,576,128]{2,1,0:T(8,128)S(1)} %all-to-all-done.1.refs_0_.got_ref, f32[5,64,384]{2,1,0:T(8,128)S(1)} %shard_map.80.refs_0_, f32[5,64,384]{2,1,0:T(8,128)} %collective-permute-done.1.refs_1_, ...), custom_call_target="tpu_custom_call" | custom-call | flops 1000000000 | bytes 1000 | tf_op jit(solution)/shard_map/pallas_call | solution.py:256
  66.6 2.1 %collective-permute-start.8 = (f32[576,128]{1,0:T(8,128)S(1)}, f32[576,128]{1,0:T(8,128)S(1)}, u32[]{:S(2)}, u32[]{:S(2)}) collective-permute-start(f32[576,128]{1,0:T(8,128)S(1)} %get-tuple-element.7), channel_id=1, source_target_pairs={{0,1},{1,0},{2,3},{3,2},{4,5},{5,4},{6,7},{7,6},{8,9},{9,8},{10,11... | collective-permute-start | bytes 884744 | tf_op jit(solution)/shard_map/ppermute | solution.py:266
  68.7 7.4 %collective-permute-done.8 = f32[576,128]{1,0:T(8,128)S(1)} collective-permute-done((f32[576,128]{1,0:T(8,128)S(1)}, f32[576,128]{1,0:T(8,128)S(1)}, u32[]{:S(2)}, u32[]{:S(2)}) %collective-permute-start.8) | collective-permute-done | bytes 294944 | tf_op jit(solution)/shard_map/ppermute | solution.py:266
  76.9 13.7 %all-to-all-start.2 = ((f32[32,1,2304]{2,1,0:T(1,128)}), f32[32,1,2304]{2,1,0:T(1,128)S(1)}, u32[]{:S(2)}, u32[]{:S(2)}) async-start(f32[32,1,2304]{2,1,0:T(1,128)} %bitcast.8), calls=%async_computation.2 | async-start | bytes 589824 | tf_op jit(solution)/shard_map/all_to_all | solution.py:267
  91.3 22.2 %all-to-all-done.2 = f32[32,1,2304]{2,1,0:T(1,128)S(1)} async-done(((f32[32,1,2304]{2,1,0:T(1,128)}), f32[32,1,2304]{2,1,0:T(1,128)S(1)}, u32[]{:S(2)}, u32[]{:S(2)}) %all-to-all-start.2) | async-done | bytes 294944 | tf_op jit(solution)/shard_map/all_to_all | solution.py:267
  113.6 2.2 %shard_map.84 = (f32[5,3,1152]{2,1,0:T(4,128)}, f32[5,3,1152]{2,1,0:T(4,128)}) custom-call(s32[6]{0:T(128)S(1)} %stack.23.place_ref, f32[40]{0:T(128)S(1)} %copy-done.5, f32[192]{0:T(256)S(1)} %copy-done.4, f32[576,128]{1,0:T(8,128)S(1)} %bitcast.14, f32[1,192]{1,0:T(1,128)S(1)} %bitcast.20, f32[5,3,1152]{2,1,0:T(4,128)S(1)} %bitcast.19), custom_call_target="tpu_custom_call" | custom-call | flops 1000000000 | bytes 1000 | tf_op jit(solution)/shard_map/pallas_call | solution.py:270
  (22 shorter events, 1.0 us)
Async XLA Ops:
  0.6 20.6 %copy-start = (f32[3,5,7680]{2,0,1:T(4,128)S(1)}, f32[3,5,7680]{2,0,1:T(4,128)}, u32[]{:S(2)}) copy-start(f32[3,5,7680]{2,0,1:T(4,128)} %param.7) | copy-start | bytes 1382404
  0.6 32.4 %collective-permute-start = (f32[5,3,1152]{2,1,0:T(4,128)}, f32[5,3,1152]{2,1,0:T(4,128)S(1)}, u32[]{:S(2)}, u32[]{:S(2)}) collective-permute-start(f32[5,3,1152]{2,1,0:T(4,128)} %bitcast.16), channel_id=1, source_target_pairs={{0,16},{16,0},{1,17},{17,1},{2,18},{18,2},{3,19},{19,3},{4,20},{20... | collective-permute-start | bytes 207368 | tf_op jit(solution)/shard_map/ppermute | solution.py:241
  14.7 0.9 copy-start.1
  16.8 23.0 %all-to-all-start = ((f32[16,24,128]{2,1,0:T(8,128)}), f32[16,24,128]{2,1,0:T(8,128)S(1)}, u32[]{:S(2)}, u32[]{:S(2)}) async-start(f32[16,24,128]{2,1,0:T(8,128)} %shard_map.78.token_ref), calls=%async_computation | async-start | bytes 393216 | tf_op jit(solution)/shard_map/all_to_all | solution.py:248
  21.3 11.8 %copy-start.2 = (f32[3,5,1152]{2,0,1:T(4,128)S(1)}, f32[3,5,1152]{2,0,1:T(4,128)}, u32[]{:S(2)}) copy-start(f32[3,5,1152]{2,0,1:T(4,128)} %param.6) | copy-start | bytes 207364
  22.4 27.4 %collective-permute-start.2 = (f32[5,64,384]{2,1,0:T(8,128)S(1)}, f32[5,64,384]{2,1,0:T(8,128)S(1)}, u32[]{:S(2)}, u32[]{:S(2)}) collective-permute-start(f32[5,64,384]{2,1,0:T(8,128)S(1)} %shard_map.80.refs_0_), channel_id=1, source_target_pairs={{0,384},{128,0},{256,128},{384,256},{1,385},{129,1},{257,129},{385... | collective-permute-start | bytes 1474568 | tf_op jit(solution)/shard_map/ppermute | solution.py:245
  27.4 24.3 %collective-permute-start.4 = (f32[5,64,384]{2,1,0:T(8,128)S(1)}, f32[5,64,384]{2,1,0:T(8,128)S(1)}, u32[]{:S(2)}, u32[]{:S(2)}) collective-permute-start(f32[5,64,384]{2,1,0:T(8,128)S(1)} %shard_map.80.refs_0_), channel_id=1, source_target_pairs={{0,256},{128,384},{256,0},{384,128},{1,257},{129,385},{257,1},{385... | collective-permute-start | bytes 1474568 | tf_op jit(solution)/shard_map/ppermute | solution.py:245
  30.2 25.2 %collective-permute-start.6 = (f32[5,64,384]{2,1,0:T(8,128)S(1)}, f32[5,64,384]{2,1,0:T(8,128)S(1)}, u32[]{:S(2)}, u32[]{:S(2)}) collective-permute-start(f32[5,64,384]{2,1,0:T(8,128)S(1)} %shard_map.80.refs_0_), channel_id=1, source_target_pairs={{0,128},{128,256},{256,384},{384,0},{1,129},{129,257},{257,385},{3... | collective-permute-start | bytes 1474568 | tf_op jit(solution)/shard_map/ppermute | solution.py:245
  40.9 20.9 %all-to-all-start.1 = ((f32[4,576,128]{2,1,0:T(8,128)}), f32[4,576,128]{2,1,0:T(8,128)S(1)}, u32[]{:S(2)}, u32[]{:S(2)}) async-start(f32[4,576,128]{2,1,0:T(8,128)} %shard_map.79), calls=%async_computation.1 | async-start | bytes 2359296 | tf_op jit(solution)/shard_map/all_to_all | solution.py:251
  45.4 16.4 %collective-permute-start.1 = (f32[5,64,384]{2,1,0:T(8,128)S(1)}, f32[5,64,384]{2,1,0:T(8,128)}, u32[]{:S(2)}, u32[]{:S(2)}) collective-permute-start(f32[5,64,384]{2,1,0:T(8,128)S(1)} %shard_map.80.refs_0_), channel_id=1, source_target_pairs={{0,8},{8,0},{1,9},{9,1},{2,10},{10,2},{3,11},{11,3},{4,12},{12,4},... | collective-permute-start | bytes 1474568 | tf_op jit(solution)/shard_map/ppermute | solution.py:247
  49.8 12.0 %collective-permute-start.3 = (f32[5,64,384]{2,1,0:T(8,128)S(1)}, f32[5,64,384]{2,1,0:T(8,128)}, u32[]{:S(2)}, u32[]{:S(2)}) collective-permute-start(f32[5,64,384]{2,1,0:T(8,128)S(1)} %collective-permute-done.2.refs_1_.refs_2_), channel_id=1, source_target_pairs={{0,8},{8,0},{1,9},{9,1},{2,10},{10,2},{3,11},{11,3},{4,12},{12,4},... | collective-permute-start | bytes 1474568 | tf_op jit(solution)/shard_map/ppermute | solution.py:247
  51.7 10.1 %collective-permute-start.5 = (f32[5,64,384]{2,1,0:T(8,128)S(1)}, f32[5,64,384]{2,1,0:T(8,128)}, u32[]{:S(2)}, u32[]{:S(2)}) collective-permute-start(f32[5,64,384]{2,1,0:T(8,128)S(1)} %collective-permute-done.4.refs_3_.refs_4_), channel_id=1, source_target_pairs={{0,8},{8,0},{1,9},{9,1},{2,10},{10,2},{3,11},{11,3},{4,12},{12,4},... | collective-permute-start | bytes 1474568 | tf_op jit(solution)/shard_map/ppermute | solution.py:247
  55.4 6.4 %collective-permute-start.7 = (f32[5,64,384]{2,1,0:T(8,128)S(1)}, f32[5,64,384]{2,1,0:T(8,128)}, u32[]{:S(2)}, u32[]{:S(2)}) collective-permute-start(f32[5,64,384]{2,1,0:T(8,128)S(1)} %collective-permute-done.6.refs_2_.refs_6_), channel_id=1, source_target_pairs={{0,8},{8,0},{1,9},{9,1},{2,10},{10,2},{3,11},{11,3},{4,12},{12,4},... | collective-permute-start | bytes 1474568 | tf_op jit(solution)/shard_map/ppermute | solution.py:247
  66.6 47.0 %copy-start.3 = (f32[3,5,1152]{2,0,1:T(4,128)S(1)}, f32[3,5,1152]{2,0,1:T(4,128)}, u32[]{:S(2)}) copy-start(f32[3,5,1152]{2,0,1:T(4,128)} %param.8) | copy-start | bytes 207364
  66.6 47.0 %copy-start.4 = (f32[192]{0:T(256)S(1)}, f32[192]{0:T(256)}, u32[]{:S(2)}) copy-start(f32[192]{0:T(256)} %va_ref.1) | copy-start | bytes 2308
  66.6 46.9 %copy-start.5 = (f32[40]{0:T(128)S(1)}, f32[40]{0:T(128)}, u32[]{:S(2)}) copy-start(f32[40]{0:T(128)} %occ_ref.1) | copy-start | bytes 484
  66.6 9.5 %collective-permute-start.8 = (f32[576,128]{1,0:T(8,128)S(1)}, f32[576,128]{1,0:T(8,128)S(1)}, u32[]{:S(2)}, u32[]{:S(2)}) collective-permute-start(f32[576,128]{1,0:T(8,128)S(1)} %get-tuple-element.7), channel_id=1, source_target_pairs={{0,1},{1,0},{2,3},{3,2},{4,5},{5,4},{6,7},{7,6},{8,9},{9,8},{10,11... | collective-permute-start | bytes 884744 | tf_op jit(solution)/shard_map/ppermute | solution.py:266
  76.9 36.7 %all-to-all-start.2 = ((f32[32,1,2304]{2,1,0:T(1,128)}), f32[32,1,2304]{2,1,0:T(1,128)S(1)}, u32[]{:S(2)}, u32[]{:S(2)}) async-start(f32[32,1,2304]{2,1,0:T(1,128)} %bitcast.8), calls=%async_computation.2 | async-start | bytes 589824 | tf_op jit(solution)/shard_map/all_to_all | solution.py:267

commit v9 on v8

--- a/solution.py
+++ b/solution.py
@@ -190,7 +190,21 @@
                     ref[to:to + 9, :] = v[at:at + 9, :]
 
 
-def final_kernel(place_ref, occ_ref, va_ref, got_ref, vb_ref, res_ref, new_ref, inc_ref, sums, cyc, den):
+def spread_kernel(place_ref, out_ref):
+    out_ref[...] = spread_matrix(place_ref[5])
+
+
+def denominator_kernel(place_ref, occ_ref, va_ref, vb_ref, out_ref):
+    row = index((3, 192), 0)
+    va = [va_ref[place_ref[2] + m] for m in range(3)]
+    va = jnp.where(row == 0, va[0], jnp.where(row == 1, va[1], va[2]))
+    base = vb_ref[...] + va
+    for j in range(5):
+        for i in range(6):
+            out_ref[j, :, i * 192:(i + 1) * 192] = base - occ_ref[place_ref[4] + i] - occ_ref[place_ref[3] + j]
+
+
+def final_kernel(place_ref, got_ref, spread_ref, den_ref, res_ref, new_ref, inc_ref, sums, cyc):
     sums[...] = jnp.zeros_like(sums)
     for yz in range(8):
         total = got_ref[yz * 72:yz * 72 + 18, :]
@@ -199,25 +213,20 @@
             total += got_ref[at:at + 18, :]
         sums[yz * 24:yz * 24 + 18, :] = total
     v = pltpu.roll(sums[...], place_ref[0] * 32, 1)
-    lane = lax.broadcasted_iota(jnp.int32, v.shape, 1)
+    lane = index(v.shape, 1)
     other = jnp.where((lane & 16) == 0, pltpu.roll(v, 112, 1), pltpu.roll(v, 16, 1))
     v = jnp.where(place_ref[1] == 0, v, other)
-    wide = moved(v, spread_matrix(place_ref[5]))
-    row = lax.broadcasted_iota(jnp.int32, (3, 192), 0)
-    va = [va_ref[place_ref[2] + m] for m in range(3)]
-    va = jnp.where(row == 0, va[0], jnp.where(row == 1, va[1], va[2]))
-    base = vb_ref[...] + va
-    for i in range(6):
-        den[:, i * 192:(i + 1) * 192] = base - occ_ref[place_ref[4] + i]
+    wide = moved(v, spread_ref[...])
     for j in range(5):
         total = wide[0:24, j * 256:(j + 1) * 256]
         for yz in range(1, 8):
             total += pltpu.roll(wide[yz * 24:(yz + 1) * 24, j * 256:(j + 1) * 256], yz * 6, 1)
         for i in range(6):
-            cyc[:, i * 192:(i + 1) * 192] = total[i % 2 * 9 + i // 2 * 3:i % 2 * 9 + i // 2 * 3 + 3, :192]
+            at = i % 2 * 9 + i // 2 * 3
+            cyc[:, i * 192:(i + 1) * 192] = total[at:at + 3, :192]
         new = res_ref[j] + cyc[...]
         new_ref[j] = new
-        inc_ref[j] = new / (den[...] - occ_ref[place_ref[3] + j])
+        inc_ref[j] = new / den_ref[j]
 
 
 def call(kernel, n_smem, n_vmem, outs, scratch, mib=8, dtype=F32, cost=1000, space=pltpu.VMEM):
@@ -267,10 +276,13 @@
     got = lax.all_to_all(half.reshape(32, 1, 2304), ("y", "zh", "pair"), 0, 0, tiled=True).reshape(576, 128)
     r = ((x * 4 + y) * 2 + zh) * 2 + core
     place = jnp.stack([x, core, r * 3, (pair * 2 + par) * 5, window_start[0], par])
+    spread = call(spread_kernel, 1, 0, [(128, 1280)], [], 8, BF16)(place)
+    den = call(denominator_kernel, 3, 1, [(5, 3, 1152)], [])(
+        place, occupied_energy, virtual_energy, virtual_energy.reshape(1, 192)
+    )
     new, inc = call(
-        final_kernel, 3, 3, [(5, 3, 1152)] * 2,
-        [pltpu.VMEM((192, 128), F32), pltpu.VMEM((3, 1152), F32), pltpu.VMEM((3, 1152), F32)],
-    )(place, occupied_energy, virtual_energy, got, virtual_energy.reshape(1, 192), res)
+        final_kernel, 1, 4, [(5, 3, 1152)] * 2, [pltpu.VMEM((192, 128), F32), pltpu.VMEM((3, 1152), F32)]
+    )(place, got, spread, den, res)
     return jnp.transpose(new, (1, 0, 2)), jnp.transpose(inc, (1, 0, 2))
 
 

time: 116 us -> 116 us (level)
  waiting for transfers between devices: 44.7 us -> 43.3 us
  Pallas kernels: 10.4 us -> 11.7 us
    all_to_all x1, waiting for transfers between devices: 22.2 us -> 20.9 us  [body(): lax.all_to_all(half.reshape(32, 1, 2304), ('y', 'zh', 'pair'), 0, 0, tile...]
    pallas_call x1 -> x3, Pallas kernels: 2.16 us -> 3.41 us  [the longest x1 2.11 us: body(): call(final_kernel, 1, 4, [(5, 3, 1152)] * 2, [pltpu.VMEM((192, 128), F32)...]
  transfers between devices with their start and end apart: 12 -> 12, of which waited for: 6 -> 6; matrix products, arithmetic and copies ran while one was open for 0% -> 0% of each run, Pallas kernels for 3% -> 4%
where the time goes in v9:
time: 116 us
  starting transfers between devices  57.2 us (49%)
  waiting for transfers between devices  43.3 us (37%)
  Pallas kernels  11.7 us (10%)
  between operations  1.51 us (1%)
    all_to_all x1, waiting for transfers between devices, body(): lax.all_to_all(half.reshape(32, 1, 2304), ('y', 'zh', 'pair'), 0, 0, tile...  20.9 us
    ppermute x1, starting transfers between devices, body(): other = lax.ppermute(amps, 'zh', [(0, 1), (1, 0)])  14.1 us
    all_to_all x1, starting transfers between devices, body(): lax.all_to_all(half.reshape(32, 1, 2304), ('y', 'zh', 'pair'), 0, 0, tile...  13.7 us
    ppermute x3, starting transfers between devices, body(): lax.ppermute(weights, 'x', [(s, (s - d) % 4) for s in range(4)])  10.6 us
    ppermute x4, starting transfers between devices, body(): across = [lax.ppermute(w, 'core', [(0, 1), (1, 0)]) for w in along]  8.14 us
    ppermute x1, waiting for transfers between devices, body(): half = keep + lax.ppermute(send, 'par', [(0, 1), (1, 0)])  7.44 us
    all_to_all x1, waiting for transfers between devices, body(): two = lax.all_to_all(two, ('x', 'zh', 'core'), 0, 0, tiled=True)  6.73 us
    pallas_call x1, Pallas kernels, body(): pl.pallas_call(product_kernel, out_shape=[jax.ShapeDtypeStruct((576, 128)...  4.73 us
  transfers between devices with their start and end apart: 12, of which 6 were waited for; matrix products, arithmetic and copies ran while one was open for 0% of the time, Pallas kernels for 4%

profile of v9, /device:TPU:64, one launch (start us, length us, event | category | flops | bytes accessed | tf_op | source)
XLA Modules:
  0.0 115.5 jit_solution(13579372891775466840)
XLA Ops:
  0.6 14.1 %collective-permute-start = (f32[5,3,1152]{2,1,0:T(4,128)}, f32[5,3,1152]{2,1,0:T(4,128)S(1)}, u32[]{:S(2)}, u32[]{:S(2)}) collective-permute-start(f32[5,3,1152]{2,1,0:T(4,128)} %bitcast.16), channel_id=1, source_target_pairs={{0,16},{16,0},{1,17},{17,1},{2,18},{18,2},{3,19},{19,3},{4,20},{20... | collective-permute-start | bytes 207368 | tf_op jit(solution)/shard_map/ppermute | solution.py:250
  14.7 0.9 copy-done.1
  15.6 1.2 %shard_map.78.token_ref = f32[16,24,128]{2,1,0:T(8,128)} custom-call(f32[5,3,1152]{2,1,0:T(4,128)S(1)} %bitcast.17), custom_call_target="tpu_custom_call" | custom-call | flops 1000000000 | bytes 1000 | tf_op jit(solution)/shard_map/pallas_call | solution.py:251
  16.8 4.4 %all-to-all-start = ((f32[16,24,128]{2,1,0:T(8,128)}), f32[16,24,128]{2,1,0:T(8,128)S(1)}, u32[]{:S(2)}, u32[]{:S(2)}) async-start(f32[16,24,128]{2,1,0:T(8,128)} %shard_map.78.token_ref), calls=%async_computation | async-start | bytes 393216 | tf_op jit(solution)/shard_map/all_to_all | solution.py:257
  21.3 1.1 shard_map.80.refs_0_
  22.4 5.1 %collective-permute-start.2 = (f32[5,64,384]{2,1,0:T(8,128)S(1)}, f32[5,64,384]{2,1,0:T(8,128)S(1)}, u32[]{:S(2)}, u32[]{:S(2)}) collective-permute-start(f32[5,64,384]{2,1,0:T(8,128)S(1)} %shard_map.80.refs_0_), channel_id=1, source_target_pairs={{0,384},{128,0},{256,128},{384,256},{1,385},{129,1},{257,129},{385... | collective-permute-start | bytes 1474568 | tf_op jit(solution)/shard_map/ppermute | solution.py:254
  27.4 2.8 %collective-permute-start.4 = (f32[5,64,384]{2,1,0:T(8,128)S(1)}, f32[5,64,384]{2,1,0:T(8,128)S(1)}, u32[]{:S(2)}, u32[]{:S(2)}) collective-permute-start(f32[5,64,384]{2,1,0:T(8,128)S(1)} %shard_map.80.refs_0_), channel_id=1, source_target_pairs={{0,256},{128,384},{256,0},{384,128},{1,257},{129,385},{257,1},{385... | collective-permute-start | bytes 1474568 | tf_op jit(solution)/shard_map/ppermute | solution.py:254
  30.2 2.8 %collective-permute-start.6 = (f32[5,64,384]{2,1,0:T(8,128)S(1)}, f32[5,64,384]{2,1,0:T(8,128)S(1)}, u32[]{:S(2)}, u32[]{:S(2)}) collective-permute-start(f32[5,64,384]{2,1,0:T(8,128)S(1)} %shard_map.80.refs_0_), channel_id=1, source_target_pairs={{0,128},{128,256},{256,384},{384,0},{1,129},{129,257},{257,385},{3... | collective-permute-start | bytes 1474568 | tf_op jit(solution)/shard_map/ppermute | solution.py:254
  33.1 6.7 %all-to-all-done.two_ref = f32[16,24,128]{2,1,0:T(8,128)S(1)} async-done(((f32[16,24,128]{2,1,0:T(8,128)}), f32[16,24,128]{2,1,0:T(8,128)S(1)}, u32[]{:S(2)}, u32[]{:S(2)}) %all-to-all-start) | async-done | bytes 196640 | tf_op jit(solution)/shard_map/all_to_all | solution.py:257
  39.8 1.1 shard_map.79
  40.9 4.5 %all-to-all-start.1 = ((f32[4,576,128]{2,1,0:T(8,128)}), f32[4,576,128]{2,1,0:T(8,128)S(1)}, u32[]{:S(2)}, u32[]{:S(2)}) async-start(f32[4,576,128]{2,1,0:T(8,128)} %shard_map.79), calls=%async_computation.1 | async-start | bytes 2359296 | tf_op jit(solution)/shard_map/all_to_all | solution.py:260
  45.4 1.9 %collective-permute-start.1 = (f32[5,64,384]{2,1,0:T(8,128)S(1)}, f32[5,64,384]{2,1,0:T(8,128)}, u32[]{:S(2)}, u32[]{:S(2)}) collective-permute-start(f32[5,64,384]{2,1,0:T(8,128)S(1)} %shard_map.80.refs_0_), channel_id=1, source_target_pairs={{0,8},{8,0},{1,9},{9,1},{2,10},{10,2},{3,11},{11,3},{4,12},{12,4},... | collective-permute-start | bytes 1474568 | tf_op jit(solution)/shard_map/ppermute | solution.py:256
  47.3 2.5 %collective-permute-done.2.refs_1_.refs_2_ = f32[5,64,384]{2,1,0:T(8,128)S(1)} collective-permute-done((f32[5,64,384]{2,1,0:T(8,128)S(1)}, f32[5,64,384]{2,1,0:T(8,128)S(1)}, u32[]{:S(2)}, u32[]{:S(2)}) %collective-permute-start.2) | collective-permute-done | bytes 491552 | tf_op jit(solution)/shard_map/ppermute | solution.py:254
  49.8 1.9 %collective-permute-start.3 = (f32[5,64,384]{2,1,0:T(8,128)S(1)}, f32[5,64,384]{2,1,0:T(8,128)}, u32[]{:S(2)}, u32[]{:S(2)}) collective-permute-start(f32[5,64,384]{2,1,0:T(8,128)S(1)} %collective-permute-done.2.refs_1_.refs_2_), channel_id=1, source_target_pairs={{0,8},{8,0},{1,9},{9,1},{2,10},{10,2},{3,11},{11,3},{4,12},{12,4},... | collective-permute-start | bytes 1474568 | tf_op jit(solution)/shard_map/ppermute | solution.py:256
  51.7 2.4 %collective-permute-start.5 = (f32[5,64,384]{2,1,0:T(8,128)S(1)}, f32[5,64,384]{2,1,0:T(8,128)}, u32[]{:S(2)}, u32[]{:S(2)}) collective-permute-start(f32[5,64,384]{2,1,0:T(8,128)S(1)} %collective-permute-done.4.refs_3_.refs_4_), channel_id=1, source_target_pairs={{0,8},{8,0},{1,9},{9,1},{2,10},{10,2},{3,11},{11,3},{4,12},{12,4},... | collective-permute-start | bytes 1474568 | tf_op jit(solution)/shard_map/ppermute | solution.py:256
  54.1 1.3 %collective-permute-done.6.refs_2_.refs_6_ = f32[5,64,384]{2,1,0:T(8,128)S(1)} collective-permute-done((f32[5,64,384]{2,1,0:T(8,128)S(1)}, f32[5,64,384]{2,1,0:T(8,128)S(1)}, u32[]{:S(2)}, u32[]{:S(2)}) %collective-permute-start.6) | collective-permute-done | bytes 491552 | tf_op jit(solution)/shard_map/ppermute | solution.py:254
  55.4 1.9 %collective-permute-start.7 = (f32[5,64,384]{2,1,0:T(8,128)S(1)}, f32[5,64,384]{2,1,0:T(8,128)}, u32[]{:S(2)}, u32[]{:S(2)}) collective-permute-start(f32[5,64,384]{2,1,0:T(8,128)S(1)} %collective-permute-done.6.refs_2_.refs_6_), channel_id=1, source_target_pairs={{0,8},{8,0},{1,9},{9,1},{2,10},{10,2},{3,11},{11,3},{4,12},{12,4},... | collective-permute-start | bytes 1474568 | tf_op jit(solution)/shard_map/ppermute | solution.py:256
  57.4 4.5 %all-to-all-done.1.refs_0_.got_ref = f32[4,576,128]{2,1,0:T(8,128)S(1)} async-done(((f32[4,576,128]{2,1,0:T(8,128)}), f32[4,576,128]{2,1,0:T(8,128)S(1)}, u32[]{:S(2)}, u32[]{:S(2)}) %all-to-all-start.1) | async-done | bytes 1179680 | tf_op jit(solution)/shard_map/all_to_all | solution.py:260
  61.9 4.7 %shard_map.83 = (f32[576,128]{1,0:T(8,128)S(1)}, f32[576,128]{1,0:T(8,128)S(1)}) custom-call(s32[1]{0:T(128)} %bitcast.4.par_ref, f32[4,576,128]{2,1,0:T(8,128)S(1)} %all-to-all-done.1.refs_0_.got_ref, f32[5,64,384]{2,1,0:T(8,128)S(1)} %shard_map.80.refs_0_, f32[5,64,384]{2,1,0:T(8,128)} %collective-permute-done.1.refs_1_, ...), custom_call_target="tpu_custom_call" | custom-call | flops 1000000000 | bytes 1000 | tf_op jit(solution)/shard_map/pallas_call | solution.py:265
  66.6 1.9 %collective-permute-start.8 = (f32[576,128]{1,0:T(8,128)S(1)}, f32[576,128]{1,0:T(8,128)S(1)}, u32[]{:S(2)}, u32[]{:S(2)}) collective-permute-start(f32[576,128]{1,0:T(8,128)S(1)} %get-tuple-element.7), channel_id=1, source_target_pairs={{0,1},{1,0},{2,3},{3,2},{4,5},{5,4},{6,7},{7,6},{8,9},{9,8},{10,11... | collective-permute-start | bytes 884744 | tf_op jit(solution)/shard_map/ppermute | solution.py:275
  68.5 7.4 %collective-permute-done.8 = f32[576,128]{1,0:T(8,128)S(1)} collective-permute-done((f32[576,128]{1,0:T(8,128)S(1)}, f32[576,128]{1,0:T(8,128)S(1)}, u32[]{:S(2)}, u32[]{:S(2)}) %collective-permute-start.8) | collective-permute-done | bytes 294944 | tf_op jit(solution)/shard_map/ppermute | solution.py:275
  76.7 13.7 %all-to-all-start.2 = ((f32[32,1,2304]{2,1,0:T(1,128)}), f32[32,1,2304]{2,1,0:T(1,128)S(1)}, u32[]{:S(2)}, u32[]{:S(2)}) async-start(f32[32,1,2304]{2,1,0:T(1,128)} %bitcast.8), calls=%async_computation.2 | async-start | bytes 589824 | tf_op jit(solution)/shard_map/all_to_all | solution.py:276
  92.5 20.9 %all-to-all-done.2 = f32[32,1,2304]{2,1,0:T(1,128)S(1)} async-done(((f32[32,1,2304]{2,1,0:T(1,128)}), f32[32,1,2304]{2,1,0:T(1,128)S(1)}, u32[]{:S(2)}, u32[]{:S(2)}) %all-to-all-start.2) | async-done | bytes 294944 | tf_op jit(solution)/shard_map/all_to_all | solution.py:276
  113.4 2.1 %shard_map.86 = (f32[5,3,1152]{2,1,0:T(4,128)}, f32[5,3,1152]{2,1,0:T(4,128)}) custom-call(s32[6]{0:T(128)S(1)} %stack.23.place_ref, f32[576,128]{1,0:T(8,128)S(1)} %bitcast.14, bf16[128,1280]{1,0:T(8,128)(2,1)S(1)} %shard_map.84.spread_ref, f32[5,3,1152]{2,1,0:T(4,128)S(1)} %shard_map.85.den_ref, f32[5,3,1152]{2,1,0:T(4,128)S(1)} %bitcast.19), custom_call_target="tpu_custom_call" | custom-call | flops 1000000000 | bytes 1000 | tf_op jit(solution)/shard_map/pallas_call | solution.py:283
  (24 shorter events, 2.3 us)
Async XLA Ops:
  0.6 20.6 %copy-start = (f32[3,5,7680]{2,0,1:T(4,128)S(1)}, f32[3,5,7680]{2,0,1:T(4,128)}, u32[]{:S(2)}) copy-start(f32[3,5,7680]{2,0,1:T(4,128)} %param.7) | copy-start | bytes 1382404
  0.6 32.4 %collective-permute-start = (f32[5,3,1152]{2,1,0:T(4,128)}, f32[5,3,1152]{2,1,0:T(4,128)S(1)}, u32[]{:S(2)}, u32[]{:S(2)}) collective-permute-start(f32[5,3,1152]{2,1,0:T(4,128)} %bitcast.16), channel_id=1, source_target_pairs={{0,16},{16,0},{1,17},{17,1},{2,18},{18,2},{3,19},{19,3},{4,20},{20... | collective-permute-start | bytes 207368 | tf_op jit(solution)/shard_map/ppermute | solution.py:250
  14.7 0.9 copy-start.1
  16.8 23.0 %all-to-all-start = ((f32[16,24,128]{2,1,0:T(8,128)}), f32[16,24,128]{2,1,0:T(8,128)S(1)}, u32[]{:S(2)}, u32[]{:S(2)}) async-start(f32[16,24,128]{2,1,0:T(8,128)} %shard_map.78.token_ref), calls=%async_computation | async-start | bytes 393216 | tf_op jit(solution)/shard_map/all_to_all | solution.py:257
  21.3 11.8 %copy-start.2 = (f32[3,5,1152]{2,0,1:T(4,128)S(1)}, f32[3,5,1152]{2,0,1:T(4,128)}, u32[]{:S(2)}) copy-start(f32[3,5,1152]{2,0,1:T(4,128)} %param.6) | copy-start | bytes 207364
  22.4 27.4 %collective-permute-start.2 = (f32[5,64,384]{2,1,0:T(8,128)S(1)}, f32[5,64,384]{2,1,0:T(8,128)S(1)}, u32[]{:S(2)}, u32[]{:S(2)}) collective-permute-start(f32[5,64,384]{2,1,0:T(8,128)S(1)} %shard_map.80.refs_0_), channel_id=1, source_target_pairs={{0,384},{128,0},{256,128},{384,256},{1,385},{129,1},{257,129},{385... | collective-permute-start | bytes 1474568 | tf_op jit(solution)/shard_map/ppermute | solution.py:254
  27.4 24.3 %collective-permute-start.4 = (f32[5,64,384]{2,1,0:T(8,128)S(1)}, f32[5,64,384]{2,1,0:T(8,128)S(1)}, u32[]{:S(2)}, u32[]{:S(2)}) collective-permute-start(f32[5,64,384]{2,1,0:T(8,128)S(1)} %shard_map.80.refs_0_), channel_id=1, source_target_pairs={{0,256},{128,384},{256,0},{384,128},{1,257},{129,385},{257,1},{385... | collective-permute-start | bytes 1474568 | tf_op jit(solution)/shard_map/ppermute | solution.py:254
  30.2 25.2 %collective-permute-start.6 = (f32[5,64,384]{2,1,0:T(8,128)S(1)}, f32[5,64,384]{2,1,0:T(8,128)S(1)}, u32[]{:S(2)}, u32[]{:S(2)}) collective-permute-start(f32[5,64,384]{2,1,0:T(8,128)S(1)} %shard_map.80.refs_0_), channel_id=1, source_target_pairs={{0,128},{128,256},{256,384},{384,0},{1,129},{129,257},{257,385},{3... | collective-permute-start | bytes 1474568 | tf_op jit(solution)/shard_map/ppermute | solution.py:254
  40.9 20.9 %all-to-all-start.1 = ((f32[4,576,128]{2,1,0:T(8,128)}), f32[4,576,128]{2,1,0:T(8,128)S(1)}, u32[]{:S(2)}, u32[]{:S(2)}) async-start(f32[4,576,128]{2,1,0:T(8,128)} %shard_map.79), calls=%async_computation.1 | async-start | bytes 2359296 | tf_op jit(solution)/shard_map/all_to_all | solution.py:260
  45.4 16.4 %collective-permute-start.1 = (f32[5,64,384]{2,1,0:T(8,128)S(1)}, f32[5,64,384]{2,1,0:T(8,128)}, u32[]{:S(2)}, u32[]{:S(2)}) collective-permute-start(f32[5,64,384]{2,1,0:T(8,128)S(1)} %shard_map.80.refs_0_), channel_id=1, source_target_pairs={{0,8},{8,0},{1,9},{9,1},{2,10},{10,2},{3,11},{11,3},{4,12},{12,4},... | collective-permute-start | bytes 1474568 | tf_op jit(solution)/shard_map/ppermute | solution.py:256
  49.8 12.0 %collective-permute-start.3 = (f32[5,64,384]{2,1,0:T(8,128)S(1)}, f32[5,64,384]{2,1,0:T(8,128)}, u32[]{:S(2)}, u32[]{:S(2)}) collective-permute-start(f32[5,64,384]{2,1,0:T(8,128)S(1)} %collective-permute-done.2.refs_1_.refs_2_), channel_id=1, source_target_pairs={{0,8},{8,0},{1,9},{9,1},{2,10},{10,2},{3,11},{11,3},{4,12},{12,4},... | collective-permute-start | bytes 1474568 | tf_op jit(solution)/shard_map/ppermute | solution.py:256
  51.7 10.1 %collective-permute-start.5 = (f32[5,64,384]{2,1,0:T(8,128)S(1)}, f32[5,64,384]{2,1,0:T(8,128)}, u32[]{:S(2)}, u32[]{:S(2)}) collective-permute-start(f32[5,64,384]{2,1,0:T(8,128)S(1)} %collective-permute-done.4.refs_3_.refs_4_), channel_id=1, source_target_pairs={{0,8},{8,0},{1,9},{9,1},{2,10},{10,2},{3,11},{11,3},{4,12},{12,4},... | collective-permute-start | bytes 1474568 | tf_op jit(solution)/shard_map/ppermute | solution.py:256
  55.4 6.4 %collective-permute-start.7 = (f32[5,64,384]{2,1,0:T(8,128)S(1)}, f32[5,64,384]{2,1,0:T(8,128)}, u32[]{:S(2)}, u32[]{:S(2)}) collective-permute-start(f32[5,64,384]{2,1,0:T(8,128)S(1)} %collective-permute-done.6.refs_2_.refs_6_), channel_id=1, source_target_pairs={{0,8},{8,0},{1,9},{9,1},{2,10},{10,2},{3,11},{11,3},{4,12},{12,4},... | collective-permute-start | bytes 1474568 | tf_op jit(solution)/shard_map/ppermute | solution.py:256
  66.6 9.4 %collective-permute-start.8 = (f32[576,128]{1,0:T(8,128)S(1)}, f32[576,128]{1,0:T(8,128)S(1)}, u32[]{:S(2)}, u32[]{:S(2)}) collective-permute-start(f32[576,128]{1,0:T(8,128)S(1)} %get-tuple-element.7), channel_id=1, source_target_pairs={{0,1},{1,0},{2,3},{3,2},{4,5},{5,4},{6,7},{7,6},{8,9},{9,8},{10,11... | collective-permute-start | bytes 884744 | tf_op jit(solution)/shard_map/ppermute | solution.py:275
  76.7 36.7 %all-to-all-start.2 = ((f32[32,1,2304]{2,1,0:T(1,128)}), f32[32,1,2304]{2,1,0:T(1,128)S(1)}, u32[]{:S(2)}, u32[]{:S(2)}) async-start(f32[32,1,2304]{2,1,0:T(1,128)} %bitcast.8), calls=%async_computation.2 | async-start | bytes 589824 | tf_op jit(solution)/shard_map/all_to_all | solution.py:276
  91.1 0.7 copy-start.4
  91.1 0.7 copy-start.5
  91.8 21.6 %copy-start.3 = (f32[3,5,1152]{2,0,1:T(4,128)S(1)}, f32[3,5,1152]{2,0,1:T(4,128)}, u32[]{:S(2)}) copy-start(f32[3,5,1152]{2,0,1:T(4,128)} %param.8) | copy-start | bytes 207364

commit v10 on v9

--- a/solution.py
+++ b/solution.py
@@ -250,9 +250,8 @@
     other = lax.ppermute(amps, "zh", [(0, 1), (1, 0)])
     two = call(swap_kernel, 0, 1, [(16, 24, 128)], [pltpu.VMEM((120, 256), F32)])(amps)
     weights = call(weights_kernel, 0, 2, [(5, 64, 384)], [])(ints, two)
-    along = [weights] + [
-        lax.ppermute(weights, "x", [(s, (s - d) % 4) for s in range(4)]) for d in (1, 3, 2)
-    ]
+    near, back = [lax.ppermute(weights, "x", [(s, (s - d) % 4) for s in range(4)]) for d in (1, 3)]
+    along = [weights, near, back, lax.ppermute(near, "x", [(s, (s - 1) % 4) for s in range(4)])]
     across = [lax.ppermute(w, "core", [(0, 1), (1, 0)]) for w in along]
     two = lax.all_to_all(two, ("x", "zh", "core"), 0, 0, tiled=True)
     one = call(merge_kernel, 1, 2, [(288, 128)], [pltpu.VMEM((96, 384), F32)], cost=8000)(zh.reshape(1), amps, other)

time: 116 us -> 116 us (level)
  waiting for transfers between devices: 43.3 us -> 40.1 us
  starting transfers between devices: 57.2 us -> 59.8 us
    all_to_all x1, waiting for transfers between devices: 6.73 us -> 0.01 us  [body(): two = lax.all_to_all(two, ('x', 'zh', 'core'), 0, 0, tiled=True)]
    ppermute x3 -> x2, waiting for transfers between devices: 3.77 us -> 9.81 us  [body(): lax.ppermute(weights, 'x', [(s, (s - d) % 4) for s in range(4)])]
    ppermute x0 -> x1, starting transfers between devices: none -> 5.59 us  [body(): lax.ppermute(near, 'x', [(s, (s - 1) % 4) for s in range(4)])]
    ppermute x3 -> x2, starting transfers between devices: 10.6 us -> 6.98 us  [body(): lax.ppermute(weights, 'x', [(s, (s - d) % 4) for s in range(4)])]
    all_to_all x1, waiting for transfers between devices: 20.9 us -> 17.5 us  [body(): lax.all_to_all(half.reshape(32, 1, 2304), ('y', 'zh', 'pair'), 0, 0, tile...]
    all_to_all x1, waiting for transfers between devices: 4.46 us -> 6.99 us  [body(): both = lax.all_to_all(both, 'y', 0, 0, tiled=True)]
    ppermute x1, waiting for transfers between devices: 7.44 us -> 5.72 us  [body(): half = keep + lax.ppermute(send, 'par', [(0, 1), (1, 0)])]
  transfers between devices with their start and end apart: 12 -> 12, of which waited for: 6 -> 4; matrix products, arithmetic and copies ran while one was open for 0% -> 0% of each run, Pallas kernels for 4% -> 4%
where the time goes in v10:
time: 116 us; the launch traced here: 115 us
  starting transfers between devices  59.8 us (52%)
  waiting for transfers between devices  40.1 us (35%)
  Pallas kernels  11.7 us (10%)
  between operations  1.52 us (1%)
    all_to_all x1, waiting for transfers between devices, body(): lax.all_to_all(half.reshape(32, 1, 2304), ('y', 'zh', 'pair'), 0, 0, tile...  17.5 us
    ppermute x1, starting transfers between devices, body(): other = lax.ppermute(amps, 'zh', [(0, 1), (1, 0)])  14.1 us
    all_to_all x1, starting transfers between devices, body(): lax.all_to_all(half.reshape(32, 1, 2304), ('y', 'zh', 'pair'), 0, 0, tile...  12.7 us
    ppermute x2, waiting for transfers between devices, body(): lax.ppermute(weights, 'x', [(s, (s - d) % 4) for s in range(4)])  9.81 us
    ppermute x4, starting transfers between devices, body(): across = [lax.ppermute(w, 'core', [(0, 1), (1, 0)]) for w in along]  8.65 us
    all_to_all x1, waiting for transfers between devices, body(): both = lax.all_to_all(both, 'y', 0, 0, tiled=True)  6.99 us
    ppermute x2, starting transfers between devices, body(): lax.ppermute(weights, 'x', [(s, (s - d) % 4) for s in range(4)])  6.98 us
    ppermute x1, waiting for transfers between devices, body(): half = keep + lax.ppermute(send, 'par', [(0, 1), (1, 0)])  5.72 us
  transfers between devices with their start and end apart: 12, of which 4 were waited for; matrix products, arithmetic and copies ran while one was open for 0% of the time, Pallas kernels for 4%

profile of v10, /device:TPU:64, one launch (start us, length us, event | category | flops | bytes accessed | tf_op | source)
XLA Modules:
  0.0 114.8 jit_solution(115253272246120857)
XLA Ops:
  0.6 14.1 %collective-permute-start = (f32[5,3,1152]{2,1,0:T(4,128)}, f32[5,3,1152]{2,1,0:T(4,128)S(1)}, u32[]{:S(2)}, u32[]{:S(2)}) collective-permute-start(f32[5,3,1152]{2,1,0:T(4,128)} %bitcast.16), channel_id=1, source_target_pairs={{0,16},{16,0},{1,17},{17,1},{2,18},{18,2},{3,19},{19,3},{4,20},{20... | collective-permute-start | bytes 207368 | tf_op jit(solution)/shard_map/ppermute | solution.py:250
  14.7 0.9 copy-done.1
  15.6 1.2 %shard_map.78.token_ref = f32[16,24,128]{2,1,0:T(8,128)} custom-call(f32[5,3,1152]{2,1,0:T(4,128)S(1)} %bitcast.17), custom_call_target="tpu_custom_call" | custom-call | flops 1000000000 | bytes 1000 | tf_op jit(solution)/shard_map/pallas_call | solution.py:251
  16.8 4.4 %all-to-all-start = ((f32[16,24,128]{2,1,0:T(8,128)}), f32[16,24,128]{2,1,0:T(8,128)S(1)}, u32[]{:S(2)}, u32[]{:S(2)}) async-start(f32[16,24,128]{2,1,0:T(8,128)} %shard_map.78.token_ref), calls=%async_computation | async-start | bytes 393216 | tf_op jit(solution)/shard_map/all_to_all | solution.py:256
  21.3 1.1 shard_map.80.refs_0_
  22.4 5.1 %collective-permute-start.2 = (f32[5,64,384]{2,1,0:T(8,128)S(1)}, f32[5,64,384]{2,1,0:T(8,128)S(1)}, u32[]{:S(2)}, u32[]{:S(2)}) collective-permute-start(f32[5,64,384]{2,1,0:T(8,128)S(1)} %shard_map.80.refs_0_), channel_id=1, source_target_pairs={{0,384},{128,0},{256,128},{384,256},{1,385},{129,1},{257,129},{385... | collective-permute-start | bytes 1474568 | tf_op jit(solution)/shard_map/ppermute | solution.py:253
  27.4 1.9 %collective-permute-start.6 = (f32[5,64,384]{2,1,0:T(8,128)S(1)}, f32[5,64,384]{2,1,0:T(8,128)S(1)}, u32[]{:S(2)}, u32[]{:S(2)}) collective-permute-start(f32[5,64,384]{2,1,0:T(8,128)S(1)} %shard_map.80.refs_0_), channel_id=1, source_target_pairs={{0,128},{128,256},{256,384},{384,0},{1,129},{129,257},{257,385},{3... | collective-permute-start | bytes 1474568 | tf_op jit(solution)/shard_map/ppermute | solution.py:253
  29.5 9.8 %collective-permute-done.2.refs_1_.refs_2_ = f32[5,64,384]{2,1,0:T(8,128)S(1)} collective-permute-done((f32[5,64,384]{2,1,0:T(8,128)S(1)}, f32[5,64,384]{2,1,0:T(8,128)S(1)}, u32[]{:S(2)}, u32[]{:S(2)}) %collective-permute-start.2) | collective-permute-done | bytes 491552 | tf_op jit(solution)/shard_map/ppermute | solution.py:253
  39.3 5.6 %collective-permute-start.4 = (f32[5,64,384]{2,1,0:T(8,128)S(1)}, f32[5,64,384]{2,1,0:T(8,128)S(1)}, u32[]{:S(2)}, u32[]{:S(2)}) collective-permute-start(f32[5,64,384]{2,1,0:T(8,128)S(1)} %collective-permute-done.2.refs_1_.refs_2_), channel_id=1, source_target_pairs={{0,384},{128,0},{256,128},{384,256},{1,385},{129,1},{257,129},{385... | collective-permute-start | bytes 1474568 | tf_op jit(solution)/shard_map/ppermute | solution.py:254
  44.9 1.1 shard_map.79
  46.0 4.5 %all-to-all-start.1 = ((f32[4,576,128]{2,1,0:T(8,128)}), f32[4,576,128]{2,1,0:T(8,128)S(1)}, u32[]{:S(2)}, u32[]{:S(2)}) async-start(f32[4,576,128]{2,1,0:T(8,128)} %shard_map.79), calls=%async_computation.1 | async-start | bytes 2359296 | tf_op jit(solution)/shard_map/all_to_all | solution.py:259
  50.5 1.9 %collective-permute-start.1 = (f32[5,64,384]{2,1,0:T(8,128)S(1)}, f32[5,64,384]{2,1,0:T(8,128)}, u32[]{:S(2)}, u32[]{:S(2)}) collective-permute-start(f32[5,64,384]{2,1,0:T(8,128)S(1)} %shard_map.80.refs_0_), channel_id=1, source_target_pairs={{0,8},{8,0},{1,9},{9,1},{2,10},{10,2},{3,11},{11,3},{4,12},{12,4},... | collective-permute-start | bytes 1474568 | tf_op jit(solution)/shard_map/ppermute | solution.py:255
  52.4 2.4 %collective-permute-start.3 = (f32[5,64,384]{2,1,0:T(8,128)S(1)}, f32[5,64,384]{2,1,0:T(8,128)}, u32[]{:S(2)}, u32[]{:S(2)}) collective-permute-start(f32[5,64,384]{2,1,0:T(8,128)S(1)} %collective-permute-done.2.refs_1_.refs_2_), channel_id=1, source_target_pairs={{0,8},{8,0},{1,9},{9,1},{2,10},{10,2},{3,11},{11,3},{4,12},{12,4},... | collective-permute-start | bytes 1474568 | tf_op jit(solution)/shard_map/ppermute | solution.py:255
  54.8 1.9 %collective-permute-start.7 = (f32[5,64,384]{2,1,0:T(8,128)S(1)}, f32[5,64,384]{2,1,0:T(8,128)}, u32[]{:S(2)}, u32[]{:S(2)}) collective-permute-start(f32[5,64,384]{2,1,0:T(8,128)S(1)} %collective-permute-done.6.refs_2_.refs_6_), channel_id=1, source_target_pairs={{0,8},{8,0},{1,9},{9,1},{2,10},{10,2},{3,11},{11,3},{4,12},{12,4},... | collective-permute-start | bytes 1474568 | tf_op jit(solution)/shard_map/ppermute | solution.py:255
  56.8 2.4 %collective-permute-start.5 = (f32[5,64,384]{2,1,0:T(8,128)S(1)}, f32[5,64,384]{2,1,0:T(8,128)}, u32[]{:S(2)}, u32[]{:S(2)}) collective-permute-start(f32[5,64,384]{2,1,0:T(8,128)S(1)} %collective-permute-done.4.refs_3_.refs_4_), channel_id=1, source_target_pairs={{0,8},{8,0},{1,9},{9,1},{2,10},{10,2},{3,11},{11,3},{4,12},{12,4},... | collective-permute-start | bytes 1474568 | tf_op jit(solution)/shard_map/ppermute | solution.py:255
  59.2 7.0 %all-to-all-done.1.refs_0_.got_ref = f32[4,576,128]{2,1,0:T(8,128)S(1)} async-done(((f32[4,576,128]{2,1,0:T(8,128)}), f32[4,576,128]{2,1,0:T(8,128)S(1)}, u32[]{:S(2)}, u32[]{:S(2)}) %all-to-all-start.1) | async-done | bytes 1179680 | tf_op jit(solution)/shard_map/all_to_all | solution.py:259
  66.2 4.7 %shard_map.83 = (f32[576,128]{1,0:T(8,128)S(1)}, f32[576,128]{1,0:T(8,128)S(1)}) custom-call(s32[1]{0:T(128)} %bitcast.4.par_ref, f32[4,576,128]{2,1,0:T(8,128)S(1)} %all-to-all-done.1.refs_0_.got_ref, f32[5,64,384]{2,1,0:T(8,128)S(1)} %shard_map.80.refs_0_, f32[5,64,384]{2,1,0:T(8,128)} %collective-permute-done.1.refs_1_, ...), custom_call_target="tpu_custom_call" | custom-call | flops 1000000000 | bytes 1000 | tf_op jit(solution)/shard_map/pallas_call | solution.py:264
  70.9 2.9 %collective-permute-start.8 = (f32[576,128]{1,0:T(8,128)S(1)}, f32[576,128]{1,0:T(8,128)S(1)}, u32[]{:S(2)}, u32[]{:S(2)}) collective-permute-start(f32[576,128]{1,0:T(8,128)S(1)} %get-tuple-element.7), channel_id=1, source_target_pairs={{0,1},{1,0},{2,3},{3,2},{4,5},{5,4},{6,7},{7,6},{8,9},{9,8},{10,11... | collective-permute-start | bytes 884744 | tf_op jit(solution)/shard_map/ppermute | solution.py:274
  73.9 5.7 %collective-permute-done.8 = f32[576,128]{1,0:T(8,128)S(1)} collective-permute-done((f32[576,128]{1,0:T(8,128)S(1)}, f32[576,128]{1,0:T(8,128)S(1)}, u32[]{:S(2)}, u32[]{:S(2)}) %collective-permute-start.8) | collective-permute-done | bytes 294944 | tf_op jit(solution)/shard_map/ppermute | solution.py:274
  79.6 0.8 add.19
  80.4 12.7 %all-to-all-start.2 = ((f32[32,1,2304]{2,1,0:T(1,128)}), f32[32,1,2304]{2,1,0:T(1,128)S(1)}, u32[]{:S(2)}, u32[]{:S(2)}) async-start(f32[32,1,2304]{2,1,0:T(1,128)} %bitcast.8), calls=%async_computation.2 | async-start | bytes 589824 | tf_op jit(solution)/shard_map/all_to_all | solution.py:275
  94.5 0.7 shard_map.85.den_ref
  95.2 17.5 %all-to-all-done.2 = f32[32,1,2304]{2,1,0:T(1,128)S(1)} async-done(((f32[32,1,2304]{2,1,0:T(1,128)}), f32[32,1,2304]{2,1,0:T(1,128)S(1)}, u32[]{:S(2)}, u32[]{:S(2)}) %all-to-all-start.2) | async-done | bytes 294944 | tf_op jit(solution)/shard_map/all_to_all | solution.py:275
  112.7 2.1 %shard_map.86 = (f32[5,3,1152]{2,1,0:T(4,128)}, f32[5,3,1152]{2,1,0:T(4,128)}) custom-call(s32[6]{0:T(128)S(1)} %stack.23.place_ref, f32[576,128]{1,0:T(8,128)S(1)} %bitcast.14, bf16[128,1280]{1,0:T(8,128)(2,1)S(1)} %shard_map.84.spread_ref, f32[5,3,1152]{2,1,0:T(4,128)S(1)} %shard_map.85.den_ref, f32[5,3,1152]{2,1,0:T(4,128)S(1)} %bitcast.19), custom_call_target="tpu_custom_call" | custom-call | flops 1000000000 | bytes 1000 | tf_op jit(solution)/shard_map/pallas_call | solution.py:282
  (24 shorter events, 0.9 us)
Async XLA Ops:
  0.6 20.6 %copy-start = (f32[3,5,7680]{2,0,1:T(4,128)S(1)}, f32[3,5,7680]{2,0,1:T(4,128)}, u32[]{:S(2)}) copy-start(f32[3,5,7680]{2,0,1:T(4,128)} %param.7) | copy-start | bytes 1382404
  0.6 28.7 %collective-permute-start = (f32[5,3,1152]{2,1,0:T(4,128)}, f32[5,3,1152]{2,1,0:T(4,128)S(1)}, u32[]{:S(2)}, u32[]{:S(2)}) collective-permute-start(f32[5,3,1152]{2,1,0:T(4,128)} %bitcast.16), channel_id=1, source_target_pairs={{0,16},{16,0},{1,17},{17,1},{2,18},{18,2},{3,19},{19,3},{4,20},{20... | collective-permute-start | bytes 207368 | tf_op jit(solution)/shard_map/ppermute | solution.py:250
  14.7 0.9 copy-start.1
  16.8 28.0 %all-to-all-start = ((f32[16,24,128]{2,1,0:T(8,128)}), f32[16,24,128]{2,1,0:T(8,128)S(1)}, u32[]{:S(2)}, u32[]{:S(2)}) async-start(f32[16,24,128]{2,1,0:T(8,128)} %shard_map.78.token_ref), calls=%async_computation | async-start | bytes 393216 | tf_op jit(solution)/shard_map/all_to_all | solution.py:256
  21.3 8.1 %copy-start.2 = (f32[3,5,1152]{2,0,1:T(4,128)S(1)}, f32[3,5,1152]{2,0,1:T(4,128)}, u32[]{:S(2)}) copy-start(f32[3,5,1152]{2,0,1:T(4,128)} %param.6) | copy-start | bytes 207364
  22.4 16.9 %collective-permute-start.2 = (f32[5,64,384]{2,1,0:T(8,128)S(1)}, f32[5,64,384]{2,1,0:T(8,128)S(1)}, u32[]{:S(2)}, u32[]{:S(2)}) collective-permute-start(f32[5,64,384]{2,1,0:T(8,128)S(1)} %shard_map.80.refs_0_), channel_id=1, source_target_pairs={{0,384},{128,0},{256,128},{384,256},{1,385},{129,1},{257,129},{385... | collective-permute-start | bytes 1474568 | tf_op jit(solution)/shard_map/ppermute | solution.py:253
  27.4 27.4 %collective-permute-start.6 = (f32[5,64,384]{2,1,0:T(8,128)S(1)}, f32[5,64,384]{2,1,0:T(8,128)S(1)}, u32[]{:S(2)}, u32[]{:S(2)}) collective-permute-start(f32[5,64,384]{2,1,0:T(8,128)S(1)} %shard_map.80.refs_0_), channel_id=1, source_target_pairs={{0,128},{128,256},{256,384},{384,0},{1,129},{129,257},{257,385},{3... | collective-permute-start | bytes 1474568 | tf_op jit(solution)/shard_map/ppermute | solution.py:253
  39.3 17.5 %collective-permute-start.4 = (f32[5,64,384]{2,1,0:T(8,128)S(1)}, f32[5,64,384]{2,1,0:T(8,128)S(1)}, u32[]{:S(2)}, u32[]{:S(2)}) collective-permute-start(f32[5,64,384]{2,1,0:T(8,128)S(1)} %collective-permute-done.2.refs_1_.refs_2_), channel_id=1, source_target_pairs={{0,384},{128,0},{256,128},{384,256},{1,385},{129,1},{257,129},{385... | collective-permute-start | bytes 1474568 | tf_op jit(solution)/shard_map/ppermute | solution.py:254
  46.0 20.2 %all-to-all-start.1 = ((f32[4,576,128]{2,1,0:T(8,128)}), f32[4,576,128]{2,1,0:T(8,128)S(1)}, u32[]{:S(2)}, u32[]{:S(2)}) async-start(f32[4,576,128]{2,1,0:T(8,128)} %shard_map.79), calls=%async_computation.1 | async-start | bytes 2359296 | tf_op jit(solution)/shard_map/all_to_all | solution.py:259
  50.5 15.7 %collective-permute-start.1 = (f32[5,64,384]{2,1,0:T(8,128)S(1)}, f32[5,64,384]{2,1,0:T(8,128)}, u32[]{:S(2)}, u32[]{:S(2)}) collective-permute-start(f32[5,64,384]{2,1,0:T(8,128)S(1)} %shard_map.80.refs_0_), channel_id=1, source_target_pairs={{0,8},{8,0},{1,9},{9,1},{2,10},{10,2},{3,11},{11,3},{4,12},{12,4},... | collective-permute-start | bytes 1474568 | tf_op jit(solution)/shard_map/ppermute | solution.py:255
  52.4 13.8 %collective-permute-start.3 = (f32[5,64,384]{2,1,0:T(8,128)S(1)}, f32[5,64,384]{2,1,0:T(8,128)}, u32[]{:S(2)}, u32[]{:S(2)}) collective-permute-start(f32[5,64,384]{2,1,0:T(8,128)S(1)} %collective-permute-done.2.refs_1_.refs_2_), channel_id=1, source_target_pairs={{0,8},{8,0},{1,9},{9,1},{2,10},{10,2},{3,11},{11,3},{4,12},{12,4},... | collective-permute-start | bytes 1474568 | tf_op jit(solution)/shard_map/ppermute | solution.py:255
  54.8 11.4 %collective-permute-start.7 = (f32[5,64,384]{2,1,0:T(8,128)S(1)}, f32[5,64,384]{2,1,0:T(8,128)}, u32[]{:S(2)}, u32[]{:S(2)}) collective-permute-start(f32[5,64,384]{2,1,0:T(8,128)S(1)} %collective-permute-done.6.refs_2_.refs_6_), channel_id=1, source_target_pairs={{0,8},{8,0},{1,9},{9,1},{2,10},{10,2},{3,11},{11,3},{4,12},{12,4},... | collective-permute-start | bytes 1474568 | tf_op jit(solution)/shard_map/ppermute | solution.py:255
  56.8 9.4 %collective-permute-start.5 = (f32[5,64,384]{2,1,0:T(8,128)S(1)}, f32[5,64,384]{2,1,0:T(8,128)}, u32[]{:S(2)}, u32[]{:S(2)}) collective-permute-start(f32[5,64,384]{2,1,0:T(8,128)S(1)} %collective-permute-done.4.refs_3_.refs_4_), channel_id=1, source_target_pairs={{0,8},{8,0},{1,9},{9,1},{2,10},{10,2},{3,11},{11,3},{4,12},{12,4},... | collective-permute-start | bytes 1474568 | tf_op jit(solution)/shard_map/ppermute | solution.py:255
  70.9 8.7 %collective-permute-start.8 = (f32[576,128]{1,0:T(8,128)S(1)}, f32[576,128]{1,0:T(8,128)S(1)}, u32[]{:S(2)}, u32[]{:S(2)}) collective-permute-start(f32[576,128]{1,0:T(8,128)S(1)} %get-tuple-element.7), channel_id=1, source_target_pairs={{0,1},{1,0},{2,3},{3,2},{4,5},{5,4},{6,7},{7,6},{8,9},{9,8},{10,11... | collective-permute-start | bytes 884744 | tf_op jit(solution)/shard_map/ppermute | solution.py:274
  80.4 32.4 %all-to-all-start.2 = ((f32[32,1,2304]{2,1,0:T(1,128)}), f32[32,1,2304]{2,1,0:T(1,128)S(1)}, u32[]{:S(2)}, u32[]{:S(2)}) async-start(f32[32,1,2304]{2,1,0:T(1,128)} %bitcast.8), calls=%async_computation.2 | async-start | bytes 589824 | tf_op jit(solution)/shard_map/all_to_all | solution.py:275
  93.9 0.7 copy-start.4
  93.9 0.7 copy-start.5
  94.5 18.2 %copy-start.3 = (f32[3,5,1152]{2,0,1:T(4,128)S(1)}, f32[3,5,1152]{2,0,1:T(4,128)}, u32[]{:S(2)}) copy-start(f32[3,5,1152]{2,0,1:T(4,128)} %param.8) | copy-start | bytes 207364

commit v11 on v9

--- a/solution.py
+++ b/solution.py
@@ -109,7 +109,8 @@
             v = pltpu.roll(chosen[k * 24:(k + 1) * 24, :], (k * 24 - n * 24) % 256, 1)[:, :128]
             part = jnp.where((lane >= k * 24) & (lane < k * 24 + 24), v, part)
         for zh in range(2):
-            two_ref[n // 2 * 4 + zh * 2 + n % 2] = part
+            at = (n // 2 * 4 + zh * 2 + n % 2) * 18
+            two_ref[at:at + 18, :] = part[:18]
 
 
 def merge_kernel(zh_ref, own_ref, other_ref, out_ref, rows):
@@ -129,8 +130,7 @@
 def pack_kernel(one_ref, two_ref, out_ref):
     for y in range(4):
         out_ref[y, :288, :] = one_ref[...]
-        for n in range(16):
-            out_ref[y, 288 + n * 18:306 + n * 18, :] = two_ref[n, :18, :]
+        out_ref[y, 288:, :] = two_ref[...]
 
 
 def mark_kernel(*refs):
@@ -248,13 +248,13 @@
     ints = jnp.transpose(integrals, (1, 0, 2))
     res = jnp.transpose(residual, (1, 0, 2))
     other = lax.ppermute(amps, "zh", [(0, 1), (1, 0)])
-    two = call(swap_kernel, 0, 1, [(16, 24, 128)], [pltpu.VMEM((120, 256), F32)])(amps)
-    weights = call(weights_kernel, 0, 2, [(5, 64, 384)], [])(ints, two)
+    two = call(swap_kernel, 0, 1, [(288, 128)], [pltpu.VMEM((120, 256), F32)])(amps)
+    weights = call(weights_kernel, 0, 2, [(5, 64, 384)], [])(ints, other)
     along = [weights] + [
         lax.ppermute(weights, "x", [(s, (s - d) % 4) for s in range(4)]) for d in (1, 3, 2)
     ]
     across = [lax.ppermute(w, "core", [(0, 1), (1, 0)]) for w in along]
-    two = lax.all_to_all(two, ("x", "zh", "core"), 0, 0, tiled=True)
+    two = lax.all_to_all(two.reshape(16, 1, 2304), ("x", "zh", "core"), 0, 0, tiled=True).reshape(288, 128)
     one = call(merge_kernel, 1, 2, [(288, 128)], [pltpu.VMEM((96, 384), F32)], cost=8000)(zh.reshape(1), amps, other)
     both = call(pack_kernel, 0, 2, [(4, 576, 128)], [])(one, two)
     both = lax.all_to_all(both, "y", 0, 0, tiled=True)

time: 116 us -> 115 us (level)
  transfers between devices with their start and end apart: 12 -> 12, of which waited for: 6 -> 6; matrix products, arithmetic and copies ran while one was open for 0% -> 0% of each run, Pallas kernels for 4% -> 3%
where the time goes in v11:
time: 115 us
  starting transfers between devices  57.1 us (50%)
  waiting for transfers between devices  43.5 us (38%)
  Pallas kernels  10.7 us (9%)
  between operations  1.51 us (1%)
    all_to_all x1, waiting for transfers between devices, body(): lax.all_to_all(half.reshape(32, 1, 2304), ('y', 'zh', 'pair'), 0, 0, tile...  20.9 us
    ppermute x1, starting transfers between devices, body(): other = lax.ppermute(amps, 'zh', [(0, 1), (1, 0)])  14.1 us
    all_to_all x1, starting transfers between devices, body(): lax.all_to_all(half.reshape(32, 1, 2304), ('y', 'zh', 'pair'), 0, 0, tile...  13.5 us
    ppermute x3, starting transfers between devices, body(): lax.ppermute(weights, 'x', [(s, (s - d) % 4) for s in range(4)])  10.6 us
    ppermute x4, starting transfers between devices, body(): across = [lax.ppermute(w, 'core', [(0, 1), (1, 0)]) for w in along]  8.14 us
    ppermute x1, waiting for transfers between devices, body(): half = keep + lax.ppermute(send, 'par', [(0, 1), (1, 0)])  7.57 us
    all_to_all x1, waiting for transfers between devices, body(): lax.all_to_all(two.reshape(16, 1, 2304), ('x', 'zh', 'core'), 0, 0, tiled...  6.67 us
    all_to_all x1, waiting for transfers between devices, body(): both = lax.all_to_all(both, 'y', 0, 0, tiled=True)  4.75 us
  transfers between devices with their start and end apart: 12, of which 6 were waited for; matrix products, arithmetic and copies ran while one was open for 0% of the time, Pallas kernels for 3%

profile of v11, /device:TPU:64, one launch (start us, length us, event | category | flops | bytes accessed | tf_op | source)
XLA Modules:
  0.0 114.5 jit_solution(3662087532049270846)
XLA Ops:
  0.6 14.1 %collective-permute-start = (f32[5,3,1152]{2,1,0:T(4,128)}, f32[5,3,1152]{2,1,0:T(4,128)S(1)}, u32[]{:S(2)}, u32[]{:S(2)}) collective-permute-start(f32[5,3,1152]{2,1,0:T(4,128)} %bitcast.19), channel_id=1, source_target_pairs={{0,16},{16,0},{1,17},{17,1},{2,18},{18,2},{3,19},{19,3},{4,20},{20... | collective-permute-start | bytes 207368 | tf_op jit(solution)/shard_map/ppermute | solution.py:250
  14.7 0.9 copy-done.1
  15.6 1.2 %shard_map.78 = f32[288,128]{1,0:T(8,128)} custom-call(f32[5,3,1152]{2,1,0:T(4,128)S(1)} %bitcast.20), custom_call_target="tpu_custom_call" | custom-call | flops 1000000000 | bytes 1000 | tf_op jit(solution)/shard_map/pallas_call | solution.py:251
  16.8 4.4 %all-to-all-start = ((f32[16,1,2304]{2,1,0:T(1,128)}), f32[16,1,2304]{2,1,0:T(1,128)S(1)}, u32[]{:S(2)}, u32[]{:S(2)}) async-start(f32[16,1,2304]{2,1,0:T(1,128)} %bitcast.7), calls=%async_computation | async-start | bytes 294912 | tf_op jit(solution)/shard_map/all_to_all | solution.py:257
  21.4 5.0 %collective-permute-start.2 = (f32[5,64,384]{2,1,0:T(8,128)S(1)}, f32[5,64,384]{2,1,0:T(8,128)S(1)}, u32[]{:S(2)}, u32[]{:S(2)}) collective-permute-start(f32[5,64,384]{2,1,0:T(8,128)S(1)} %shard_map.80.refs_0_), channel_id=1, source_target_pairs={{0,384},{128,0},{256,128},{384,256},{1,385},{129,1},{257,129},{385... | collective-permute-start | bytes 1474568 | tf_op jit(solution)/shard_map/ppermute | solution.py:254
  26.5 2.8 %collective-permute-start.4 = (f32[5,64,384]{2,1,0:T(8,128)S(1)}, f32[5,64,384]{2,1,0:T(8,128)S(1)}, u32[]{:S(2)}, u32[]{:S(2)}) collective-permute-start(f32[5,64,384]{2,1,0:T(8,128)S(1)} %shard_map.80.refs_0_), channel_id=1, source_target_pairs={{0,256},{128,384},{256,0},{384,128},{1,257},{129,385},{257,1},{385... | collective-permute-start | bytes 1474568 | tf_op jit(solution)/shard_map/ppermute | solution.py:254
  29.2 2.8 %collective-permute-start.6 = (f32[5,64,384]{2,1,0:T(8,128)S(1)}, f32[5,64,384]{2,1,0:T(8,128)S(1)}, u32[]{:S(2)}, u32[]{:S(2)}) collective-permute-start(f32[5,64,384]{2,1,0:T(8,128)S(1)} %shard_map.80.refs_0_), channel_id=1, source_target_pairs={{0,128},{128,256},{256,384},{384,0},{1,129},{129,257},{257,385},{3... | collective-permute-start | bytes 1474568 | tf_op jit(solution)/shard_map/ppermute | solution.py:254
  32.1 6.7 %all-to-all-done = f32[16,1,2304]{2,1,0:T(1,128)S(1)} async-done(((f32[16,1,2304]{2,1,0:T(1,128)}), f32[16,1,2304]{2,1,0:T(1,128)S(1)}, u32[]{:S(2)}, u32[]{:S(2)}) %all-to-all-start) | async-done | bytes 147488 | tf_op jit(solution)/shard_map/all_to_all | solution.py:257
  38.8 1.1 shard_map.79
  39.9 4.5 %all-to-all-start.1 = ((f32[4,576,128]{2,1,0:T(8,128)}), f32[4,576,128]{2,1,0:T(8,128)S(1)}, u32[]{:S(2)}, u32[]{:S(2)}) async-start(f32[4,576,128]{2,1,0:T(8,128)} %shard_map.79), calls=%async_computation.1 | async-start | bytes 2359296 | tf_op jit(solution)/shard_map/all_to_all | solution.py:260
  44.3 1.9 %collective-permute-start.1 = (f32[5,64,384]{2,1,0:T(8,128)S(1)}, f32[5,64,384]{2,1,0:T(8,128)}, u32[]{:S(2)}, u32[]{:S(2)}) collective-permute-start(f32[5,64,384]{2,1,0:T(8,128)S(1)} %shard_map.80.refs_0_), channel_id=1, source_target_pairs={{0,8},{8,0},{1,9},{9,1},{2,10},{10,2},{3,11},{11,3},{4,12},{12,4},... | collective-permute-start | bytes 1474568 | tf_op jit(solution)/shard_map/ppermute | solution.py:256
  46.2 2.3 %collective-permute-done.2.refs_1_.refs_2_ = f32[5,64,384]{2,1,0:T(8,128)S(1)} collective-permute-done((f32[5,64,384]{2,1,0:T(8,128)S(1)}, f32[5,64,384]{2,1,0:T(8,128)S(1)}, u32[]{:S(2)}, u32[]{:S(2)}) %collective-permute-start.2) | collective-permute-done | bytes 491552 | tf_op jit(solution)/shard_map/ppermute | solution.py:254
  48.6 1.9 %collective-permute-start.3 = (f32[5,64,384]{2,1,0:T(8,128)S(1)}, f32[5,64,384]{2,1,0:T(8,128)}, u32[]{:S(2)}, u32[]{:S(2)}) collective-permute-start(f32[5,64,384]{2,1,0:T(8,128)S(1)} %collective-permute-done.2.refs_1_.refs_2_), channel_id=1, source_target_pairs={{0,8},{8,0},{1,9},{9,1},{2,10},{10,2},{3,11},{11,3},{4,12},{12,4},... | collective-permute-start | bytes 1474568 | tf_op jit(solution)/shard_map/ppermute | solution.py:256
  50.5 2.4 %collective-permute-start.5 = (f32[5,64,384]{2,1,0:T(8,128)S(1)}, f32[5,64,384]{2,1,0:T(8,128)}, u32[]{:S(2)}, u32[]{:S(2)}) collective-permute-start(f32[5,64,384]{2,1,0:T(8,128)S(1)} %collective-permute-done.4.refs_3_.refs_4_), channel_id=1, source_target_pairs={{0,8},{8,0},{1,9},{9,1},{2,10},{10,2},{3,11},{11,3},{4,12},{12,4},... | collective-permute-start | bytes 1474568 | tf_op jit(solution)/shard_map/ppermute | solution.py:256
  52.9 1.3 %collective-permute-done.6.refs_2_.refs_6_ = f32[5,64,384]{2,1,0:T(8,128)S(1)} collective-permute-done((f32[5,64,384]{2,1,0:T(8,128)S(1)}, f32[5,64,384]{2,1,0:T(8,128)S(1)}, u32[]{:S(2)}, u32[]{:S(2)}) %collective-permute-start.6) | collective-permute-done | bytes 491552 | tf_op jit(solution)/shard_map/ppermute | solution.py:254
  54.2 1.9 %collective-permute-start.7 = (f32[5,64,384]{2,1,0:T(8,128)S(1)}, f32[5,64,384]{2,1,0:T(8,128)}, u32[]{:S(2)}, u32[]{:S(2)}) collective-permute-start(f32[5,64,384]{2,1,0:T(8,128)S(1)} %collective-permute-done.6.refs_2_.refs_6_), channel_id=1, source_target_pairs={{0,8},{8,0},{1,9},{9,1},{2,10},{10,2},{3,11},{11,3},{4,12},{12,4},... | collective-permute-start | bytes 1474568 | tf_op jit(solution)/shard_map/ppermute | solution.py:256
  56.1 4.7 %all-to-all-done.1.refs_0_.got_ref = f32[4,576,128]{2,1,0:T(8,128)S(1)} async-done(((f32[4,576,128]{2,1,0:T(8,128)}), f32[4,576,128]{2,1,0:T(8,128)S(1)}, u32[]{:S(2)}, u32[]{:S(2)}) %all-to-all-start.1) | async-done | bytes 1179680 | tf_op jit(solution)/shard_map/all_to_all | solution.py:260
  60.9 4.7 %shard_map.83 = (f32[576,128]{1,0:T(8,128)S(1)}, f32[576,128]{1,0:T(8,128)S(1)}) custom-call(s32[1]{0:T(128)} %bitcast.4.par_ref, f32[4,576,128]{2,1,0:T(8,128)S(1)} %all-to-all-done.1.refs_0_.got_ref, f32[5,64,384]{2,1,0:T(8,128)S(1)} %shard_map.80.refs_0_, f32[5,64,384]{2,1,0:T(8,128)} %collective-permute-done.1.refs_1_, ...), custom_call_target="tpu_custom_call" | custom-call | flops 1000000000 | bytes 1000 | tf_op jit(solution)/shard_map/pallas_call | solution.py:265
  65.6 1.9 %collective-permute-start.8 = (f32[576,128]{1,0:T(8,128)S(1)}, f32[576,128]{1,0:T(8,128)S(1)}, u32[]{:S(2)}, u32[]{:S(2)}) collective-permute-start(f32[576,128]{1,0:T(8,128)S(1)} %get-tuple-element.7), channel_id=1, source_target_pairs={{0,1},{1,0},{2,3},{3,2},{4,5},{5,4},{6,7},{7,6},{8,9},{9,8},{10,11... | collective-permute-start | bytes 884744 | tf_op jit(solution)/shard_map/ppermute | solution.py:275
  67.6 7.6 %collective-permute-done.8 = f32[576,128]{1,0:T(8,128)S(1)} collective-permute-done((f32[576,128]{1,0:T(8,128)S(1)}, f32[576,128]{1,0:T(8,128)S(1)}, u32[]{:S(2)}, u32[]{:S(2)}) %collective-permute-start.8) | collective-permute-done | bytes 294944 | tf_op jit(solution)/shard_map/ppermute | solution.py:275
  75.1 0.8 add.19
  75.9 13.5 %all-to-all-start.2 = ((f32[32,1,2304]{2,1,0:T(1,128)}), f32[32,1,2304]{2,1,0:T(1,128)S(1)}, u32[]{:S(2)}, u32[]{:S(2)}) async-start(f32[32,1,2304]{2,1,0:T(1,128)} %bitcast.10), calls=%async_computation.2 | async-start | bytes 589824 | tf_op jit(solution)/shard_map/all_to_all | solution.py:276
  91.5 20.9 %all-to-all-done.2 = f32[32,1,2304]{2,1,0:T(1,128)S(1)} async-done(((f32[32,1,2304]{2,1,0:T(1,128)}), f32[32,1,2304]{2,1,0:T(1,128)S(1)}, u32[]{:S(2)}, u32[]{:S(2)}) %all-to-all-start.2) | async-done | bytes 294944 | tf_op jit(solution)/shard_map/all_to_all | solution.py:276
  112.4 2.1 %shard_map.86 = (f32[5,3,1152]{2,1,0:T(4,128)}, f32[5,3,1152]{2,1,0:T(4,128)}) custom-call(s32[6]{0:T(128)S(1)} %stack.23.place_ref, f32[576,128]{1,0:T(8,128)S(1)} %bitcast.16, bf16[128,1280]{1,0:T(8,128)(2,1)S(1)} %shard_map.84.spread_ref, f32[5,3,1152]{2,1,0:T(4,128)S(1)} %shard_map.85.den_ref, f32[5,3,1152]{2,1,0:T(4,128)S(1)} %bitcast.22), custom_call_target="tpu_custom_call" | custom-call | flops 1000000000 | bytes 1000 | tf_op jit(solution)/shard_map/pallas_call | solution.py:283
  (24 shorter events, 1.7 us)
Async XLA Ops:
  0.6 20.6 %copy-start = (f32[3,5,7680]{2,0,1:T(4,128)S(1)}, f32[3,5,7680]{2,0,1:T(4,128)}, u32[]{:S(2)}) copy-start(f32[3,5,7680]{2,0,1:T(4,128)} %param.7) | copy-start | bytes 1382404
  0.6 20.6 %collective-permute-start = (f32[5,3,1152]{2,1,0:T(4,128)}, f32[5,3,1152]{2,1,0:T(4,128)S(1)}, u32[]{:S(2)}, u32[]{:S(2)}) collective-permute-start(f32[5,3,1152]{2,1,0:T(4,128)} %bitcast.19), channel_id=1, source_target_pairs={{0,16},{16,0},{1,17},{17,1},{2,18},{18,2},{3,19},{19,3},{4,20},{20... | collective-permute-start | bytes 207368 | tf_op jit(solution)/shard_map/ppermute | solution.py:250
  14.7 0.9 copy-start.1
  16.8 21.9 %all-to-all-start = ((f32[16,1,2304]{2,1,0:T(1,128)}), f32[16,1,2304]{2,1,0:T(1,128)S(1)}, u32[]{:S(2)}, u32[]{:S(2)}) async-start(f32[16,1,2304]{2,1,0:T(1,128)} %bitcast.7), calls=%async_computation | async-start | bytes 294912 | tf_op jit(solution)/shard_map/all_to_all | solution.py:257
  21.3 10.8 %copy-start.2 = (f32[3,5,1152]{2,0,1:T(4,128)S(1)}, f32[3,5,1152]{2,0,1:T(4,128)}, u32[]{:S(2)}) copy-start(f32[3,5,1152]{2,0,1:T(4,128)} %param.6) | copy-start | bytes 207364
  21.4 27.1 %collective-permute-start.2 = (f32[5,64,384]{2,1,0:T(8,128)S(1)}, f32[5,64,384]{2,1,0:T(8,128)S(1)}, u32[]{:S(2)}, u32[]{:S(2)}) collective-permute-start(f32[5,64,384]{2,1,0:T(8,128)S(1)} %shard_map.80.refs_0_), channel_id=1, source_target_pairs={{0,384},{128,0},{256,128},{384,256},{1,385},{129,1},{257,129},{385... | collective-permute-start | bytes 1474568 | tf_op jit(solution)/shard_map/ppermute | solution.py:254
  26.5 24.0 %collective-permute-start.4 = (f32[5,64,384]{2,1,0:T(8,128)S(1)}, f32[5,64,384]{2,1,0:T(8,128)S(1)}, u32[]{:S(2)}, u32[]{:S(2)}) collective-permute-start(f32[5,64,384]{2,1,0:T(8,128)S(1)} %shard_map.80.refs_0_), channel_id=1, source_target_pairs={{0,256},{128,384},{256,0},{384,128},{1,257},{129,385},{257,1},{385... | collective-permute-start | bytes 1474568 | tf_op jit(solution)/shard_map/ppermute | solution.py:254
  29.2 24.9 %collective-permute-start.6 = (f32[5,64,384]{2,1,0:T(8,128)S(1)}, f32[5,64,384]{2,1,0:T(8,128)S(1)}, u32[]{:S(2)}, u32[]{:S(2)}) collective-permute-start(f32[5,64,384]{2,1,0:T(8,128)S(1)} %shard_map.80.refs_0_), channel_id=1, source_target_pairs={{0,128},{128,256},{256,384},{384,0},{1,129},{129,257},{257,385},{3... | collective-permute-start | bytes 1474568 | tf_op jit(solution)/shard_map/ppermute | solution.py:254
  39.9 21.0 %all-to-all-start.1 = ((f32[4,576,128]{2,1,0:T(8,128)}), f32[4,576,128]{2,1,0:T(8,128)S(1)}, u32[]{:S(2)}, u32[]{:S(2)}) async-start(f32[4,576,128]{2,1,0:T(8,128)} %shard_map.79), calls=%async_computation.1 | async-start | bytes 2359296 | tf_op jit(solution)/shard_map/all_to_all | solution.py:260
  44.3 16.5 %collective-permute-start.1 = (f32[5,64,384]{2,1,0:T(8,128)S(1)}, f32[5,64,384]{2,1,0:T(8,128)}, u32[]{:S(2)}, u32[]{:S(2)}) collective-permute-start(f32[5,64,384]{2,1,0:T(8,128)S(1)} %shard_map.80.refs_0_), channel_id=1, source_target_pairs={{0,8},{8,0},{1,9},{9,1},{2,10},{10,2},{3,11},{11,3},{4,12},{12,4},... | collective-permute-start | bytes 1474568 | tf_op jit(solution)/shard_map/ppermute | solution.py:256
  48.6 12.3 %collective-permute-start.3 = (f32[5,64,384]{2,1,0:T(8,128)S(1)}, f32[5,64,384]{2,1,0:T(8,128)}, u32[]{:S(2)}, u32[]{:S(2)}) collective-permute-start(f32[5,64,384]{2,1,0:T(8,128)S(1)} %collective-permute-done.2.refs_1_.refs_2_), channel_id=1, source_target_pairs={{0,8},{8,0},{1,9},{9,1},{2,10},{10,2},{3,11},{11,3},{4,12},{12,4},... | collective-permute-start | bytes 1474568 | tf_op jit(solution)/shard_map/ppermute | solution.py:256
  50.5 10.4 %collective-permute-start.5 = (f32[5,64,384]{2,1,0:T(8,128)S(1)}, f32[5,64,384]{2,1,0:T(8,128)}, u32[]{:S(2)}, u32[]{:S(2)}) collective-permute-start(f32[5,64,384]{2,1,0:T(8,128)S(1)} %collective-permute-done.4.refs_3_.refs_4_), channel_id=1, source_target_pairs={{0,8},{8,0},{1,9},{9,1},{2,10},{10,2},{3,11},{11,3},{4,12},{12,4},... | collective-permute-start | bytes 1474568 | tf_op jit(solution)/shard_map/ppermute | solution.py:256
  54.2 6.7 %collective-permute-start.7 = (f32[5,64,384]{2,1,0:T(8,128)S(1)}, f32[5,64,384]{2,1,0:T(8,128)}, u32[]{:S(2)}, u32[]{:S(2)}) collective-permute-start(f32[5,64,384]{2,1,0:T(8,128)S(1)} %collective-permute-done.6.refs_2_.refs_6_), channel_id=1, source_target_pairs={{0,8},{8,0},{1,9},{9,1},{2,10},{10,2},{3,11},{11,3},{4,12},{12,4},... | collective-permute-start | bytes 1474568 | tf_op jit(solution)/shard_map/ppermute | solution.py:256
  65.6 9.5 %collective-permute-start.8 = (f32[576,128]{1,0:T(8,128)S(1)}, f32[576,128]{1,0:T(8,128)S(1)}, u32[]{:S(2)}, u32[]{:S(2)}) collective-permute-start(f32[576,128]{1,0:T(8,128)S(1)} %get-tuple-element.7), channel_id=1, source_target_pairs={{0,1},{1,0},{2,3},{3,2},{4,5},{5,4},{6,7},{7,6},{8,9},{9,8},{10,11... | collective-permute-start | bytes 884744 | tf_op jit(solution)/shard_map/ppermute | solution.py:275
  75.9 36.5 %all-to-all-start.2 = ((f32[32,1,2304]{2,1,0:T(1,128)}), f32[32,1,2304]{2,1,0:T(1,128)S(1)}, u32[]{:S(2)}, u32[]{:S(2)}) async-start(f32[32,1,2304]{2,1,0:T(1,128)} %bitcast.10), calls=%async_computation.2 | async-start | bytes 589824 | tf_op jit(solution)/shard_map/all_to_all | solution.py:276
  90.2 0.7 copy-start.4
  90.2 0.7 copy-start.5
  90.9 21.6 %copy-start.3 = (f32[3,5,1152]{2,0,1:T(4,128)S(1)}, f32[3,5,1152]{2,0,1:T(4,128)}, u32[]{:S(2)}) copy-start(f32[3,5,1152]{2,0,1:T(4,128)} %param.8) | copy-start | bytes 207364

commit v12 on v11

--- a/solution.py
+++ b/solution.py
@@ -250,9 +250,8 @@
     other = lax.ppermute(amps, "zh", [(0, 1), (1, 0)])
     two = call(swap_kernel, 0, 1, [(288, 128)], [pltpu.VMEM((120, 256), F32)])(amps)
     weights = call(weights_kernel, 0, 2, [(5, 64, 384)], [])(ints, other)
-    along = [weights] + [
-        lax.ppermute(weights, "x", [(s, (s - d) % 4) for s in range(4)]) for d in (1, 3, 2)
-    ]
+    near, back = [lax.ppermute(weights, "x", [(s, (s - d) % 4) for s in range(4)]) for d in (1, 3)]
+    along = [weights, near, back, lax.ppermute(near, "x", [(s, (s - 1) % 4) for s in range(4)])]
     across = [lax.ppermute(w, "core", [(0, 1), (1, 0)]) for w in along]
     two = lax.all_to_all(two.reshape(16, 1, 2304), ("x", "zh", "core"), 0, 0, tiled=True).reshape(288, 128)
     one = call(merge_kernel, 1, 2, [(288, 128)], [pltpu.VMEM((96, 384), F32)], cost=8000)(zh.reshape(1), amps, other)

time: 115 us -> 115 us (level)
  starting transfers between devices: 57.1 us -> 59.6 us
  waiting for transfers between devices: 43.5 us -> 41 us
    all_to_all x1, waiting for transfers between devices: 6.67 us -> 0.01 us  [body(): lax.all_to_all(two.reshape(16, 1, 2304), ('x', 'zh', 'core'), 0, 0, tiled...]
    ppermute x3 -> x2, waiting for transfers between devices: 3.6 us -> 9.57 us  [body(): lax.ppermute(weights, 'x', [(s, (s - d) % 4) for s in range(4)])]
    ppermute x0 -> x1, starting transfers between devices: none -> 5.59 us  [body(): lax.ppermute(near, 'x', [(s, (s - 1) % 4) for s in range(4)])]
    ppermute x3 -> x2, starting transfers between devices: 10.6 us -> 6.96 us  [body(): lax.ppermute(weights, 'x', [(s, (s - d) % 4) for s in range(4)])]
    all_to_all x1, waiting for transfers between devices: 20.9 us -> 18.3 us  [body(): lax.all_to_all(half.reshape(32, 1, 2304), ('y', 'zh', 'pair'), 0, 0, tile...]
    all_to_all x1, waiting for transfers between devices: 4.75 us -> 6.99 us  [body(): both = lax.all_to_all(both, 'y', 0, 0, tiled=True)]
    ppermute x1, waiting for transfers between devices: 7.57 us -> 6.13 us  [body(): half = keep + lax.ppermute(send, 'par', [(0, 1), (1, 0)])]
  transfers between devices with their start and end apart: 12 -> 12, of which waited for: 6 -> 4; matrix products, arithmetic and copies ran while one was open for 0% -> 0% of each run, Pallas kernels for 3% -> 3%
where the time goes in v12:
time: 115 us
  starting transfers between devices  59.6 us (52%)
  waiting for transfers between devices  41 us (36%)
  Pallas kernels  10.7 us (9%)
  between operations  1.52 us (1%)
    all_to_all x1, waiting for transfers between devices, body(): lax.all_to_all(half.reshape(32, 1, 2304), ('y', 'zh', 'pair'), 0, 0, tile...  18.3 us
    ppermute x1, starting transfers between devices, body(): other = lax.ppermute(amps, 'zh', [(0, 1), (1, 0)])  14.1 us
    all_to_all x1, starting transfers between devices, body(): lax.all_to_all(half.reshape(32, 1, 2304), ('y', 'zh', 'pair'), 0, 0, tile...  12.9 us
    ppermute x2, waiting for transfers between devices, body(): lax.ppermute(weights, 'x', [(s, (s - d) % 4) for s in range(4)])  9.57 us
    ppermute x4, starting transfers between devices, body(): across = [lax.ppermute(w, 'core', [(0, 1), (1, 0)]) for w in along]  8.65 us
    all_to_all x1, waiting for transfers between devices, body(): both = lax.all_to_all(both, 'y', 0, 0, tiled=True)  6.99 us
    ppermute x2, starting transfers between devices, body(): lax.ppermute(weights, 'x', [(s, (s - d) % 4) for s in range(4)])  6.96 us
    ppermute x1, waiting for transfers between devices, body(): half = keep + lax.ppermute(send, 'par', [(0, 1), (1, 0)])  6.13 us
  transfers between devices with their start and end apart: 12, of which 4 were waited for; matrix products, arithmetic and copies ran while one was open for 0% of the time, Pallas kernels for 3%

profile of v12, /device:TPU:64, one launch (start us, length us, event | category | flops | bytes accessed | tf_op | source)
XLA Modules:
  0.0 114.6 jit_solution(7827726130375431357)
XLA Ops:
  0.6 14.1 %collective-permute-start = (f32[5,3,1152]{2,1,0:T(4,128)}, f32[5,3,1152]{2,1,0:T(4,128)S(1)}, u32[]{:S(2)}, u32[]{:S(2)}) collective-permute-start(f32[5,3,1152]{2,1,0:T(4,128)} %bitcast.19), channel_id=1, source_target_pairs={{0,16},{16,0},{1,17},{17,1},{2,18},{18,2},{3,19},{19,3},{4,20},{20... | collective-permute-start | bytes 207368 | tf_op jit(solution)/shard_map/ppermute | solution.py:250
  14.7 0.9 copy-done.1
  15.6 1.2 %shard_map.78 = f32[288,128]{1,0:T(8,128)} custom-call(f32[5,3,1152]{2,1,0:T(4,128)S(1)} %bitcast.20), custom_call_target="tpu_custom_call" | custom-call | flops 1000000000 | bytes 1000 | tf_op jit(solution)/shard_map/pallas_call | solution.py:251
  16.8 4.4 %all-to-all-start = ((f32[16,1,2304]{2,1,0:T(1,128)}), f32[16,1,2304]{2,1,0:T(1,128)S(1)}, u32[]{:S(2)}, u32[]{:S(2)}) async-start(f32[16,1,2304]{2,1,0:T(1,128)} %bitcast.7), calls=%async_computation | async-start | bytes 294912 | tf_op jit(solution)/shard_map/all_to_all | solution.py:256
  21.4 5.0 %collective-permute-start.2 = (f32[5,64,384]{2,1,0:T(8,128)S(1)}, f32[5,64,384]{2,1,0:T(8,128)S(1)}, u32[]{:S(2)}, u32[]{:S(2)}) collective-permute-start(f32[5,64,384]{2,1,0:T(8,128)S(1)} %shard_map.80.refs_0_), channel_id=1, source_target_pairs={{0,384},{128,0},{256,128},{384,256},{1,385},{129,1},{257,129},{385... | collective-permute-start | bytes 1474568 | tf_op jit(solution)/shard_map/ppermute | solution.py:253
  26.5 1.9 %collective-permute-start.6 = (f32[5,64,384]{2,1,0:T(8,128)S(1)}, f32[5,64,384]{2,1,0:T(8,128)S(1)}, u32[]{:S(2)}, u32[]{:S(2)}) collective-permute-start(f32[5,64,384]{2,1,0:T(8,128)S(1)} %shard_map.80.refs_0_), channel_id=1, source_target_pairs={{0,128},{128,256},{256,384},{384,0},{1,129},{129,257},{257,385},{3... | collective-permute-start | bytes 1474568 | tf_op jit(solution)/shard_map/ppermute | solution.py:253
  28.5 9.6 %collective-permute-done.2.refs_1_.refs_2_ = f32[5,64,384]{2,1,0:T(8,128)S(1)} collective-permute-done((f32[5,64,384]{2,1,0:T(8,128)S(1)}, f32[5,64,384]{2,1,0:T(8,128)S(1)}, u32[]{:S(2)}, u32[]{:S(2)}) %collective-permute-start.2) | collective-permute-done | bytes 491552 | tf_op jit(solution)/shard_map/ppermute | solution.py:253
  38.0 5.6 %collective-permute-start.4 = (f32[5,64,384]{2,1,0:T(8,128)S(1)}, f32[5,64,384]{2,1,0:T(8,128)S(1)}, u32[]{:S(2)}, u32[]{:S(2)}) collective-permute-start(f32[5,64,384]{2,1,0:T(8,128)S(1)} %collective-permute-done.2.refs_1_.refs_2_), channel_id=1, source_target_pairs={{0,384},{128,0},{256,128},{384,256},{1,385},{129,1},{257,129},{385... | collective-permute-start | bytes 1474568 | tf_op jit(solution)/shard_map/ppermute | solution.py:254
  43.6 1.1 shard_map.79
  44.8 4.5 %all-to-all-start.1 = ((f32[4,576,128]{2,1,0:T(8,128)}), f32[4,576,128]{2,1,0:T(8,128)S(1)}, u32[]{:S(2)}, u32[]{:S(2)}) async-start(f32[4,576,128]{2,1,0:T(8,128)} %shard_map.79), calls=%async_computation.1 | async-start | bytes 2359296 | tf_op jit(solution)/shard_map/all_to_all | solution.py:259
  49.2 1.9 %collective-permute-start.1 = (f32[5,64,384]{2,1,0:T(8,128)S(1)}, f32[5,64,384]{2,1,0:T(8,128)}, u32[]{:S(2)}, u32[]{:S(2)}) collective-permute-start(f32[5,64,384]{2,1,0:T(8,128)S(1)} %shard_map.80.refs_0_), channel_id=1, source_target_pairs={{0,8},{8,0},{1,9},{9,1},{2,10},{10,2},{3,11},{11,3},{4,12},{12,4},... | collective-permute-start | bytes 1474568 | tf_op jit(solution)/shard_map/ppermute | solution.py:255
  51.1 2.4 %collective-permute-start.3 = (f32[5,64,384]{2,1,0:T(8,128)S(1)}, f32[5,64,384]{2,1,0:T(8,128)}, u32[]{:S(2)}, u32[]{:S(2)}) collective-permute-start(f32[5,64,384]{2,1,0:T(8,128)S(1)} %collective-permute-done.2.refs_1_.refs_2_), channel_id=1, source_target_pairs={{0,8},{8,0},{1,9},{9,1},{2,10},{10,2},{3,11},{11,3},{4,12},{12,4},... | collective-permute-start | bytes 1474568 | tf_op jit(solution)/shard_map/ppermute | solution.py:255
  53.6 1.9 %collective-permute-start.7 = (f32[5,64,384]{2,1,0:T(8,128)S(1)}, f32[5,64,384]{2,1,0:T(8,128)}, u32[]{:S(2)}, u32[]{:S(2)}) collective-permute-start(f32[5,64,384]{2,1,0:T(8,128)S(1)} %collective-permute-done.6.refs_2_.refs_6_), channel_id=1, source_target_pairs={{0,8},{8,0},{1,9},{9,1},{2,10},{10,2},{3,11},{11,3},{4,12},{12,4},... | collective-permute-start | bytes 1474568 | tf_op jit(solution)/shard_map/ppermute | solution.py:255
  55.5 2.4 %collective-permute-start.5 = (f32[5,64,384]{2,1,0:T(8,128)S(1)}, f32[5,64,384]{2,1,0:T(8,128)}, u32[]{:S(2)}, u32[]{:S(2)}) collective-permute-start(f32[5,64,384]{2,1,0:T(8,128)S(1)} %collective-permute-done.4.refs_3_.refs_4_), channel_id=1, source_target_pairs={{0,8},{8,0},{1,9},{9,1},{2,10},{10,2},{3,11},{11,3},{4,12},{12,4},... | collective-permute-start | bytes 1474568 | tf_op jit(solution)/shard_map/ppermute | solution.py:255
  57.9 7.0 %all-to-all-done.1.refs_0_.got_ref = f32[4,576,128]{2,1,0:T(8,128)S(1)} async-done(((f32[4,576,128]{2,1,0:T(8,128)}), f32[4,576,128]{2,1,0:T(8,128)S(1)}, u32[]{:S(2)}, u32[]{:S(2)}) %all-to-all-start.1) | async-done | bytes 1179680 | tf_op jit(solution)/shard_map/all_to_all | solution.py:259
  65.0 4.7 %shard_map.83 = (f32[576,128]{1,0:T(8,128)S(1)}, f32[576,128]{1,0:T(8,128)S(1)}) custom-call(s32[1]{0:T(128)} %bitcast.4.par_ref, f32[4,576,128]{2,1,0:T(8,128)S(1)} %all-to-all-done.1.refs_0_.got_ref, f32[5,64,384]{2,1,0:T(8,128)S(1)} %shard_map.80.refs_0_, f32[5,64,384]{2,1,0:T(8,128)} %collective-permute-done.1.refs_1_, ...), custom_call_target="tpu_custom_call" | custom-call | flops 1000000000 | bytes 1000 | tf_op jit(solution)/shard_map/pallas_call | solution.py:264
  69.7 2.5 %collective-permute-start.8 = (f32[576,128]{1,0:T(8,128)S(1)}, f32[576,128]{1,0:T(8,128)S(1)}, u32[]{:S(2)}, u32[]{:S(2)}) collective-permute-start(f32[576,128]{1,0:T(8,128)S(1)} %get-tuple-element.7), channel_id=1, source_target_pairs={{0,1},{1,0},{2,3},{3,2},{4,5},{5,4},{6,7},{7,6},{8,9},{9,8},{10,11... | collective-permute-start | bytes 884744 | tf_op jit(solution)/shard_map/ppermute | solution.py:274
  72.2 6.1 %collective-permute-done.8 = f32[576,128]{1,0:T(8,128)S(1)} collective-permute-done((f32[576,128]{1,0:T(8,128)S(1)}, f32[576,128]{1,0:T(8,128)S(1)}, u32[]{:S(2)}, u32[]{:S(2)}) %collective-permute-start.8) | collective-permute-done | bytes 294944 | tf_op jit(solution)/shard_map/ppermute | solution.py:274
  78.3 0.8 add.19
  79.1 12.9 %all-to-all-start.2 = ((f32[32,1,2304]{2,1,0:T(1,128)}), f32[32,1,2304]{2,1,0:T(1,128)S(1)}, u32[]{:S(2)}, u32[]{:S(2)}) async-start(f32[32,1,2304]{2,1,0:T(1,128)} %bitcast.10), calls=%async_computation.2 | async-start | bytes 589824 | tf_op jit(solution)/shard_map/all_to_all | solution.py:275
  92.8 0.6 shard_map.84.spread_ref
  93.5 0.7 shard_map.85.den_ref
  94.1 18.3 %all-to-all-done.2 = f32[32,1,2304]{2,1,0:T(1,128)S(1)} async-done(((f32[32,1,2304]{2,1,0:T(1,128)}), f32[32,1,2304]{2,1,0:T(1,128)S(1)}, u32[]{:S(2)}, u32[]{:S(2)}) %all-to-all-start.2) | async-done | bytes 294944 | tf_op jit(solution)/shard_map/all_to_all | solution.py:275
  112.5 2.1 %shard_map.86 = (f32[5,3,1152]{2,1,0:T(4,128)}, f32[5,3,1152]{2,1,0:T(4,128)}) custom-call(s32[6]{0:T(128)S(1)} %stack.23.place_ref, f32[576,128]{1,0:T(8,128)S(1)} %bitcast.16, bf16[128,1280]{1,0:T(8,128)(2,1)S(1)} %shard_map.84.spread_ref, f32[5,3,1152]{2,1,0:T(4,128)S(1)} %shard_map.85.den_ref, f32[5,3,1152]{2,1,0:T(4,128)S(1)} %bitcast.22), custom_call_target="tpu_custom_call" | custom-call | flops 1000000000 | bytes 1000 | tf_op jit(solution)/shard_map/pallas_call | solution.py:282
  (24 shorter events, 0.4 us)
Async XLA Ops:
  0.6 20.6 %copy-start = (f32[3,5,7680]{2,0,1:T(4,128)S(1)}, f32[3,5,7680]{2,0,1:T(4,128)}, u32[]{:S(2)}) copy-start(f32[3,5,7680]{2,0,1:T(4,128)} %param.7) | copy-start | bytes 1382404
  0.6 20.6 %collective-permute-start = (f32[5,3,1152]{2,1,0:T(4,128)}, f32[5,3,1152]{2,1,0:T(4,128)S(1)}, u32[]{:S(2)}, u32[]{:S(2)}) collective-permute-start(f32[5,3,1152]{2,1,0:T(4,128)} %bitcast.19), channel_id=1, source_target_pairs={{0,16},{16,0},{1,17},{17,1},{2,18},{18,2},{3,19},{19,3},{4,20},{20... | collective-permute-start | bytes 207368 | tf_op jit(solution)/shard_map/ppermute | solution.py:250
  14.7 0.9 copy-start.1
  16.8 26.8 %all-to-all-start = ((f32[16,1,2304]{2,1,0:T(1,128)}), f32[16,1,2304]{2,1,0:T(1,128)S(1)}, u32[]{:S(2)}, u32[]{:S(2)}) async-start(f32[16,1,2304]{2,1,0:T(1,128)} %bitcast.7), calls=%async_computation | async-start | bytes 294912 | tf_op jit(solution)/shard_map/all_to_all | solution.py:256
  21.3 7.1 %copy-start.2 = (f32[3,5,1152]{2,0,1:T(4,128)S(1)}, f32[3,5,1152]{2,0,1:T(4,128)}, u32[]{:S(2)}) copy-start(f32[3,5,1152]{2,0,1:T(4,128)} %param.6) | copy-start | bytes 207364
  21.4 16.6 %collective-permute-start.2 = (f32[5,64,384]{2,1,0:T(8,128)S(1)}, f32[5,64,384]{2,1,0:T(8,128)S(1)}, u32[]{:S(2)}, u32[]{:S(2)}) collective-permute-start(f32[5,64,384]{2,1,0:T(8,128)S(1)} %shard_map.80.refs_0_), channel_id=1, source_target_pairs={{0,384},{128,0},{256,128},{384,256},{1,385},{129,1},{257,129},{385... | collective-permute-start | bytes 1474568 | tf_op jit(solution)/shard_map/ppermute | solution.py:253
  26.5 27.1 %collective-permute-start.6 = (f32[5,64,384]{2,1,0:T(8,128)S(1)}, f32[5,64,384]{2,1,0:T(8,128)S(1)}, u32[]{:S(2)}, u32[]{:S(2)}) collective-permute-start(f32[5,64,384]{2,1,0:T(8,128)S(1)} %shard_map.80.refs_0_), channel_id=1, source_target_pairs={{0,128},{128,256},{256,384},{384,0},{1,129},{129,257},{257,385},{3... | collective-permute-start | bytes 1474568 | tf_op jit(solution)/shard_map/ppermute | solution.py:253
  38.0 17.5 %collective-permute-start.4 = (f32[5,64,384]{2,1,0:T(8,128)S(1)}, f32[5,64,384]{2,1,0:T(8,128)S(1)}, u32[]{:S(2)}, u32[]{:S(2)}) collective-permute-start(f32[5,64,384]{2,1,0:T(8,128)S(1)} %collective-permute-done.2.refs_1_.refs_2_), channel_id=1, source_target_pairs={{0,384},{128,0},{256,128},{384,256},{1,385},{129,1},{257,129},{385... | collective-permute-start | bytes 1474568 | tf_op jit(solution)/shard_map/ppermute | solution.py:254
  44.8 20.2 %all-to-all-start.1 = ((f32[4,576,128]{2,1,0:T(8,128)}), f32[4,576,128]{2,1,0:T(8,128)S(1)}, u32[]{:S(2)}, u32[]{:S(2)}) async-start(f32[4,576,128]{2,1,0:T(8,128)} %shard_map.79), calls=%async_computation.1 | async-start | bytes 2359296 | tf_op jit(solution)/shard_map/all_to_all | solution.py:259
  49.2 15.7 %collective-permute-start.1 = (f32[5,64,384]{2,1,0:T(8,128)S(1)}, f32[5,64,384]{2,1,0:T(8,128)}, u32[]{:S(2)}, u32[]{:S(2)}) collective-permute-start(f32[5,64,384]{2,1,0:T(8,128)S(1)} %shard_map.80.refs_0_), channel_id=1, source_target_pairs={{0,8},{8,0},{1,9},{9,1},{2,10},{10,2},{3,11},{11,3},{4,12},{12,4},... | collective-permute-start | bytes 1474568 | tf_op jit(solution)/shard_map/ppermute | solution.py:255
  51.1 13.8 %collective-permute-start.3 = (f32[5,64,384]{2,1,0:T(8,128)S(1)}, f32[5,64,384]{2,1,0:T(8,128)}, u32[]{:S(2)}, u32[]{:S(2)}) collective-permute-start(f32[5,64,384]{2,1,0:T(8,128)S(1)} %collective-permute-done.2.refs_1_.refs_2_), channel_id=1, source_target_pairs={{0,8},{8,0},{1,9},{9,1},{2,10},{10,2},{3,11},{11,3},{4,12},{12,4},... | collective-permute-start | bytes 1474568 | tf_op jit(solution)/shard_map/ppermute | solution.py:255
  53.6 11.4 %collective-permute-start.7 = (f32[5,64,384]{2,1,0:T(8,128)S(1)}, f32[5,64,384]{2,1,0:T(8,128)}, u32[]{:S(2)}, u32[]{:S(2)}) collective-permute-start(f32[5,64,384]{2,1,0:T(8,128)S(1)} %collective-permute-done.6.refs_2_.refs_6_), channel_id=1, source_target_pairs={{0,8},{8,0},{1,9},{9,1},{2,10},{10,2},{3,11},{11,3},{4,12},{12,4},... | collective-permute-start | bytes 1474568 | tf_op jit(solution)/shard_map/ppermute | solution.py:255
  55.5 9.4 %collective-permute-start.5 = (f32[5,64,384]{2,1,0:T(8,128)S(1)}, f32[5,64,384]{2,1,0:T(8,128)}, u32[]{:S(2)}, u32[]{:S(2)}) collective-permute-start(f32[5,64,384]{2,1,0:T(8,128)S(1)} %collective-permute-done.4.refs_3_.refs_4_), channel_id=1, source_target_pairs={{0,8},{8,0},{1,9},{9,1},{2,10},{10,2},{3,11},{11,3},{4,12},{12,4},... | collective-permute-start | bytes 1474568 | tf_op jit(solution)/shard_map/ppermute | solution.py:255
  69.7 8.6 %collective-permute-start.8 = (f32[576,128]{1,0:T(8,128)S(1)}, f32[576,128]{1,0:T(8,128)S(1)}, u32[]{:S(2)}, u32[]{:S(2)}) collective-permute-start(f32[576,128]{1,0:T(8,128)S(1)} %get-tuple-element.7), channel_id=1, source_target_pairs={{0,1},{1,0},{2,3},{3,2},{4,5},{5,4},{6,7},{7,6},{8,9},{9,8},{10,11... | collective-permute-start | bytes 884744 | tf_op jit(solution)/shard_map/ppermute | solution.py:274
  79.1 33.4 %all-to-all-start.2 = ((f32[32,1,2304]{2,1,0:T(1,128)}), f32[32,1,2304]{2,1,0:T(1,128)S(1)}, u32[]{:S(2)}, u32[]{:S(2)}) async-start(f32[32,1,2304]{2,1,0:T(1,128)} %bitcast.10), calls=%async_computation.2 | async-start | bytes 589824 | tf_op jit(solution)/shard_map/all_to_all | solution.py:275
  92.8 0.7 copy-start.4
  92.8 0.7 copy-start.5
  93.5 19.0 %copy-start.3 = (f32[3,5,1152]{2,0,1:T(4,128)S(1)}, f32[3,5,1152]{2,0,1:T(4,128)}, u32[]{:S(2)}) copy-start(f32[3,5,1152]{2,0,1:T(4,128)} %param.8) | copy-start | bytes 207364
